TPU v7x, 32 devices: a whole 2x2x4 slice. The times are simulated.
32 devices in a mesh: parts: 2 (over x), dp: 8 (over z, y), mp: 2 (over core).
Axes of the slice: x: 2, y: 2, z: 4, core: 2. Of those that a mesh axis runs over, the one named last changes fastest.
Arguments:
- inputs: bfloat16 [3072, 8192], P(('parts', 'dp'), 'mp'), parts along dimension 0, may hold values from -6 to 6
- gate_pre: bfloat16 [3072, 14336], P(('parts', 'dp'), 'mp'), parts along dimension 0, may hold values from -8 to 8
- up_pre: bfloat16 [3072, 14336], P(('parts', 'dp'), 'mp'), parts along dimension 0, may hold values from -6 to 6
- hidden_grad: bfloat16 [3072, 14336], P(('parts', 'dp'), 'mp'), parts along dimension 0, may hold values from -6 to 6
- out_grad: bfloat16 [3072, 8192], P(('parts', 'dp'), 'mp'), parts along dimension 0, may hold values from -6 to 6
- example_ids: int32 [3072], P(('parts', 'dp')), parts along dimension 0, may hold values from 0 to 15, as said below
- gate_in: bfloat16 [8192, 64], P('mp'), may hold values from -0.0625 to 0.0625
- gate_out: bfloat16 [14336, 64], P('mp'), may hold values from -0.046875 to 0.046875
- up_in: bfloat16 [8192, 64], P('mp'), may hold values from -0.0625 to 0.0625
- up_out: bfloat16 [14336, 64], P('mp'), may hold values from -0.046875 to 0.046875
- down_in: bfloat16 [14336, 64], P('mp'), may hold values from -0.046875 to 0.046875
- down_out: bfloat16 [8192, 64], P('mp'), may hold values from -0.0625 to 0.0625
- queries: bfloat16 [512, 12288], P(None, ('dp', 'mp')), may hold values from -0.005859375 to 0.005859375
Outputs:
- scores: float32 [32, 512], P(('parts', 'dp', 'mp')), parts along dimension 0
There are 2 independent parts, one for each index of `parts`. A program takes and returns all parts, laid end to end along the dimension named above; an argument that names none is the same for every part. Nothing has to cross between parts.
Inputs may be any that keep to these rules, and one draw needn't show every extreme that they name: example_ids never fall along the tokens: each example is one run of consecutive tokens; example 0 begins at token 0 and example e > 0 begins at a token in [e * 96, (e + 1) * 96).
All inputs are finite; a program needn't handle non-finite values.
Results may differ from a plain program's by a relative error of at most 0.0029.
Values may be sent and summed in bfloat16 or wider, within the bound.
No kernel may reach another device: no remote copies, remote signals or barrier semaphores. Data moves between devices by JAX's collectives and lax.ppermute only.
A program may use at most 128 MiB of HBM per device.

v0:
```python
import jax
import jax.numpy as jnp
from jax import lax
from jax.sharding import PartitionSpec as P

EX_DEV = 1


def shifted(block, axis, distance):
    devices = range(lax.axis_size(axis))
    route = [(i - distance, i) for i in devices if i - distance in devices]
    return lax.ppermute(block, axis, route)


def per_example(onehot, left, right):
    weighted = (onehot[:, :, None] * left[:, None, :]).reshape(left.shape[0], -1)
    outer = jnp.einsum("tc,tj->cj", weighted, right, precision=lax.Precision.HIGHEST)
    return outer.reshape(onehot.shape[1], -1)


def body(
    inputs,
    gate_pre,
    up_pre,
    hidden_grad,
    out_grad,
    example_ids,
    gate_in,
    gate_out,
    up_in,
    up_out,
    down_in,
    down_out,
    queries,
):
    row_count = inputs.shape[0]
    half_rows = row_count // lax.axis_size("mp")
    width = gate_in.shape[1]
    gate_value = gate_pre.astype(jnp.float32)
    up_value = up_pre.astype(jnp.float32)
    sigmoid_gate = jax.nn.sigmoid(gate_value)
    hidden = (gate_value * sigmoid_gate * up_value).astype(jnp.bfloat16)
    back_value = hidden_grad.astype(jnp.float32)
    gate_grad = (
        back_value * up_value * sigmoid_gate * (1.0 + gate_value * (1.0 - sigmoid_gate))
    ).astype(jnp.bfloat16)
    up_grad = (back_value * gate_value * sigmoid_gate).astype(jnp.bfloat16)
    projected = [
        jnp.dot(inputs, gate_in, preferred_element_type=jnp.float32),
        jnp.dot(gate_grad, gate_out, preferred_element_type=jnp.float32),
        jnp.dot(inputs, up_in, preferred_element_type=jnp.float32),
        jnp.dot(up_grad, up_out, preferred_element_type=jnp.float32),
        jnp.dot(hidden, down_in, preferred_element_type=jnp.float32),
        jnp.dot(out_grad, down_out, preferred_element_type=jnp.float32),
    ]
    summed = lax.psum_scatter(
        jnp.concatenate(projected, axis=1), "mp", scatter_dimension=0, tiled=True
    )
    my_ids = lax.dynamic_slice_in_dim(example_ids, lax.axis_index("mp") * half_rows, half_rows, 0)
    first_label = lax.axis_index(("dp", "mp")) * EX_DEV - 1
    labels = first_label + jnp.arange(EX_DEV + 1, dtype=jnp.int32)
    onehot = (my_ids[:, None] == labels[None, :]).astype(jnp.float32)
    modules = []
    for module in range(3):
        left = summed[:, 2 * module * width : (2 * module + 1) * width]
        right = summed[:, (2 * module + 1) * width : (2 * module + 2) * width]
        modules.append(per_example(onehot, left, right))
    partial_value = jnp.concatenate(modules, axis=1)
    received = shifted(partial_value[0:1], ("dp", "mp"), -1)
    own_rows = partial_value[1:]
    own_rows = own_rows.at[EX_DEV - 1].add(received[0])
    return jnp.dot(
        own_rows,
        lax.all_gather(queries, ("dp", "mp"), axis=1, tiled=True).astype(jnp.float32).T,
        precision=lax.Precision.HIGHEST,
    )


def solution(mesh):
    placed = (
        P(("parts", "dp"), "mp"),
        P(("parts", "dp"), "mp"),
        P(("parts", "dp"), "mp"),
        P(("parts", "dp"), "mp"),
        P(("parts", "dp"), "mp"),
        P(("parts", "dp")),
        P("mp", None),
        P("mp", None),
        P("mp", None),
        P("mp", None),
        P("mp", None),
        P("mp", None),
        P(None, ("dp", "mp")),
    )
    return jax.shard_map(
        body, mesh=mesh, in_specs=placed, out_specs=P(("parts", "dp", "mp"), None), check_vma=False
    )
```

profile of v0, /device:TPU:0, one launch (start us, length us, event | category | flops | bytes accessed | tf_op | source)
XLA Modules:
  0.0 149.3 jit_solution(12384476014042980349)
XLA Ops:
  7.4 0.0 copy-start
  7.4 0.0 reduce-scatter.4.cloned.1.call-start
  7.4 1.4 copy-done
  8.8 1.7 %convolution_dynamic-update-slice_fusion.2 = f32[192,384]{0,1:T(8,128)S(1)} fusion(bf16[192,4096]{1,0:T(8,128)(2,1)S(1)} %copy-done, bf16[4096,64]{0,1:T(8,128)(2,1)} %param.21), kind=kOutput, calls=%fused_computation.21 | convolution fusion | flops 100663296 | bytes 2162688 | tf_op jit(solution)/shard_map/dot_general | solution.py:49
  10.4 0.0 copy-start.2
  10.5 0.0 copy-start.4
  10.5 0.0 copy-start.6
  10.5 0.0 copy-start.7
  10.5 6.3 %fusion.16 = f32[192,384]{0,1:T(8,128)S(1)} fusion(f32[192,384]{0,1:T(8,128)S(1)} %convolution_dynamic-update-slice_fusion.2, bf16[7168,64]{0,1:T(8,128)(2,1)} %param.22, bf16[192,7168]{1,0:T(8,128)(2,1)} %param.17, bf16[192,7168]{1,0:T(8,128)(2,1)} %param.18, bf16[192,7168]{1,0:T(8,128)(2,1)} %param.16), kind=kOutput, calls=%fused_computation.22 | convolution fusion | flops 194052096 | bytes 9240576 | tf_op jit(solution)/shard_map/dot_general | solution.py:50
  16.8 0.0 copy-done.2
  16.8 0.6 convolution_dynamic-update-slice_fusion.1
  17.4 0.0 copy-done.4
  17.4 0.0 copy-done.6
  17.5 0.0 copy-done.7
  17.5 0.0 copy-start.5
  17.5 0.0 copy-start.8
  17.5 1.7 %fusion.22 = f32[192,384]{0,1:T(8,128)S(1)} fusion(f32[192,384]{0,1:T(8,128)S(1)} %convolution_dynamic-update-slice_fusion.1, bf16[7168,64]{0,1:T(8,128)(2,1)S(1)} %copy-done.7, bf16[192,7168]{1,0:T(8,128)(2,1)S(1)} %copy-done.6, bf16[192,7168]{1,0:T(8,128)(2,1)S(1)} %copy-done.4), kind=kOutput, calls=%fused_computation.24 | convolution fusion | flops 187170816 | bytes 6488064 | tf_op jit(solution)/shard_map/dot_general | solution.py:52
  19.2 0.0 copy-done.5
  19.2 0.2 copy-done.8
  19.5 0.0 copy-start.1
  19.5 0.0 copy-start.3
  19.5 0.0 copy-start.9
  19.5 1.7 %fusion.19 = f32[192,384]{0,1:T(8,128)S(1)} fusion(f32[192,384]{0,1:T(8,128)S(1)} %fusion.22, bf16[7168,64]{0,1:T(8,128)(2,1)S(1)} %copy-done.8, bf16[192,7168]{1,0:T(8,128)(2,1)S(1)} %copy-done.5, bf16[192,7168]{1,0:T(8,128)(2,1)S(1)} %copy-done.6), kind=kOutput, calls=%fused_computation.23 | convolution fusion | flops 187170816 | bytes 6488064 | tf_op jit(solution)/shard_map/dot_general | solution.py:53
  21.2 0.0 copy-done.1
  21.2 0.0 copy-done.3
  21.3 0.6 convolution_dynamic-update-slice_fusion
  21.9 0.9 copy.26
  22.8 0.0 reduce-scatter.4.cloned.1.call-update
  22.8 0.0 all-gather.2.cloned.1.call-start
  22.8 0.5 all-gather.2.cloned.1.call-update
  23.4 0.0 copy-done.9
  23.4 0.1 dynamic_slice.3
  23.5 0.1 compare_convert_fusion
  23.5 9.8 %reduce-scatter.4.cloned.1.call-done = f32[96,384]{1,0:T(8,128)} async-done(((f32[192,384]{1,0:T(8,128)}), f32[96,384]{1,0:T(8,128)}) %reduce-scatter.4.cloned.1.call-update) | async-done | bytes 147472
  33.3 0.9 fusion.37
  34.2 0.1 copy.28
  34.3 0.1 copy.30
  34.3 0.1 copy.32
  34.5 1.1 fusion.30
  35.5 0.1 reshape.87
  35.6 1.1 fusion.32
  36.7 0.1 reshape.86
  36.8 1.1 fusion.28
  37.9 0.1 reshape.88
  38.1 1.3 collective-permute-start
  39.4 1.8 %collective-permute-done = f32[1,12288]{1,0:T(1,128)S(1)} collective-permute-done((f32[1,12288]{1,0:T(1,128)S(1)}, f32[1,12288]{1,0:T(1,128)S(1)}, u32[]{:S(2)}, u32[]{:S(2)}) %collective-permute-start) | collective-permute-done | bytes 49184 | tf_op jit(solution)/shard_map/ppermute | solution.py:12
  41.2 87.3 %all-gather.2.cloned.1.call-done = bf16[512,12288]{1,0:T(8,128)(2,1)} async-done(((bf16[512,768]{1,0:T(8,128)(2,1)}), bf16[512,12288]{1,0:T(8,128)(2,1)}) %all-gather.2.cloned.1.call-update) | async-done | bytes 12582928 | tf_op jit(solution)/shard_map/all_gather | solution.py:74
  128.5 13.4 %fusion.26 = f32[1,512]{1,0:T(1,128)} fusion(bf16[512,12288]{1,0:T(8,128)(2,1)} %all-gather.2.cloned.1.call-done, f32[1,12288]{1,0:T(1,128)S(1)} %collective-permute-done, f32[2,12288]{1,0:T(2,128)S(1)} %constant_dynamic-update-slice_fusion), kind=kOutput, calls=%fused_computation.27 | convolution fusion | flops 75509760 | bytes 12683264 | tf_op jit(solution)/shard_map/dot_general | solution.py:72
  (6 shorter events, 0.1 us)
Async XLA Ops:
  7.4 1.4 copy-start
  7.4 26.0 %reduce-scatter.4.cloned.1.call-start = ((), (), s32[]{:S(2)}) async-start(), calls=%async_computation.2 | async-start | bytes 442368
  10.4 6.4 %copy-start.2 = (bf16[4096,64]{0,1:T(8,128)(2,1)S(1)}, bf16[4096,64]{0,1:T(8,128)(2,1)}, u32[]{:S(2)}) copy-start(bf16[4096,64]{0,1:T(8,128)(2,1)} %param.23) | copy-start | bytes 1572868
  10.5 7.0 %copy-start.4 = (bf16[192,7168]{1,0:T(8,128)(2,1)S(1)}, bf16[192,7168]{1,0:T(8,128)(2,1)}, u32[]{:S(2)}) copy-start(bf16[192,7168]{1,0:T(8,128)(2,1)} %param.18) | copy-start | bytes 8257540
  10.5 7.0 %copy-start.6 = (bf16[192,7168]{1,0:T(8,128)(2,1)S(1)}, bf16[192,7168]{1,0:T(8,128)(2,1)}, u32[]{:S(2)}) copy-start(bf16[192,7168]{1,0:T(8,128)(2,1)} %param.16) | copy-start | bytes 8257540
  10.5 7.0 %copy-start.7 = (bf16[7168,64]{0,1:T(8,128)(2,1)S(1)}, bf16[7168,64]{0,1:T(8,128)(2,1)}, u32[]{:S(2)}) copy-start(bf16[7168,64]{0,1:T(8,128)(2,1)} %param.24) | copy-start | bytes 2752516
  17.5 1.8 %copy-start.5 = (bf16[192,7168]{1,0:T(8,128)(2,1)S(1)}, bf16[192,7168]{1,0:T(8,128)(2,1)}, u32[]{:S(2)}) copy-start(bf16[192,7168]{1,0:T(8,128)(2,1)} %param.17) | copy-start | bytes 8257540
  17.5 2.0 %copy-start.8 = (bf16[7168,64]{0,1:T(8,128)(2,1)S(1)}, bf16[7168,64]{0,1:T(8,128)(2,1)}, u32[]{:S(2)}) copy-start(bf16[7168,64]{0,1:T(8,128)(2,1)} %param.25) | copy-start | bytes 2752516
  19.5 1.8 %copy-start.1 = (bf16[192,4096]{1,0:T(8,128)(2,1)S(1)}, bf16[192,4096]{1,0:T(8,128)(2,1)}, u32[]{:S(2)}) copy-start(bf16[192,4096]{1,0:T(8,128)(2,1)} %param.19) | copy-start | bytes 4718596
  19.5 1.8 %copy-start.3 = (bf16[4096,64]{0,1:T(8,128)(2,1)S(1)}, bf16[4096,64]{0,1:T(8,128)(2,1)}, u32[]{:S(2)}) copy-start(bf16[4096,64]{0,1:T(8,128)(2,1)} %param.26) | copy-start | bytes 1572868
  19.5 3.9 %copy-start.9 = (s32[192]{0:T(256)S(1)}, s32[192]{0:T(256)}, u32[]{:S(2)}) copy-start(s32[192]{0:T(256)} %param.20) | copy-start | bytes 2308
  22.8 105.7 %all-gather.2.cloned.1.call-start = ((), (), s32[]{:S(2)}) async-start(), calls=%async_computation.1 | async-start | bytes 13369344 | tf_op jit(solution)/shard_map/all_gather | solution.py:74
  38.1 3.1 %collective-permute-start = (f32[1,12288]{1,0:T(1,128)S(1)}, f32[1,12288]{1,0:T(1,128)S(1)}, u32[]{:S(2)}, u32[]{:S(2)}) collective-permute-start(f32[1,12288]{1,0:T(1,128)S(1)} %slice.53), channel_id=1, source_target_pairs={{1,0},{2,1},{3,2},{4,3},{5,4},{6,5},{7,6},{8,7},{9,8},{10,9},{11,1... | collective-permute-start | bytes 147464 | tf_op jit(solution)/shard_map/ppermute | solution.py:12
Sparse Core Ops, SparseCore 0:
  22.9 10.3 reduce-scatter.3
Sparse Core Ops, SparseCore 1:
  25.6 102.9 all-gather.1
where the time goes:
time: 150 us; the launch traced here: 149 us
  waiting for transfers between devices  99.5 us (66%)
  matrix products  29.3 us (20%)
  between operations  15 us (10%)
  local copies, waits for them, and re-layouts  4.09 us (3%)
    all_gather x1, waiting for transfers between devices, body(): lax.all_gather(queries, ('dp', 'mp'), axis=1, tiled=True)  87.3 us
    dot_general x1, matrix products, body(): jnp.dot(own_rows, lax.all_gather(queries, ('dp', 'mp'), axis=1, tiled=Tru...  13.4 us
    unnamed x3, waiting for transfers between devices  10.3 us
    dot_general x1, matrix products, body(): jnp.dot(gate_grad, gate_out, preferred_element_type=jnp.float32)  6.31 us
    dot_general x3, matrix products, per_example(): jnp.einsum('tc,tj->cj', weighted, right, precision=lax.Precision.HIGHEST)  3.22 us
  transfers between devices with their start and end apart: 3, of which 3 were waited for; matrix products, arithmetic and copies ran while one was open for 3% of the time, Pallas kernels for 0%

commit v1 on v0

v1 whole, which is shorter than its diff:
```python
import jax
import jax.numpy as jnp
from jax import lax
from jax.sharding import PartitionSpec as P

HIGHEST = lax.Precision.HIGHEST


def body(
    inputs,
    gate_pre,
    up_pre,
    hidden_grad,
    out_grad,
    example_ids,
    gate_in,
    gate_out,
    up_in,
    up_out,
    down_in,
    down_out,
    queries,
):
    half_rows = inputs.shape[0] // 2
    width = gate_in.shape[1]
    count = lax.axis_size(("dp", "mp"))
    coords = queries.shape[1]
    gate_value = gate_pre.astype(jnp.float32)
    up_value = up_pre.astype(jnp.float32)
    sigmoid_gate = jax.nn.sigmoid(gate_value)
    hidden = (gate_value * sigmoid_gate * up_value).astype(jnp.bfloat16)
    back_value = hidden_grad.astype(jnp.float32)
    gate_grad = (
        back_value * up_value * sigmoid_gate * (1.0 + gate_value * (1.0 - sigmoid_gate))
    ).astype(jnp.bfloat16)
    up_grad = (back_value * gate_value * sigmoid_gate).astype(jnp.bfloat16)
    projected = jnp.concatenate(
        [
            jnp.dot(inputs, gate_in, preferred_element_type=jnp.float32),
            jnp.dot(gate_grad, gate_out, preferred_element_type=jnp.float32),
            jnp.dot(inputs, up_in, preferred_element_type=jnp.float32),
            jnp.dot(up_grad, up_out, preferred_element_type=jnp.float32),
            jnp.dot(hidden, down_in, preferred_element_type=jnp.float32),
            jnp.dot(out_grad, down_out, preferred_element_type=jnp.float32),
        ],
        axis=1,
    )
    core = lax.axis_index("mp")
    kept = lax.dynamic_slice_in_dim(projected, core * half_rows, half_rows, 0)
    given = lax.dynamic_slice_in_dim(projected, (1 - core) * half_rows, half_rows, 0)
    summed = kept + lax.ppermute(given, "mp", [(0, 1), (1, 0)])
    my_ids = lax.dynamic_slice_in_dim(example_ids, core * half_rows, half_rows, 0)
    labels = lax.axis_index(("dp", "mp")) + jnp.arange(-1, 1, dtype=jnp.int32)
    onehot = (my_ids[:, None] == labels[None, :]).astype(jnp.float32)
    modules = []
    for module in range(3):
        left = summed[:, 2 * module * width : (2 * module + 1) * width]
        right = summed[:, (2 * module + 1) * width : (2 * module + 2) * width]
        weighted = onehot.T[:, :, None] * left[None, :, :]
        modules.append(jnp.einsum("cti,tj->cij", weighted, right, precision=HIGHEST))
    partial_value = jnp.stack(modules, axis=1).reshape(2, count, coords)
    received = lax.all_to_all(partial_value, ("dp", "mp"), split_axis=1, concat_axis=0, tiled=True)
    received = received.reshape(count, 2, coords)
    rows = received[:, 1].at[:-1].add(received[1:, 0])
    scores = jnp.einsum("ec,qc->eq", rows, queries.astype(jnp.float32), precision=HIGHEST)
    pieces = lax.all_to_all(scores, ("dp", "mp"), split_axis=0, concat_axis=0, tiled=True)
    return jnp.sum(pieces, axis=0, keepdims=True)


def solution(mesh):
    placed = (
        P(("parts", "dp"), "mp"),
        P(("parts", "dp"), "mp"),
        P(("parts", "dp"), "mp"),
        P(("parts", "dp"), "mp"),
        P(("parts", "dp"), "mp"),
        P(("parts", "dp")),
        P("mp", None),
        P("mp", None),
        P("mp", None),
        P("mp", None),
        P("mp", None),
        P("mp", None),
        P(None, ("dp", "mp")),
    )
    return jax.shard_map(
        body, mesh=mesh, in_specs=placed, out_specs=P(("parts", "dp", "mp"), None), check_vma=False
    )
```

time: 150 us -> 43.1 us (0.29)
  waiting for transfers between devices: 99.5 us -> 0.92 us
  blocking collectives: 0 us -> 23.7 us
  matrix products: 29.3 us -> 14 us
  between operations: 15 us -> 0.24 us
  local copies, waits for them, and re-layouts: 4.09 us -> 2.51 us
    all_gather x1 -> x0, waiting for transfers between devices: 87.3 us -> none  [body(): lax.all_gather(queries, ('dp', 'mp'), axis=1, tiled=True)]
    all_to_all x0 -> x2, blocking collectives: none -> 23.7 us  [the longest x1 14.5 us: body(): lax.all_to_all(partial_value, ('dp', 'mp'), split_axis=1, concat_axis=0,...]
    dot_general x4, matrix products: 16.6 us -> 1.33 us  [the longest x1 0.71 us: body(): jnp.einsum('ec,qc->eq', rows, queries.astype(jnp.float32), precision=HIGH...]
    unnamed x3 -> x0, waiting for transfers between devices: 10.3 us -> none
  transfers between devices with their start and end apart: 3 -> 1, of which waited for: 3 -> 1; matrix products, arithmetic and copies ran while one was open for 3% -> 0% of each run, Pallas kernels for 0% -> 0%
where the time goes in v1:
time: 43.1 us; the launch traced here: 42.8 us
  blocking collectives  23.7 us (55%)
  matrix products  14 us (32%)
  local copies, waits for them, and re-layouts  2.51 us (6%)
  waiting for transfers between devices  0.92 us (2%)
  other arithmetic  0.88 us (2%)
  starting transfers between devices  0.52 us (1%)
    all_to_all x1, blocking collectives, body(): lax.all_to_all(partial_value, ('dp', 'mp'), split_axis=1, concat_axis=0,...  14.5 us
    all_to_all x1, blocking collectives, body(): lax.all_to_all(scores, ('dp', 'mp'), split_axis=0, concat_axis=0, tiled=T...  9.2 us
    dot_general x1, matrix products, body(): jnp.dot(gate_grad, gate_out, preferred_element_type=jnp.float32)  6.31 us
    dot_general x1, matrix products, body(): jnp.dot(hidden, down_in, preferred_element_type=jnp.float32)  1.75 us
    dot_general x1, matrix products, body(): jnp.dot(up_grad, up_out, preferred_element_type=jnp.float32)  1.74 us
    unnamed x24, local copies, waits for them, and re-layouts  1.72 us
    dot_general x1, matrix products, body(): jnp.dot(inputs, gate_in, preferred_element_type=jnp.float32)  1.66 us
    ppermute x1, waiting for transfers between devices, body(): summed = kept + lax.ppermute(given, 'mp', [(0, 1), (1, 0)])  0.92 us
  transfers between devices with their start and end apart: 1, of which 1 were waited for; matrix products, arithmetic and copies ran while one was open for 0% of the time, Pallas kernels for 0%

profile of v1, /device:TPU:0, one launch (start us, length us, event | category | flops | bytes accessed | tf_op | source)
XLA Modules:
  0.0 42.8 jit_solution(2574657737346240345)
XLA Ops:
  0.0 0.0 copy-start
  0.0 1.4 %copy-done = bf16[192,4096]{1,0:T(8,128)(2,1)S(1)} copy-done((bf16[192,4096]{1,0:T(8,128)(2,1)S(1)}, bf16[192,4096]{1,0:T(8,128)(2,1)}, u32[]{:S(2)}) %copy-start) | copy-done | bytes 1572888
  1.4 1.7 %convolution_dynamic-update-slice_fusion.2 = f32[192,384]{0,1:T(8,128)S(1)} fusion(bf16[192,4096]{1,0:T(8,128)(2,1)S(1)} %copy-done, bf16[4096,64]{0,1:T(8,128)(2,1)} %param.21), kind=kOutput, calls=%fused_computation.21 | convolution fusion | flops 100663296 | bytes 2162688 | tf_op jit(solution)/shard_map/dot_general | solution.py:39
  3.1 0.0 copy-start.3
  3.1 0.0 copy-start.5
  3.1 0.0 copy-start.7
  3.1 0.0 copy-start.8
  3.1 6.3 %fusion.16 = f32[192,384]{0,1:T(8,128)S(1)} fusion(f32[192,384]{0,1:T(8,128)S(1)} %convolution_dynamic-update-slice_fusion.2, bf16[7168,64]{0,1:T(8,128)(2,1)} %param.22, bf16[192,7168]{1,0:T(8,128)(2,1)} %param.17, bf16[192,7168]{1,0:T(8,128)(2,1)} %param.18, bf16[192,7168]{1,0:T(8,128)(2,1)} %param.16), kind=kOutput, calls=%fused_computation.22 | convolution fusion | flops 194052096 | bytes 9240576 | tf_op jit(solution)/shard_map/dot_general | solution.py:40
  9.4 0.0 copy-done.3
  9.4 0.6 %convolution_dynamic-update-slice_fusion.1 = f32[192,384]{0,1:T(8,128)S(1)} fusion(f32[192,384]{0,1:T(8,128)S(1)} %fusion.16, bf16[192,4096]{1,0:T(8,128)(2,1)S(1)} %copy-done, bf16[4096,64]{0,1:T(8,128)(2,1)S(1)} %copy-done.3), kind=kOutput, calls=%fused_computation.20 | convolution fusion | flops 100663296 | bytes 2162688 | tf_op jit(solution)/shard_map/dot_general | solution.py:41
  10.1 0.0 copy-done.5
  10.1 0.0 copy-done.7
  10.1 0.0 copy-done.8
  10.1 0.0 copy-start.6
  10.1 0.0 copy-start.9
  10.1 1.7 %fusion.22 = f32[192,384]{0,1:T(8,128)S(1)} fusion(f32[192,384]{0,1:T(8,128)S(1)} %convolution_dynamic-update-slice_fusion.1, bf16[7168,64]{0,1:T(8,128)(2,1)S(1)} %copy-done.8, bf16[192,7168]{1,0:T(8,128)(2,1)S(1)} %copy-done.7, bf16[192,7168]{1,0:T(8,128)(2,1)S(1)} %copy-done.5), kind=kOutput, calls=%fused_computation.24 | convolution fusion | flops 187170816 | bytes 6488064 | tf_op jit(solution)/shard_map/dot_general | solution.py:42
  11.9 0.0 copy-done.6
  11.9 0.2 copy-done.9
  12.1 0.0 copy-start.1
  12.1 0.0 copy-start.4
  12.1 0.0 copy-start.10
  12.1 1.7 %fusion.19 = f32[192,384]{0,1:T(8,128)S(1)} fusion(f32[192,384]{0,1:T(8,128)S(1)} %fusion.22, bf16[7168,64]{0,1:T(8,128)(2,1)S(1)} %copy-done.9, bf16[192,7168]{1,0:T(8,128)(2,1)S(1)} %copy-done.6, bf16[192,7168]{1,0:T(8,128)(2,1)S(1)} %copy-done.7), kind=kOutput, calls=%fused_computation.23 | convolution fusion | flops 187170816 | bytes 6488064 | tf_op jit(solution)/shard_map/dot_general | solution.py:43
  13.9 0.0 copy-done.1
  13.9 0.0 copy-done.4
  13.9 0.0 copy-start.2
  13.9 0.6 %convolution_dynamic-update-slice_fusion = f32[192,384]{0,1:T(8,128)S(1)} fusion(f32[192,384]{0,1:T(8,128)S(1)} %fusion.19, bf16[192,4096]{1,0:T(8,128)(2,1)S(1)} %copy-done.1, bf16[4096,64]{0,1:T(8,128)(2,1)S(1)} %copy-done.4), kind=kOutput, calls=%fused_computation.19 | convolution fusion | flops 100663296 | bytes 2162688 | tf_op jit(solution)/shard_map/dot_general | solution.py:44
  14.5 0.1 constant_dynamic-slice_fusion
  14.6 0.5 %collective-permute-start = (f32[96,384]{0,1:T(8,128)S(1)}, f32[96,384]{0,1:T(8,128)S(1)}, u32[]{:S(2)}, u32[]{:S(2)}) collective-permute-start(f32[96,384]{0,1:T(8,128)S(1)} %constant_dynamic-slice_fusion), channel_id=1, source_target_pairs={{0,1},{1,0},{2,3},{3,2},{4,5},{5,4},{6,7},{7,6},{8,9},{9,8},{10,11... | collective-permute-start | bytes 442376 | tf_op jit(solution)/shard_map/ppermute | solution.py:51
  15.2 0.0 copy-done.10
  15.2 0.1 dynamic_slice.9
  15.2 0.1 compare_convert_fusion
  15.3 0.9 %collective-permute-done = f32[96,384]{0,1:T(8,128)S(1)} collective-permute-done((f32[96,384]{0,1:T(8,128)S(1)}, f32[96,384]{0,1:T(8,128)S(1)}, u32[]{:S(2)}, u32[]{:S(2)}) %collective-permute-start) | collective-permute-done | bytes 147488 | tf_op jit(solution)/shard_map/ppermute | solution.py:51
  16.2 0.1 dynamic-slice_add_fusion
  16.4 0.2 convolution_bitcast_fusion.2
  16.6 0.2 convolution_bitcast_fusion.1
  16.8 0.2 convolution_bitcast_fusion
  17.1 0.1 reshape.72
  17.2 0.1 copy.16
  17.3 14.5 %all_to_all.24 = f32[2,16,768]{2,0,1:T(2,128)S(1)} all-to-all(f32[2,16,768]{2,0,1:T(2,128)S(1)} %copy.16), channel_id=1, replica_groups=mesh['parts'=2,'dp'=8,'mp'=2] {'dp','mp'}, dimensions={1} | all-to-all | bytes 196608 | tf_op jit(solution)/shard_map/all_to_all | solution.py:62
  31.8 0.1 slice.59
  31.8 0.1 slice_add_fusion
  31.9 0.3 scatter-add.4
  32.2 0.0 copy-done.2
  32.2 0.7 %convolution_bitcast_fusion.3 = f32[16,1,512]{2,0,1:T(8,128)S(1)} fusion(f32[16,768]{1,0:T(8,128)S(1)} %scatter-add.4, bf16[512,768]{1,0:T(8,128)(2,1)S(1)} %copy-done.2), kind=kOutput, calls=%fused_computation.28 | convolution fusion | flops 75497472 | bytes 868352 | tf_op jit(solution)/shard_map/ec,qc->eq/dot_general | solution.py:65
  33.0 9.2 %all_to_all.25 = f32[16,1,512]{2,1,0:T(1,128)S(1)} all-to-all(f32[16,1,512]{2,1,0:T(1,128)S(1)} %copy.17), channel_id=1, replica_groups=mesh['parts'=2,'dp'=8,'mp'=2] {'dp','mp'}, dimensions={0} | all-to-all | bytes 65536 | tf_op jit(solution)/shard_map/all_to_all | solution.py:66
  42.2 0.6 %reduce_sum.9 = f32[512]{0:T(512)} reduce(f32[16,1,512]{2,1,0:T(1,128)S(1)} %all_to_all.25, f32[]{:T(128)} %constant.51.clone.1), dimensions={0,1}, to_apply=%region_0.0 | reduce | flops 7680 | bytes 34820 | tf_op jit(solution)/shard_map/reduce_sum | solution.py:67
  (7 shorter events, 0.1 us)
Async XLA Ops:
  0.0 1.4 %copy-start = (bf16[192,4096]{1,0:T(8,128)(2,1)S(1)}, bf16[192,4096]{1,0:T(8,128)(2,1)}, u32[]{:S(2)}) copy-start(bf16[192,4096]{1,0:T(8,128)(2,1)} %param.15) | copy-start | bytes 4718596
  3.1 6.4 %copy-start.3 = (bf16[4096,64]{0,1:T(8,128)(2,1)S(1)}, bf16[4096,64]{0,1:T(8,128)(2,1)}, u32[]{:S(2)}) copy-start(bf16[4096,64]{0,1:T(8,128)(2,1)} %param.23) | copy-start | bytes 1572868
  3.1 7.0 %copy-start.5 = (bf16[192,7168]{1,0:T(8,128)(2,1)S(1)}, bf16[192,7168]{1,0:T(8,128)(2,1)}, u32[]{:S(2)}) copy-start(bf16[192,7168]{1,0:T(8,128)(2,1)} %param.18) | copy-start | bytes 8257540
  3.1 7.0 %copy-start.7 = (bf16[192,7168]{1,0:T(8,128)(2,1)S(1)}, bf16[192,7168]{1,0:T(8,128)(2,1)}, u32[]{:S(2)}) copy-start(bf16[192,7168]{1,0:T(8,128)(2,1)} %param.16) | copy-start | bytes 8257540
  3.1 7.0 %copy-start.8 = (bf16[7168,64]{0,1:T(8,128)(2,1)S(1)}, bf16[7168,64]{0,1:T(8,128)(2,1)}, u32[]{:S(2)}) copy-start(bf16[7168,64]{0,1:T(8,128)(2,1)} %param.24) | copy-start | bytes 2752516
  10.1 1.8 %copy-start.6 = (bf16[192,7168]{1,0:T(8,128)(2,1)S(1)}, bf16[192,7168]{1,0:T(8,128)(2,1)}, u32[]{:S(2)}) copy-start(bf16[192,7168]{1,0:T(8,128)(2,1)} %param.17) | copy-start | bytes 8257540
  10.1 2.0 %copy-start.9 = (bf16[7168,64]{0,1:T(8,128)(2,1)S(1)}, bf16[7168,64]{0,1:T(8,128)(2,1)}, u32[]{:S(2)}) copy-start(bf16[7168,64]{0,1:T(8,128)(2,1)} %param.25) | copy-start | bytes 2752516
  12.1 1.8 %copy-start.1 = (bf16[192,4096]{1,0:T(8,128)(2,1)S(1)}, bf16[192,4096]{1,0:T(8,128)(2,1)}, u32[]{:S(2)}) copy-start(bf16[192,4096]{1,0:T(8,128)(2,1)} %param.19) | copy-start | bytes 4718596
  12.1 1.8 %copy-start.4 = (bf16[4096,64]{0,1:T(8,128)(2,1)S(1)}, bf16[4096,64]{0,1:T(8,128)(2,1)}, u32[]{:S(2)}) copy-start(bf16[4096,64]{0,1:T(8,128)(2,1)} %param.26) | copy-start | bytes 1572868
  12.1 3.1 %copy-start.10 = (s32[192]{0:T(256)S(1)}, s32[192]{0:T(256)}, u32[]{:S(2)}) copy-start(s32[192]{0:T(256)} %param.20) | copy-start | bytes 2308
  13.9 18.3 %copy-start.2 = (bf16[512,768]{1,0:T(8,128)(2,1)S(1)}, bf16[512,768]{1,0:T(8,128)(2,1)}, u32[]{:S(2)}) copy-start(bf16[512,768]{1,0:T(8,128)(2,1)} %param.27) | copy-start | bytes 2359300
  14.6 1.6 %collective-permute-start = (f32[96,384]{0,1:T(8,128)S(1)}, f32[96,384]{0,1:T(8,128)S(1)}, u32[]{:S(2)}, u32[]{:S(2)}) collective-permute-start(f32[96,384]{0,1:T(8,128)S(1)} %constant_dynamic-slice_fusion), channel_id=1, source_target_pairs={{0,1},{1,0},{2,3},{3,2},{4,5},{5,4},{6,7},{7,6},{8,9},{9,8},{10,11... | collective-permute-start | bytes 442376 | tf_op jit(solution)/shard_map/ppermute | solution.py:51

commit v2 on v1

--- a/solution.py
+++ b/solution.py
@@ -23,7 +23,9 @@
 ):
     half_rows = inputs.shape[0] // 2
     width = gate_in.shape[1]
-    count = lax.axis_size(("dp", "mp"))
+    chips = lax.axis_size("dp")
+    swap = [(0, 1), (1, 0)]
+    other_queries = lax.ppermute(queries, "mp", swap)
     coords = queries.shape[1]
     gate_value = gate_pre.astype(jnp.float32)
     up_value = up_pre.astype(jnp.float32)
@@ -48,7 +50,7 @@
     core = lax.axis_index("mp")
     kept = lax.dynamic_slice_in_dim(projected, core * half_rows, half_rows, 0)
     given = lax.dynamic_slice_in_dim(projected, (1 - core) * half_rows, half_rows, 0)
-    summed = kept + lax.ppermute(given, "mp", [(0, 1), (1, 0)])
+    summed = kept + lax.ppermute(given, "mp", swap)
     my_ids = lax.dynamic_slice_in_dim(example_ids, core * half_rows, half_rows, 0)
     labels = lax.axis_index(("dp", "mp")) + jnp.arange(-1, 1, dtype=jnp.int32)
     onehot = (my_ids[:, None] == labels[None, :]).astype(jnp.float32)
@@ -58,12 +60,21 @@
         right = summed[:, (2 * module + 1) * width : (2 * module + 2) * width]
         weighted = onehot.T[:, :, None] * left[None, :, :]
         modules.append(jnp.einsum("cti,tj->cij", weighted, right, precision=HIGHEST))
-    partial_value = jnp.stack(modules, axis=1).reshape(2, count, coords)
-    received = lax.all_to_all(partial_value, ("dp", "mp"), split_axis=1, concat_axis=0, tiled=True)
-    received = received.reshape(count, 2, coords)
-    rows = received[:, 1].at[:-1].add(received[1:, 0])
-    scores = jnp.einsum("ec,qc->eq", rows, queries.astype(jnp.float32), precision=HIGHEST)
-    pieces = lax.all_to_all(scores, ("dp", "mp"), split_axis=0, concat_axis=0, tiled=True)
+    partial_value = jnp.stack(modules, axis=1).reshape(2, chips, 2 * coords)
+    received = lax.all_to_all(partial_value, "dp", split_axis=1, concat_axis=0, tiled=True)
+    received = received.reshape(2 * chips, 2, coords)
+    first, second = jnp.where(core == 0, 0, 1), jnp.where(core == 0, 1, 0)
+    pair_queries = jnp.concatenate([queries, other_queries], axis=1).astype(jnp.float32)
+    swapped = jnp.concatenate(
+        [jnp.take(received, first, axis=1), jnp.take(received, second, axis=1)], axis=1
+    )
+    scores = jnp.einsum("ec,qc->eq", swapped, pair_queries, precision=HIGHEST)
+    scores = scores.reshape(chips, 2, -1)
+    early = scores[:, 0]
+    moved = jnp.concatenate([early[1:], jnp.zeros_like(early[:1])], axis=0)
+    sent = jnp.where(core == 0, moved, early)
+    mine = scores[:, 1] + lax.ppermute(sent, "mp", swap)
+    pieces = lax.all_to_all(mine, "dp", split_axis=0, concat_axis=0, tiled=True)
     return jnp.sum(pieces, axis=0, keepdims=True)
 
 

time: 43.1 us -> 46.2 us (1.072)
  blocking collectives: 23.7 us -> 8.94 us
  waiting for transfers between devices: 0.92 us -> 9.12 us
  starting transfers between devices: 0.52 us -> 7.88 us
  matrix products: 14 us -> 15.8 us
    all_to_all x2 -> x1, blocking collectives: 23.7 us -> 8.94 us  [body(): pieces = lax.all_to_all(mine, 'dp', split_axis=0, concat_axis=0, tiled=True)]
    all_to_all x0 -> x1, starting transfers between devices: none -> 7.2 us  [body(): lax.all_to_all(partial_value, 'dp', split_axis=1, concat_axis=0, tiled=True)]
    all_to_all x0 -> x1, waiting for transfers between devices: none -> 7.12 us  [body(): lax.all_to_all(partial_value, 'dp', split_axis=1, concat_axis=0, tiled=True)]
    dot_general x1, matrix products: 0.71 us -> 2.45 us  [body(): scores = jnp.einsum('ec,qc->eq', swapped, pair_queries, precision=HIGHEST)]
    ppermute x1 -> x3, waiting for transfers between devices: 0.92 us -> 2 us  [the longest x1 1.17 us: body(): mine = scores[:, 1] + lax.ppermute(sent, 'mp', swap)]
    reshape x2 -> x4, local copies, waits for them, and re-layouts: 0.18 us -> 0.96 us  [the longest x2 0.81 us: body(): partial_value = jnp.stack(modules, axis=1).reshape(2, chips, 2 * coords)]
    unnamed x24 -> x23, local copies, waits for them, and re-layouts: 1.72 us -> 1.71 us
  transfers between devices with their start and end apart: 1 -> 4, of which waited for: 1 -> 3; matrix products, arithmetic and copies ran while one was open for 0% -> 4% of each run, Pallas kernels for 0% -> 0%
where the time goes in v2:
time: 46.2 us; the launch traced here: 45.9 us
  matrix products  15.8 us (34%)
  waiting for transfers between devices  9.12 us (20%)
  blocking collectives  8.94 us (19%)
  starting transfers between devices  7.88 us (17%)
  local copies, waits for them, and re-layouts  2.94 us (6%)
  other arithmetic  0.94 us (2%)
    all_to_all x1, blocking collectives, body(): pieces = lax.all_to_all(mine, 'dp', split_axis=0, concat_axis=0, tiled=True)  8.94 us
    all_to_all x1, starting transfers between devices, body(): lax.all_to_all(partial_value, 'dp', split_axis=1, concat_axis=0, tiled=True)  7.2 us
    all_to_all x1, waiting for transfers between devices, body(): lax.all_to_all(partial_value, 'dp', split_axis=1, concat_axis=0, tiled=True)  7.12 us
    dot_general x1, matrix products, body(): jnp.dot(gate_grad, gate_out, preferred_element_type=jnp.float32)  6.31 us
    dot_general x1, matrix products, body(): scores = jnp.einsum('ec,qc->eq', swapped, pair_queries, precision=HIGHEST)  2.45 us
    dot_general x1, matrix products, body(): jnp.dot(hidden, down_in, preferred_element_type=jnp.float32)  1.75 us
    dot_general x1, matrix products, body(): jnp.dot(up_grad, up_out, preferred_element_type=jnp.float32)  1.74 us
    unnamed x23, local copies, waits for them, and re-layouts  1.71 us
  transfers between devices with their start and end apart: 4, of which 3 were waited for; matrix products, arithmetic and copies ran while one was open for 4% of the time, Pallas kernels for 0%

profile of v2, /device:TPU:0, one launch (start us, length us, event | category | flops | bytes accessed | tf_op | source)
XLA Modules:
  0.0 45.9 jit_solution(14316557878738432433)
XLA Ops:
  0.0 0.0 copy-start
  0.0 1.4 %copy-done = bf16[192,4096]{1,0:T(8,128)(2,1)S(1)} copy-done((bf16[192,4096]{1,0:T(8,128)(2,1)S(1)}, bf16[192,4096]{1,0:T(8,128)(2,1)}, u32[]{:S(2)}) %copy-start) | copy-done | bytes 1572888
  1.4 1.7 %convolution_dynamic-update-slice_fusion.2 = f32[192,384]{0,1:T(8,128)S(1)} fusion(bf16[192,4096]{1,0:T(8,128)(2,1)S(1)} %copy-done, bf16[4096,64]{0,1:T(8,128)(2,1)} %param.21), kind=kOutput, calls=%fused_computation.25 | convolution fusion | flops 100663296 | bytes 2162688 | tf_op jit(solution)/shard_map/dot_general | solution.py:41
  3.1 0.0 copy-start.2
  3.1 0.0 copy-start.4
  3.1 0.0 copy-start.6
  3.1 0.0 copy-start.7
  3.1 6.3 %fusion.20 = f32[192,384]{0,1:T(8,128)S(1)} fusion(f32[192,384]{0,1:T(8,128)S(1)} %convolution_dynamic-update-slice_fusion.2, bf16[7168,64]{0,1:T(8,128)(2,1)} %param.22, bf16[192,7168]{1,0:T(8,128)(2,1)} %param.17, bf16[192,7168]{1,0:T(8,128)(2,1)} %param.18, bf16[192,7168]{1,0:T(8,128)(2,1)} %param.16), kind=kOutput, calls=%fused_computation.26 | convolution fusion | flops 194052096 | bytes 9240576 | tf_op jit(solution)/shard_map/dot_general | solution.py:42
  9.4 0.0 copy-done.2
  9.4 0.6 %convolution_dynamic-update-slice_fusion.1 = f32[192,384]{0,1:T(8,128)S(1)} fusion(f32[192,384]{0,1:T(8,128)S(1)} %fusion.20, bf16[192,4096]{1,0:T(8,128)(2,1)S(1)} %copy-done, bf16[4096,64]{0,1:T(8,128)(2,1)S(1)} %copy-done.2), kind=kOutput, calls=%fused_computation.24 | convolution fusion | flops 100663296 | bytes 2162688 | tf_op jit(solution)/shard_map/dot_general | solution.py:43
  10.1 0.0 copy-done.4
  10.1 0.0 copy-done.6
  10.1 0.0 copy-done.7
  10.1 0.0 copy-start.5
  10.1 0.0 copy-start.8
  10.1 1.7 %fusion.26 = f32[192,384]{0,1:T(8,128)S(1)} fusion(f32[192,384]{0,1:T(8,128)S(1)} %convolution_dynamic-update-slice_fusion.1, bf16[7168,64]{0,1:T(8,128)(2,1)S(1)} %copy-done.7, bf16[192,7168]{1,0:T(8,128)(2,1)S(1)} %copy-done.6, bf16[192,7168]{1,0:T(8,128)(2,1)S(1)} %copy-done.4), kind=kOutput, calls=%fused_computation.28 | convolution fusion | flops 187170816 | bytes 6488064 | tf_op jit(solution)/shard_map/dot_general | solution.py:44
  11.9 0.0 copy-done.5
  11.9 0.2 copy-done.8
  12.1 0.0 copy-start.1
  12.1 0.0 copy-start.3
  12.1 1.8 %fusion.23 = f32[192,384]{0,1:T(8,128)S(1)} fusion(f32[192,384]{0,1:T(8,128)S(1)} %fusion.26, bf16[7168,64]{0,1:T(8,128)(2,1)S(1)} %copy-done.8, bf16[192,7168]{1,0:T(8,128)(2,1)S(1)} %copy-done.5, bf16[192,7168]{1,0:T(8,128)(2,1)S(1)} %copy-done.6), kind=kOutput, calls=%fused_computation.27 | convolution fusion | flops 187170816 | bytes 6488064 | tf_op jit(solution)/shard_map/dot_general | solution.py:45
  13.9 0.0 copy-done.1
  13.9 0.0 copy-done.3
  13.9 0.6 %convolution_dynamic-update-slice_fusion = f32[192,384]{0,1:T(8,128)S(1)} fusion(f32[192,384]{0,1:T(8,128)S(1)} %fusion.23, bf16[192,4096]{1,0:T(8,128)(2,1)S(1)} %copy-done.1, bf16[4096,64]{0,1:T(8,128)(2,1)S(1)} %copy-done.3), kind=kOutput, calls=%fused_computation.23 | convolution fusion | flops 100663296 | bytes 2162688 | tf_op jit(solution)/shard_map/dot_general | solution.py:46
  14.5 0.1 constant_dynamic-slice_fusion.1
  14.6 0.5 %collective-permute-start = (f32[96,384]{0,1:T(8,128)S(1)}, f32[96,384]{0,1:T(8,128)S(1)}, u32[]{:S(2)}, u32[]{:S(2)}) collective-permute-start(f32[96,384]{0,1:T(8,128)S(1)} %constant_dynamic-slice_fusion.1), channel_id=1, source_target_pairs={{0,1},{1,0},{2,3},{3,2},{4,5},{5,4},{6,7},{7,6},{8,9},{9,8},{10,11... | collective-permute-start | bytes 442376 | tf_op jit(solution)/shard_map/ppermute | solution.py:53
  15.2 0.0 copy-done.9
  15.2 0.1 collective-permute-start.1
  15.3 0.0 copy-done.10
  15.3 0.1 dynamic_slice.9
  15.3 0.1 compare_convert_fusion
  15.4 0.8 %collective-permute-done = f32[96,384]{0,1:T(8,128)S(1)} collective-permute-done((f32[96,384]{0,1:T(8,128)S(1)}, f32[96,384]{0,1:T(8,128)S(1)}, u32[]{:S(2)}, u32[]{:S(2)}) %collective-permute-start) | collective-permute-done | bytes 147488 | tf_op jit(solution)/shard_map/ppermute | solution.py:53
  16.2 0.1 dynamic-slice_add_fusion
  16.4 0.2 convolution_bitcast_fusion.2
  16.6 0.2 convolution_bitcast_fusion
  16.8 0.2 convolution_bitcast_fusion.1
  17.1 0.1 reshape.49
  17.2 0.7 %copy.23 = f32[2,8,1536]{2,0,1:T(2,128)} copy(f32[2,8,1536]{2,1,0:T(8,128)S(1)} %reshape.49) | data formatting | bytes 196608 | tf_op jit(solution)/shard_map/reshape | solution.py:63
  17.9 7.2 %all-to-all-start = ((f32[2,8,1536]{2,0,1:T(2,128)}), f32[2,8,1536]{2,0,1:T(2,128)S(1)}, u32[]{:S(2)}, u32[]{:S(2)}) async-start(f32[2,8,1536]{2,0,1:T(2,128)} %copy.23), calls=%async_computation | async-start | bytes 196608 | tf_op jit(solution)/shard_map/all_to_all | solution.py:64
  25.1 7.1 %all-to-all-done = f32[2,8,1536]{2,0,1:T(2,128)S(1)} async-done(((f32[2,8,1536]{2,0,1:T(2,128)}), f32[2,8,1536]{2,0,1:T(2,128)S(1)}, u32[]{:S(2)}, u32[]{:S(2)}) %all-to-all-start) | async-done | bytes 98336 | tf_op jit(solution)/shard_map/all_to_all | solution.py:64
  32.2 0.1 reshape.50
  32.3 0.1 constant_dynamic-slice_fusion
  32.4 0.0 collective-permute-done.1
  32.5 2.4 %fusion.16 = f32[16,512]{1,0:T(8,128)S(1)} fusion(bf16[512,768]{1,0:T(8,128)(2,1)} %collective-permute-done.1, bf16[512,768]{1,0:T(8,128)(2,1)S(1)} %copy-done.9, f32[16,768]{1,0:T(8,128)S(1)} %get-tuple-element.25, f32[16,768]{1,0:T(8,128)S(1)} %get-tuple-element.24), kind=kOutput, calls=%fused_computation.19 | convolution fusion | flops 154165248 | bytes 1703936 | tf_op jit(solution)/shard_map/ec,qc->eq/dot_general | solution.py:71
  35.0 0.1 collective-permute-start.2
  35.1 1.2 %collective-permute-done.2 = f32[8,512]{1,0:T(8,128)S(1)} collective-permute-done((f32[8,512]{1,0:T(8,128)S(1)}, f32[8,512]{1,0:T(8,128)S(1)}, u32[]{:S(2)}, u32[]{:S(2)}) %collective-permute-start.2) | collective-permute-done | bytes 16416 | tf_op jit(solution)/shard_map/ppermute | solution.py:76
  36.3 8.9 %all_to_all.24 = f32[8,1,512]{2,1,0:T(1,128)S(1)} all-to-all(f32[8,1,512]{2,1,0:T(1,128)S(1)} %all_to_all.20), channel_id=1, replica_groups=mesh['parts'=2,'dp'=8,'mp'=2] {'dp'}, dimensions={0} | all-to-all | bytes 32768 | tf_op jit(solution)/shard_map/all_to_all | solution.py:77
  45.2 0.6 %reduce_sum.9 = f32[512]{0:T(512)} reduce(f32[8,1,512]{2,1,0:T(1,128)S(1)} %all_to_all.24, f32[]{:T(128)} %constant.13.clone.1), dimensions={0,1}, to_apply=%region_0.2 | reduce | flops 3584 | bytes 18436 | tf_op jit(solution)/shard_map/reduce_sum | solution.py:78
  (14 shorter events, 0.2 us)
Async XLA Ops:
  0.0 1.4 %copy-start = (bf16[192,4096]{1,0:T(8,128)(2,1)S(1)}, bf16[192,4096]{1,0:T(8,128)(2,1)}, u32[]{:S(2)}) copy-start(bf16[192,4096]{1,0:T(8,128)(2,1)} %param.15) | copy-start | bytes 4718596
  3.1 6.4 %copy-start.2 = (bf16[4096,64]{0,1:T(8,128)(2,1)S(1)}, bf16[4096,64]{0,1:T(8,128)(2,1)}, u32[]{:S(2)}) copy-start(bf16[4096,64]{0,1:T(8,128)(2,1)} %param.23) | copy-start | bytes 1572868
  3.1 7.0 %copy-start.4 = (bf16[192,7168]{1,0:T(8,128)(2,1)S(1)}, bf16[192,7168]{1,0:T(8,128)(2,1)}, u32[]{:S(2)}) copy-start(bf16[192,7168]{1,0:T(8,128)(2,1)} %param.18) | copy-start | bytes 8257540
  3.1 7.0 %copy-start.6 = (bf16[192,7168]{1,0:T(8,128)(2,1)S(1)}, bf16[192,7168]{1,0:T(8,128)(2,1)}, u32[]{:S(2)}) copy-start(bf16[192,7168]{1,0:T(8,128)(2,1)} %param.16) | copy-start | bytes 8257540
  3.1 7.0 %copy-start.7 = (bf16[7168,64]{0,1:T(8,128)(2,1)S(1)}, bf16[7168,64]{0,1:T(8,128)(2,1)}, u32[]{:S(2)}) copy-start(bf16[7168,64]{0,1:T(8,128)(2,1)} %param.24) | copy-start | bytes 2752516
  10.1 1.8 %copy-start.5 = (bf16[192,7168]{1,0:T(8,128)(2,1)S(1)}, bf16[192,7168]{1,0:T(8,128)(2,1)}, u32[]{:S(2)}) copy-start(bf16[192,7168]{1,0:T(8,128)(2,1)} %param.17) | copy-start | bytes 8257540
  10.1 2.0 %copy-start.8 = (bf16[7168,64]{0,1:T(8,128)(2,1)S(1)}, bf16[7168,64]{0,1:T(8,128)(2,1)}, u32[]{:S(2)}) copy-start(bf16[7168,64]{0,1:T(8,128)(2,1)} %param.25) | copy-start | bytes 2752516
  12.1 1.8 %copy-start.1 = (bf16[192,4096]{1,0:T(8,128)(2,1)S(1)}, bf16[192,4096]{1,0:T(8,128)(2,1)}, u32[]{:S(2)}) copy-start(bf16[192,4096]{1,0:T(8,128)(2,1)} %param.19) | copy-start | bytes 4718596
  12.1 1.8 %copy-start.3 = (bf16[4096,64]{0,1:T(8,128)(2,1)S(1)}, bf16[4096,64]{0,1:T(8,128)(2,1)}, u32[]{:S(2)}) copy-start(bf16[4096,64]{0,1:T(8,128)(2,1)} %param.26) | copy-start | bytes 1572868
  12.1 3.0 %copy-start.9 = (bf16[512,768]{1,0:T(8,128)(2,1)S(1)}, bf16[512,768]{1,0:T(8,128)(2,1)}, u32[]{:S(2)}) copy-start(bf16[512,768]{1,0:T(8,128)(2,1)} %param.27) | copy-start | bytes 2359300
  12.1 3.1 %copy-start.10 = (s32[192]{0:T(256)S(1)}, s32[192]{0:T(256)}, u32[]{:S(2)}) copy-start(s32[192]{0:T(256)} %param.20) | copy-start | bytes 2308
  14.6 1.6 %collective-permute-start = (f32[96,384]{0,1:T(8,128)S(1)}, f32[96,384]{0,1:T(8,128)S(1)}, u32[]{:S(2)}, u32[]{:S(2)}) collective-permute-start(f32[96,384]{0,1:T(8,128)S(1)} %constant_dynamic-slice_fusion.1), channel_id=1, source_target_pairs={{0,1},{1,0},{2,3},{3,2},{4,5},{5,4},{6,7},{7,6},{8,9},{9,8},{10,11... | collective-permute-start | bytes 442376 | tf_op jit(solution)/shard_map/ppermute | solution.py:53
  15.2 17.3 %collective-permute-start.1 = (bf16[512,768]{1,0:T(8,128)(2,1)S(1)}, bf16[512,768]{1,0:T(8,128)(2,1)}, u32[]{:S(2)}, u32[]{:S(2)}) collective-permute-start(bf16[512,768]{1,0:T(8,128)(2,1)S(1)} %copy-done.9), channel_id=1, source_target_pairs={{0,1},{1,0},{2,3},{3,2},{4,5},{5,4},{6,7},{7,6},{8,9},{9,8},{10,11... | collective-permute-start | bytes 2359304 | tf_op jit(solution)/shard_map/ppermute | solution.py:28
  17.9 14.3 %all-to-all-start = ((f32[2,8,1536]{2,0,1:T(2,128)}), f32[2,8,1536]{2,0,1:T(2,128)S(1)}, u32[]{:S(2)}, u32[]{:S(2)}) async-start(f32[2,8,1536]{2,0,1:T(2,128)} %copy.23), calls=%async_computation | async-start | bytes 196608 | tf_op jit(solution)/shard_map/all_to_all | solution.py:64
  35.0 1.2 %collective-permute-start.2 = (f32[8,512]{1,0:T(8,128)S(1)}, f32[8,512]{1,0:T(8,128)S(1)}, u32[]{:S(2)}, u32[]{:S(2)}) collective-permute-start(f32[8,512]{1,0:T(8,128)S(1)} %fusion.42), channel_id=1, source_target_pairs={{0,1},{1,0},{2,3},{3,2},{4,5},{5,4},{6,7},{7,6},{8,9},{9,8},{10,11... | collective-permute-start | bytes 49160 | tf_op jit(solution)/shard_map/ppermute | solution.py:76

commit v3 on v1

v3 whole, which is shorter than its diff:
```python
import functools

import jax
import jax.numpy as jnp
from jax import lax
from jax.experimental import pallas as pl
from jax.experimental.pallas import tpu as pltpu
from jax.sharding import PartitionSpec as P

HIGHEST = lax.Precision.HIGHEST
NT = (((1,), (1,)), ((), ()))
STEP = 1024
ROWS = 16
AHEAD = 3


def project(
    inputs,
    gate_pre,
    up_pre,
    hidden_grad,
    out_grad,
    gate_in,
    gate_out,
    up_in,
    up_out,
    down_in,
    down_out,
    out,
    v_inputs,
    v_gate,
    v_up,
    v_back,
    v_out_grad,
    v_in,
    v_gate_out,
    v_up_out,
    v_down_in,
    v_down_out,
    made,
    sems,
):
    width = gate_in.shape[0]
    tokens = inputs.shape[0]
    hidden_steps = gate_pre.shape[1] // STEP
    model_steps = inputs.shape[1] // STEP
    copies = []

    def plan(pairs):
        made_here = []
        for source, target in pairs:
            copy = pltpu.make_async_copy(source, target, sems.at[sum(map(len, copies)) + len(made_here)])
            made_here.append(copy)
        copies.append(made_here)

    for step in range(hidden_steps):
        at = pl.ds(step * STEP, STEP)
        pairs = [
            (gate_pre.at[:, at], v_gate.at[:, at]),
            (up_pre.at[:, at], v_up.at[:, at]),
            (hidden_grad.at[:, at], v_back.at[:, at]),
            (gate_out.at[:, at], v_gate_out.at[:, at]),
            (up_out.at[:, at], v_up_out.at[:, at]),
            (down_in.at[:, at], v_down_in.at[:, at]),
        ]
        if step < model_steps:
            pairs += [
                (inputs.at[:, at], v_inputs.at[:, at]),
                (gate_in.at[:, at], v_in.at[pl.ds(0, width), at]),
                (up_in.at[:, at], v_in.at[pl.ds(width, width), at]),
                (out_grad.at[:, at], v_out_grad.at[:, at]),
                (down_out.at[:, at], v_down_out.at[:, at]),
            ]
        plan(pairs)

    def elementwise(step, target):
        for top in range(0, tokens, ROWS):
            for part in range(0, STEP, 256):
                at = (slice(top, top + ROWS), slice(step * STEP + part, step * STEP + part + 256))
                put = (slice(top, top + ROWS), slice(part, part + 256))
                gate = v_gate[at].astype(jnp.float32)
                up = v_up[at].astype(jnp.float32)
                back = v_back[at].astype(jnp.float32)
                sig = 0.5 * jnp.tanh(0.5 * gate) + 0.5
                silu = gate * sig
                made[(target, 0) + put] = (silu * up).astype(jnp.bfloat16)
                made[(target, 1) + put] = (back * silu).astype(jnp.bfloat16)
                slope = sig + silu * (1.0 - sig)
                made[(target, 2) + put] = (back * up * slope).astype(jnp.bfloat16)

    def dot(base, values):
        return lax.dot_general(base, values, NT, preferred_element_type=jnp.float32)

    def add(at, value, first):
        if first:
            out[at] = value
        else:
            out[at] += value

    def hidden_dots(step, target):
        at = slice(step * STEP, (step + 1) * STEP)
        add(slice(2 * width, 3 * width), dot(v_gate_out[:, at], made[target, 2]), step == 0)
        add(slice(3 * width, 4 * width), dot(v_up_out[:, at], made[target, 1]), step == 0)
        add(slice(4 * width, 5 * width), dot(v_down_in[:, at], made[target, 0]), step == 0)

    def model_dots(step):
        at = slice(step * STEP, (step + 1) * STEP)
        add(slice(0, 2 * width), dot(v_in[:, at], v_inputs[:, at]), step == 0)
        add(slice(5 * width, 6 * width), dot(v_down_out[:, at], v_out_grad[:, at]), step == 0)

    for step in range(min(AHEAD, hidden_steps)):
        for copy in copies[step]:
            copy.start()
    for step in range(hidden_steps):
        if step + AHEAD < hidden_steps:
            for copy in copies[step + AHEAD]:
                copy.start()
        for copy in copies[step]:
            copy.wait()
        elementwise(step, step % 2)
        if step >= 1:
            hidden_dots(step - 1, (step - 1) % 2)
        if step < model_steps:
            model_dots(step)
    hidden_dots(hidden_steps - 1, (hidden_steps - 1) % 2)


def projections(*operands):
    inputs, gate_pre = operands[:2]
    width = operands[5].shape[0]
    tokens, model = inputs.shape
    hidden = gate_pre.shape[1]
    assert hidden % STEP == 0 and model % STEP == 0 and model <= hidden
    assert tokens % ROWS == 0
    steps = 6 * (hidden // STEP) + 5 * (model // STEP)
    bf16 = jnp.bfloat16
    return pl.pallas_call(
        project,
        out_shape=jax.ShapeDtypeStruct((6 * width, tokens), jnp.float32),
        in_specs=[pl.BlockSpec(memory_space=pltpu.HBM)] * len(operands),
        out_specs=pl.BlockSpec(memory_space=pltpu.VMEM),
        scratch_shapes=[
            pltpu.VMEM((tokens, model), bf16),
            pltpu.VMEM((tokens, hidden), bf16),
            pltpu.VMEM((tokens, hidden), bf16),
            pltpu.VMEM((tokens, hidden), bf16),
            pltpu.VMEM((tokens, model), bf16),
            pltpu.VMEM((2 * width, model), bf16),
            pltpu.VMEM((width, hidden), bf16),
            pltpu.VMEM((width, hidden), bf16),
            pltpu.VMEM((width, hidden), bf16),
            pltpu.VMEM((width, model), bf16),
            pltpu.VMEM((2, 3, tokens, STEP), bf16),
            pltpu.SemaphoreType.DMA((steps,)),
        ],
        compiler_params=pltpu.CompilerParams(vmem_limit_bytes=40 * 2**20),
        cost_estimate=pl.CostEstimate(
            flops=6 * tokens * width * (model + hidden),
            bytes_accessed=2 * (2 * tokens * model + 3 * tokens * hidden),
            transcendentals=tokens * hidden,
        ),
        name="project",
    )(*operands)


def outer(chips, own, other, ids, *refs):
    outs, (summed, products, blocks) = refs[:chips], refs[chips:]
    chip, core = lax.axis_index("dp"), lax.axis_index("mp")
    width = own.shape[0] // 6
    half = width // 2
    span = 3 * half // chips
    summed[...] = own[...] + other[...]
    own_label = 2 * chip + core
    tail_label = jnp.where(core == 1, 2 * chip - 1, -1)
    masks = [(ids[...] == label).astype(jnp.float32) for label in (tail_label, own_label)]
    lane = lax.broadcasted_iota(jnp.int32, (half, 2 * width), 1)
    for module, (left, right) in enumerate(((0, 2), (1, 3), (4, 5))):
        factor = summed[left * width : (left + 1) * width, :]
        other_factor = summed[right * width : (right + 1) * width, :]
        products[module] = lax.dot_general(
            jnp.concatenate([factor * mask for mask in masks], axis=0),
            jnp.concatenate([other_factor, other_factor], axis=0),
            NT,
            precision=HIGHEST,
            preferred_element_type=jnp.float32,
        )
        for label in range(2):
            even = products[module, pl.ds(label * width, half, stride=2), :]
            odd = products[module, pl.ds(label * width + 1, half, stride=2), :]
            packed = jnp.where(lane < width, even, odd)
            row = 0
            while row < half:
                chip_to, inside = divmod(module * half + row, span)
                count = min(span - inside, half - row)
                put = slice(label * span + inside, label * span + inside + count)
                blocks[chip_to, put, :] = packed[row : row + count]
                row += count
    for flip in range(chips):
        outs[flip][...] = blocks[chip ^ flip]


def example_blocks(chips, own, other, ids):
    width = own.shape[0] // 6
    block = (3 * width // chips, 2 * width)
    return pl.pallas_call(
        functools.partial(outer, chips),
        out_shape=[jax.ShapeDtypeStruct(block, jnp.float32)] * chips,
        in_specs=[pl.BlockSpec(memory_space=pltpu.VMEM)] * 3,
        out_specs=[pl.BlockSpec(memory_space=pltpu.VMEM)] * chips,
        scratch_shapes=[
            pltpu.VMEM(own.shape, jnp.float32),
            pltpu.VMEM((3, 2 * width, 2 * width), jnp.float32),
            pltpu.VMEM((chips,) + block, jnp.float32),
        ],
        name="outer",
    )(own, other, ids)


def score(chips, queries, swapped, *refs):
    received, outs, (rows, result) = refs[:chips], refs[chips : 2 * chips], refs[2 * chips :]
    chip, core = lax.axis_index("dp"), lax.axis_index("mp")
    height, lanes = received[0].shape
    span = height // 2
    for flip in range(chips):
        rows[pl.ds(pl.multiple_of((chip ^ flip) * height, height), height), :] = received[flip][...]
    rows[chips * height :, :] = jnp.zeros((height, lanes), jnp.float32)
    grads = []
    for at in range(span):
        own = rows[pl.ds(span + at, chips, stride=height), :]
        tail = rows[pl.ds(height + at, chips, stride=height), :]
        grads.append(own + tail)
    grads = jnp.concatenate(grads, axis=1)
    high = grads.astype(jnp.bfloat16)
    rest = grads - high.astype(jnp.float32)
    middle = rest.astype(jnp.bfloat16)
    low = (rest - middle.astype(jnp.float32)).astype(jnp.bfloat16)
    terms = jnp.concatenate([high, middle, low], axis=0)
    coords = queries.shape[1]
    halves = (terms[:, :coords], terms[:, coords:])
    first = core == 0
    mine = jnp.where(first, halves[0], halves[1])
    theirs = jnp.where(first, halves[1], halves[0])
    scores = lax.dot_general(mine, queries[...], NT, preferred_element_type=jnp.float32)
    scores += lax.dot_general(theirs, swapped[...], NT, preferred_element_type=jnp.float32)
    result[:, 0, :] = scores[:chips] + scores[chips : 2 * chips] + scores[2 * chips :]
    for flip in range(chips):
        outs[flip][...] = result[chip ^ flip]


def partial_scores(chips, queries, swapped, received):
    height, lanes = received[0].shape
    total = queries.shape[0]
    return pl.pallas_call(
        functools.partial(score, chips),
        out_shape=[jax.ShapeDtypeStruct((1, total), jnp.float32)] * chips,
        in_specs=[pl.BlockSpec(memory_space=pltpu.VMEM)] * (2 + chips),
        out_specs=[pl.BlockSpec(memory_space=pltpu.VMEM)] * chips,
        scratch_shapes=[
            pltpu.VMEM(((chips + 1) * height, lanes), jnp.float32),
            pltpu.VMEM((chips, 1, total), jnp.float32),
        ],
        name="score",
    )(queries, swapped, *received)


def exchanged(blocks):
    chips = len(blocks)
    moved = {0: blocks[0]}
    for flip in reversed(range(1, chips)):
        moved[flip] = lax.ppermute(blocks[flip], "dp", [(i, i ^ flip) for i in range(chips)])
    return [moved[flip] for flip in range(chips)]


def body(
    inputs,
    gate_pre,
    up_pre,
    hidden_grad,
    out_grad,
    example_ids,
    gate_in,
    gate_out,
    up_in,
    up_out,
    down_in,
    down_out,
    queries,
):
    chips = lax.axis_size("dp")
    swap = [(0, 1), (1, 0)]
    swapped = lax.ppermute(queries, "mp", swap)
    bases = [base.T for base in (gate_in, gate_out, up_in, up_out, down_in, down_out)]
    own = projections(inputs, gate_pre, up_pre, hidden_grad, out_grad, *bases)
    other = lax.ppermute(own, "mp", swap)
    blocks = exchanged(example_blocks(chips, own, other, example_ids.reshape(1, -1)))
    pieces = exchanged(partial_scores(chips, queries, swapped, blocks))
    return functools.reduce(jnp.add, pieces)


def solution(mesh):
    placed = (
        P(("parts", "dp"), "mp"),
        P(("parts", "dp"), "mp"),
        P(("parts", "dp"), "mp"),
        P(("parts", "dp"), "mp"),
        P(("parts", "dp"), "mp"),
        P(("parts", "dp")),
        P("mp", None),
        P("mp", None),
        P("mp", None),
        P("mp", None),
        P("mp", None),
        P("mp", None),
        P(None, ("dp", "mp")),
    )
    return jax.shard_map(
        body, mesh=mesh, in_specs=placed, out_specs=P(("parts", "dp", "mp"), None), check_vma=False
    )
```

time: 43.1 us -> 65.4 us (1.52)
  blocking collectives: 23.7 us -> 0 us
  starting transfers between devices: 0.52 us -> 24.1 us
  Pallas kernels: 0 us -> 14.7 us
  matrix products: 14 us -> 0 us
  local copies, waits for them, and re-layouts: 2.51 us -> 14.6 us
  waiting for transfers between devices: 0.92 us -> 10 us
    all_to_all x2 -> x0, blocking collectives: 23.7 us -> none  [the longest x1 14.5 us: body(): lax.all_to_all(partial_value, ('dp', 'mp'), split_axis=1, concat_axis=0,...]
    ppermute x1 -> x16, starting transfers between devices: 0.52 us -> 24.1 us  [the longest x14 23.6 us: exchanged(): lax.ppermute(blocks[flip], 'dp', [(i, i ^ flip) for i in range(chips)])]
    pallas_call x0 -> x3, Pallas kernels: none -> 14.7 us  [the longest x1 9.7 us: projections(): pl.pallas_call(project, out_shape=jax.ShapeDtypeStruct((6 * width, tokens...]
    dot_general x10 -> x0, matrix products: 14 us -> none  [the longest x1 6.31 us: body(): jnp.dot(gate_grad, gate_out, preferred_element_type=jnp.float32)]
    unnamed x24 -> x40, local copies, waits for them, and re-layouts: 1.72 us -> 14.6 us
    ppermute x1 -> x16, waiting for transfers between devices: 0.92 us -> 10 us  [the longest x14 8.38 us: exchanged(): lax.ppermute(blocks[flip], 'dp', [(i, i ^ flip) for i in range(chips)])]
    add x3 -> x1, other arithmetic: 0.18 us -> 1.27 us  [body(): return functools.reduce(jnp.add, pieces)]
  transfers between devices with their start and end apart: 1 -> 16, of which waited for: 1 -> 6; matrix products, arithmetic and copies ran while one was open for 0% -> 0% of each run, Pallas kernels for 0% -> 19%
where the time goes in v3:
time: 65.4 us; the launch traced here: 64.9 us
  starting transfers between devices  24.1 us (37%)
  Pallas kernels  14.7 us (22%)
  local copies, waits for them, and re-layouts  14.6 us (22%)
  waiting for transfers between devices  10 us (15%)
  other arithmetic  1.27 us (2%)
    ppermute x14, starting transfers between devices, exchanged(): lax.ppermute(blocks[flip], 'dp', [(i, i ^ flip) for i in range(chips)])  23.6 us
    unnamed x40, local copies, waits for them, and re-layouts  14.6 us
    pallas_call x1, Pallas kernels, projections(): pl.pallas_call(project, out_shape=jax.ShapeDtypeStruct((6 * width, tokens...  9.7 us
    ppermute x14, waiting for transfers between devices, exchanged(): lax.ppermute(blocks[flip], 'dp', [(i, i ^ flip) for i in range(chips)])  8.38 us
    pallas_call x1, Pallas kernels, partial_scores(): pl.pallas_call(functools.partial(score, chips), out_shape=[jax.ShapeDtype...  2.66 us
    pallas_call x1, Pallas kernels, example_blocks(): pl.pallas_call(functools.partial(outer, chips), out_shape=[jax.ShapeDtype...  2.31 us
    ppermute x1, waiting for transfers between devices, body(): other = lax.ppermute(own, 'mp', swap)  1.66 us
  transfers between devices with their start and end apart: 16, of which 6 were waited for; matrix products, arithmetic and copies ran while one was open for 0% of the time, Pallas kernels for 19%

profile of v3, /device:TPU:0, one launch (start us, length us, event | category | flops | bytes accessed | tf_op | source)
XLA Modules:
  0.0 64.9 jit_solution(8365038265808685009)
XLA Ops:
  0.0 0.5 collective-permute-start
  0.5 1.8 %copy-done = bf16[192,7168]{1,0:T(8,128)(2,1)S(1)} copy-done((bf16[192,7168]{1,0:T(8,128)(2,1)S(1)}, bf16[192,7168]{1,0:T(8,128)(2,1)}, u32[]{:S(2)}) %copy-start) | copy-done | bytes 2752536
  2.2 1.8 %copy-done.1 = bf16[192,7168]{1,0:T(8,128)(2,1)S(1)} copy-done((bf16[192,7168]{1,0:T(8,128)(2,1)S(1)}, bf16[192,7168]{1,0:T(8,128)(2,1)}, u32[]{:S(2)}) %copy-start.1) | copy-done | bytes 2752536
  4.0 1.4 %copy-done.3 = bf16[192,4096]{1,0:T(8,128)(2,1)S(1)} copy-done((bf16[192,4096]{1,0:T(8,128)(2,1)S(1)}, bf16[192,4096]{1,0:T(8,128)(2,1)}, u32[]{:S(2)}) %copy-start.3) | copy-done | bytes 1572888
  5.4 1.4 %copy-done.4 = bf16[192,4096]{1,0:T(8,128)(2,1)S(1)} copy-done((bf16[192,4096]{1,0:T(8,128)(2,1)S(1)}, bf16[192,4096]{1,0:T(8,128)(2,1)}, u32[]{:S(2)}) %copy-start.4) | copy-done | bytes 1572888
  6.8 1.2 %copy-done.5 = bf16[7168,64]{0,1:T(8,128)(2,1)S(1)} copy-done((bf16[7168,64]{0,1:T(8,128)(2,1)S(1)}, bf16[7168,64]{0,1:T(8,128)(2,1)}, u32[]{:S(2)}) %copy-start.5) | copy-done | bytes 917528
  8.0 1.2 %copy-done.6 = bf16[7168,64]{0,1:T(8,128)(2,1)S(1)} copy-done((bf16[7168,64]{0,1:T(8,128)(2,1)S(1)}, bf16[7168,64]{0,1:T(8,128)(2,1)}, u32[]{:S(2)}) %copy-start.6) | copy-done | bytes 917528
  9.2 1.2 %copy-done.7 = bf16[7168,64]{0,1:T(8,128)(2,1)S(1)} copy-done((bf16[7168,64]{0,1:T(8,128)(2,1)S(1)}, bf16[7168,64]{0,1:T(8,128)(2,1)}, u32[]{:S(2)}) %copy-start.7) | copy-done | bytes 917528
  10.4 1.0 %copy-done.8 = bf16[4096,64]{0,1:T(8,128)(2,1)S(1)} copy-done((bf16[4096,64]{0,1:T(8,128)(2,1)S(1)}, bf16[4096,64]{0,1:T(8,128)(2,1)}, u32[]{:S(2)}) %copy-start.8) | copy-done | bytes 524312
  11.4 1.0 %copy-done.9 = bf16[4096,64]{0,1:T(8,128)(2,1)S(1)} copy-done((bf16[4096,64]{0,1:T(8,128)(2,1)S(1)}, bf16[4096,64]{0,1:T(8,128)(2,1)}, u32[]{:S(2)}) %copy-start.9) | copy-done | bytes 524312
  12.5 1.0 %copy-done.10 = bf16[4096,64]{0,1:T(8,128)(2,1)S(1)} copy-done((bf16[4096,64]{0,1:T(8,128)(2,1)S(1)}, bf16[4096,64]{0,1:T(8,128)(2,1)}, u32[]{:S(2)}) %copy-start.10) | copy-done | bytes 524312
  13.5 9.7 %project.1.own = f32[384,192]{1,0:T(8,128)S(1)} custom-call(bf16[192,4096]{1,0:T(8,128)(2,1)S(1)} %copy-done.3, bf16[192,7168]{1,0:T(8,128)(2,1)S(1)} %copy-done, bf16[192,7168]{1,0:T(8,128)(2,1)S(1)} %copy-done.1, bf16[192,7168]{1,0:T(8,128)(2,1)} %hidden_grad.1, bf16[192,4096]{1,0:T(8,128)(2,1)S(1)} %copy-done.4, bf16[64,4096]{1,0:T(8,128)(2,1)S(1)} %bitcast.10, ...), custom_call_target="tpu_custom_call" | custom-call | flops 830472192 | bytes 11403264 | tf_op jit(solution)/shard_map/project/pallas_call | solution.py:137
  23.2 0.1 collective-permute-start.1
  23.3 1.7 %collective-permute-done.1.other = f32[384,192]{1,0:T(8,128)S(1)} collective-permute-done((f32[384,192]{1,0:T(8,128)S(1)}, f32[384,192]{1,0:T(8,128)S(1)}, u32[]{:S(2)}, u32[]{:S(2)}) %collective-permute-start.1) | collective-permute-done | bytes 294944 | tf_op jit(solution)/shard_map/ppermute | solution.py:294
  25.0 0.7 %copy-done.12 = f32[384,192]{1,0:T(8,128)} copy-done((f32[384,192]{1,0:T(8,128)}, f32[384,192]{1,0:T(8,128)S(1)}, u32[]{:S(2)}) %copy-start.12) | copy-done | bytes 294936
  25.7 2.3 %outer.1 = (f32[24,128]{1,0:T(8,128)}, f32[24,128]{1,0:T(8,128)}, f32[24,128]{1,0:T(8,128)}, f32[24,128]{1,0:T(8,128)}, f32[24,128]{1,0:T(8,128)}, /*index=5*/f3...) custom-call(f32[384,192]{1,0:T(8,128)} %copy-done.2, f32[384,192]{1,0:T(8,128)} %copy-done.12, s32[1,192]{1,0:T(1,128)} %bitcast.13), custom_call_target="tpu_custom_call" | custom-call | tf_op jit(solution)/shard_map/outer/pallas_call | solution.py:205
  28.1 2.7 %collective-permute-start.2 = (f32[24,128]{1,0:T(8,128)}, f32[24,128]{1,0:T(8,128)S(1)}, u32[]{:S(2)}, u32[]{:S(2)}) collective-permute-start(f32[24,128]{1,0:T(8,128)} %get-tuple-element.22), channel_id=1, source_target_pairs={{0,2},{2,0},{4,6},{6,4},{8,10},{10,8},{12,14},{14,12},{1,3},{3,1},... | collective-permute-start | bytes 36872 | tf_op jit(solution)/shard_map/ppermute | solution.py:270
  30.7 1.6 %collective-permute-start.3 = (f32[24,128]{1,0:T(8,128)}, f32[24,128]{1,0:T(8,128)S(1)}, u32[]{:S(2)}, u32[]{:S(2)}) collective-permute-start(f32[24,128]{1,0:T(8,128)} %get-tuple-element.23), channel_id=1, source_target_pairs={{0,4},{2,6},{4,0},{6,2},{8,12},{10,14},{12,8},{14,10},{1,5},{3,7},... | collective-permute-start | bytes 36872 | tf_op jit(solution)/shard_map/ppermute | solution.py:270
  32.3 0.0 collective-permute-start.4
  32.3 3.0 %collective-permute-start.5 = (f32[24,128]{1,0:T(8,128)}, f32[24,128]{1,0:T(8,128)S(1)}, u32[]{:S(2)}, u32[]{:S(2)}) collective-permute-start(f32[24,128]{1,0:T(8,128)} %get-tuple-element.25), channel_id=1, source_target_pairs={{0,8},{2,10},{4,12},{6,14},{8,0},{10,2},{12,4},{14,6},{1,9},{3,11}... | collective-permute-start | bytes 36872 | tf_op jit(solution)/shard_map/ppermute | solution.py:270
  35.3 0.0 collective-permute-done.2.refs_1_
  35.3 1.4 %collective-permute-start.6 = (f32[24,128]{1,0:T(8,128)}, f32[24,128]{1,0:T(8,128)S(1)}, u32[]{:S(2)}, u32[]{:S(2)}) collective-permute-start(f32[24,128]{1,0:T(8,128)} %get-tuple-element.26), channel_id=1, source_target_pairs={{0,10},{2,8},{4,14},{6,12},{8,2},{10,0},{12,6},{14,4},{1,11},{3,9}... | collective-permute-start | bytes 36872 | tf_op jit(solution)/shard_map/ppermute | solution.py:270
  36.7 0.0 collective-permute-done.3.refs_2_
  36.7 3.5 %collective-permute-start.7 = (f32[24,128]{1,0:T(8,128)}, f32[24,128]{1,0:T(8,128)S(1)}, u32[]{:S(2)}, u32[]{:S(2)}) collective-permute-start(f32[24,128]{1,0:T(8,128)} %get-tuple-element.27), channel_id=1, source_target_pairs={{0,12},{2,14},{4,8},{6,10},{8,4},{10,6},{12,0},{14,2},{1,13},{3,15... | collective-permute-start | bytes 36872 | tf_op jit(solution)/shard_map/ppermute | solution.py:270
  40.2 0.0 collective-permute-done.4.refs_3_
  40.2 0.2 collective-permute-start.8
  40.4 0.0 collective-permute-done.5.refs_4_
  40.4 0.6 collective-permute-done.6.refs_5_
  41.0 1.4 %collective-permute-done.7.refs_6_ = f32[24,128]{1,0:T(8,128)S(1)} collective-permute-done((f32[24,128]{1,0:T(8,128)}, f32[24,128]{1,0:T(8,128)S(1)}, u32[]{:S(2)}, u32[]{:S(2)}) %collective-permute-start.7) | collective-permute-done | bytes 12320 | tf_op jit(solution)/shard_map/ppermute | solution.py:270
  42.4 4.4 %collective-permute-done.8.refs_7_ = f32[24,128]{1,0:T(8,128)S(1)} collective-permute-done((f32[24,128]{1,0:T(8,128)}, f32[24,128]{1,0:T(8,128)S(1)}, u32[]{:S(2)}, u32[]{:S(2)}) %collective-permute-start.8) | collective-permute-done | bytes 12320 | tf_op jit(solution)/shard_map/ppermute | solution.py:270
  46.8 0.0 collective-permute-done.swapped
  46.9 0.5 copy-done.19
  47.4 0.3 copy-done.11
  47.7 2.7 %score.1 = (f32[1,512]{1,0:T(1,128)}, f32[1,512]{1,0:T(1,128)}, f32[1,512]{1,0:T(1,128)}, f32[1,512]{1,0:T(1,128)}, f32[1,512]{1,0:T(1,128)}, /*index=5*/f32[1,5...) custom-call(bf16[512,768]{1,0:T(8,128)(2,1)} %queries.1, bf16[512,768]{1,0:T(8,128)(2,1)} %copy-done.11, ...), custom_call_target="tpu_custom_call" | custom-call | tf_op jit(solution)/shard_map/score/pallas_call | solution.py:253
  50.4 0.6 collective-permute-start.9
  50.9 0.0 collective-permute-start.10
  50.9 3.0 %collective-permute-start.11 = (f32[1,512]{1,0:T(1,128)}, f32[1,512]{1,0:T(1,128)S(1)}, u32[]{:S(2)}, u32[]{:S(2)}) collective-permute-start(f32[1,512]{1,0:T(1,128)} %get-tuple-element.32), channel_id=1, source_target_pairs={{0,6},{2,4},{4,2},{6,0},{8,14},{10,12},{12,10},{14,8},{1,7},{3,5},... | collective-permute-start | bytes 6152 | tf_op jit(solution)/shard_map/ppermute | solution.py:270
  53.9 0.0 collective-permute-start.12
  53.9 2.9 %collective-permute-start.13 = (f32[1,512]{1,0:T(1,128)}, f32[1,512]{1,0:T(1,128)S(1)}, u32[]{:S(2)}, u32[]{:S(2)}) collective-permute-start(f32[1,512]{1,0:T(1,128)} %get-tuple-element.34), channel_id=1, source_target_pairs={{0,10},{2,8},{4,14},{6,12},{8,2},{10,0},{12,6},{14,4},{1,11},{3,9}... | collective-permute-start | bytes 6152 | tf_op jit(solution)/shard_map/ppermute | solution.py:270
  56.8 0.0 collective-permute-done.9
  56.8 0.3 collective-permute-start.14
  57.1 4.5 %collective-permute-start.15 = (f32[1,512]{1,0:T(1,128)}, f32[1,512]{1,0:T(1,128)S(1)}, u32[]{:S(2)}, u32[]{:S(2)}) collective-permute-start(f32[1,512]{1,0:T(1,128)} %get-tuple-element.36), channel_id=1, source_target_pairs={{0,14},{2,12},{4,10},{6,8},{8,6},{10,4},{12,2},{14,0},{1,15},{3,13... | collective-permute-start | bytes 6152 | tf_op jit(solution)/shard_map/ppermute | solution.py:270
  61.6 0.0 collective-permute-done.11
  61.6 0.0 collective-permute-done.12
  61.6 0.0 collective-permute-done.13
  61.6 0.8 %collective-permute-done.14 = f32[1,512]{1,0:T(1,128)S(1)} collective-permute-done((f32[1,512]{1,0:T(1,128)}, f32[1,512]{1,0:T(1,128)S(1)}, u32[]{:S(2)}, u32[]{:S(2)}) %collective-permute-start.14) | collective-permute-done | bytes 2080 | tf_op jit(solution)/shard_map/ppermute | solution.py:270
  62.4 1.2 %collective-permute-done.15 = f32[1,512]{1,0:T(1,128)S(1)} collective-permute-done((f32[1,512]{1,0:T(1,128)}, f32[1,512]{1,0:T(1,128)S(1)}, u32[]{:S(2)}, u32[]{:S(2)}) %collective-permute-start.15) | collective-permute-done | bytes 2080 | tf_op jit(solution)/shard_map/ppermute | solution.py:270
  63.6 1.3 %add_add_fusion = f32[1,512]{1,0:T(1,128)} fusion(f32[1,512]{1,0:T(1,128)S(1)} %collective-permute-done.15, f32[1,512]{1,0:T(1,128)S(1)} %collective-permute-done.14, f32[1,512]{1,0:T(1,128)S(1)} %collective-permute-done.13, f32[1,512]{1,0:T(1,128)S(1)} %collective-permute-done.12, f32[1,512]{1,0:T(1,128)S(1)} %collective-permute-done.11, ...), kind=kLoop, calls=%fused_computation | loop fusion | flops 3584 | bytes 18432 | tf_op jit(solution)/shard_map/add | solution.py:297
  (28 shorter events, 0.0 us)
Async XLA Ops:
  0.0 46.8 %collective-permute-start = (bf16[512,768]{1,0:T(8,128)(2,1)}, bf16[512,768]{1,0:T(8,128)(2,1)S(1)}, u32[]{:S(2)}, u32[]{:S(2)}) collective-permute-start(bf16[512,768]{1,0:T(8,128)(2,1)} %queries.1), channel_id=1, source_target_pairs={{0,1},{1,0},{2,3},{3,2},{4,5},{5,4},{6,7},{7,6},{8,9},{9,8},{10,11... | collective-permute-start | bytes 2359304 | tf_op jit(solution)/shard_map/ppermute | solution.py:291
  0.5 1.8 %copy-start = (bf16[192,7168]{1,0:T(8,128)(2,1)S(1)}, bf16[192,7168]{1,0:T(8,128)(2,1)}, u32[]{:S(2)}) copy-start(bf16[192,7168]{1,0:T(8,128)(2,1)} %gate_pre.1) | copy-start | bytes 8257540
  2.2 1.8 %copy-start.1 = (bf16[192,7168]{1,0:T(8,128)(2,1)S(1)}, bf16[192,7168]{1,0:T(8,128)(2,1)}, u32[]{:S(2)}) copy-start(bf16[192,7168]{1,0:T(8,128)(2,1)} %up_pre.1) | copy-start | bytes 8257540
  4.0 1.4 %copy-start.3 = (bf16[192,4096]{1,0:T(8,128)(2,1)S(1)}, bf16[192,4096]{1,0:T(8,128)(2,1)}, u32[]{:S(2)}) copy-start(bf16[192,4096]{1,0:T(8,128)(2,1)} %inputs.1) | copy-start | bytes 4718596
  5.4 1.4 %copy-start.4 = (bf16[192,4096]{1,0:T(8,128)(2,1)S(1)}, bf16[192,4096]{1,0:T(8,128)(2,1)}, u32[]{:S(2)}) copy-start(bf16[192,4096]{1,0:T(8,128)(2,1)} %out_grad.1) | copy-start | bytes 4718596
  6.8 1.2 %copy-start.5 = (bf16[7168,64]{0,1:T(8,128)(2,1)S(1)}, bf16[7168,64]{0,1:T(8,128)(2,1)}, u32[]{:S(2)}) copy-start(bf16[7168,64]{0,1:T(8,128)(2,1)} %param.20) | copy-start | bytes 2752516
  8.0 1.2 %copy-start.6 = (bf16[7168,64]{0,1:T(8,128)(2,1)S(1)}, bf16[7168,64]{0,1:T(8,128)(2,1)}, u32[]{:S(2)}) copy-start(bf16[7168,64]{0,1:T(8,128)(2,1)} %param.22) | copy-start | bytes 2752516
  9.2 1.2 %copy-start.7 = (bf16[7168,64]{0,1:T(8,128)(2,1)S(1)}, bf16[7168,64]{0,1:T(8,128)(2,1)}, u32[]{:S(2)}) copy-start(bf16[7168,64]{0,1:T(8,128)(2,1)} %param.23) | copy-start | bytes 2752516
  10.4 1.0 %copy-start.8 = (bf16[4096,64]{0,1:T(8,128)(2,1)S(1)}, bf16[4096,64]{0,1:T(8,128)(2,1)}, u32[]{:S(2)}) copy-start(bf16[4096,64]{0,1:T(8,128)(2,1)} %param.19) | copy-start | bytes 1572868
  11.4 1.0 %copy-start.9 = (bf16[4096,64]{0,1:T(8,128)(2,1)S(1)}, bf16[4096,64]{0,1:T(8,128)(2,1)}, u32[]{:S(2)}) copy-start(bf16[4096,64]{0,1:T(8,128)(2,1)} %param.21) | copy-start | bytes 1572868
  12.4 1.0 %copy-start.10 = (bf16[4096,64]{0,1:T(8,128)(2,1)S(1)}, bf16[4096,64]{0,1:T(8,128)(2,1)}, u32[]{:S(2)}) copy-start(bf16[4096,64]{0,1:T(8,128)(2,1)} %param.24) | copy-start | bytes 1572868
  23.2 1.8 %copy-start.2 = (f32[384,192]{1,0:T(8,128)}, f32[384,192]{1,0:T(8,128)S(1)}, u32[]{:S(2)}) copy-start(f32[384,192]{1,0:T(8,128)S(1)} %project.1.own) | copy-start | bytes 884740
  23.2 1.8 %collective-permute-start.1 = (f32[384,192]{1,0:T(8,128)S(1)}, f32[384,192]{1,0:T(8,128)S(1)}, u32[]{:S(2)}, u32[]{:S(2)}) collective-permute-start(f32[384,192]{1,0:T(8,128)S(1)} %project.1.own), channel_id=1, source_target_pairs={{0,1},{1,0},{2,3},{3,2},{4,5},{5,4},{6,7},{7,6},{8,9},{9,8},{10,11... | collective-permute-start | bytes 884744 | tf_op jit(solution)/shard_map/ppermute | solution.py:294
  25.0 0.7 %copy-start.12 = (f32[384,192]{1,0:T(8,128)}, f32[384,192]{1,0:T(8,128)S(1)}, u32[]{:S(2)}) copy-start(f32[384,192]{1,0:T(8,128)S(1)} %collective-permute-done.1.other) | copy-start | bytes 884740
  28.1 7.2 %collective-permute-start.2 = (f32[24,128]{1,0:T(8,128)}, f32[24,128]{1,0:T(8,128)S(1)}, u32[]{:S(2)}, u32[]{:S(2)}) collective-permute-start(f32[24,128]{1,0:T(8,128)} %get-tuple-element.22), channel_id=1, source_target_pairs={{0,2},{2,0},{4,6},{6,4},{8,10},{10,8},{12,14},{14,12},{1,3},{3,1},... | collective-permute-start | bytes 36872 | tf_op jit(solution)/shard_map/ppermute | solution.py:270
  30.7 5.9 %collective-permute-start.3 = (f32[24,128]{1,0:T(8,128)}, f32[24,128]{1,0:T(8,128)S(1)}, u32[]{:S(2)}, u32[]{:S(2)}) collective-permute-start(f32[24,128]{1,0:T(8,128)} %get-tuple-element.23), channel_id=1, source_target_pairs={{0,4},{2,6},{4,0},{6,2},{8,12},{10,14},{12,8},{14,10},{1,5},{3,7},... | collective-permute-start | bytes 36872 | tf_op jit(solution)/shard_map/ppermute | solution.py:270
  32.3 7.9 %collective-permute-start.4 = (f32[24,128]{1,0:T(8,128)}, f32[24,128]{1,0:T(8,128)S(1)}, u32[]{:S(2)}, u32[]{:S(2)}) collective-permute-start(f32[24,128]{1,0:T(8,128)} %get-tuple-element.24), channel_id=1, source_target_pairs={{0,6},{2,4},{4,2},{6,0},{8,14},{10,12},{12,10},{14,8},{1,7},{3,5},... | collective-permute-start | bytes 36872 | tf_op jit(solution)/shard_map/ppermute | solution.py:270
  32.3 8.1 %collective-permute-start.5 = (f32[24,128]{1,0:T(8,128)}, f32[24,128]{1,0:T(8,128)S(1)}, u32[]{:S(2)}, u32[]{:S(2)}) collective-permute-start(f32[24,128]{1,0:T(8,128)} %get-tuple-element.25), channel_id=1, source_target_pairs={{0,8},{2,10},{4,12},{6,14},{8,0},{10,2},{12,4},{14,6},{1,9},{3,11}... | collective-permute-start | bytes 36872 | tf_op jit(solution)/shard_map/ppermute | solution.py:270
  35.3 11.5 %copy-start.13 = (f32[24,128]{1,0:T(8,128)}, f32[24,128]{1,0:T(8,128)S(1)}, u32[]{:S(2)}) copy-start(f32[24,128]{1,0:T(8,128)S(1)} %collective-permute-done.2.refs_1_) | copy-start | bytes 36868
  35.3 5.7 %collective-permute-start.6 = (f32[24,128]{1,0:T(8,128)}, f32[24,128]{1,0:T(8,128)S(1)}, u32[]{:S(2)}, u32[]{:S(2)}) collective-permute-start(f32[24,128]{1,0:T(8,128)} %get-tuple-element.26), channel_id=1, source_target_pairs={{0,10},{2,8},{4,14},{6,12},{8,2},{10,0},{12,6},{14,4},{1,11},{3,9}... | collective-permute-start | bytes 36872 | tf_op jit(solution)/shard_map/ppermute | solution.py:270
  36.7 10.2 %copy-start.14 = (f32[24,128]{1,0:T(8,128)}, f32[24,128]{1,0:T(8,128)S(1)}, u32[]{:S(2)}) copy-start(f32[24,128]{1,0:T(8,128)S(1)} %collective-permute-done.3.refs_2_) | copy-start | bytes 36868
  36.7 5.7 %collective-permute-start.7 = (f32[24,128]{1,0:T(8,128)}, f32[24,128]{1,0:T(8,128)S(1)}, u32[]{:S(2)}, u32[]{:S(2)}) collective-permute-start(f32[24,128]{1,0:T(8,128)} %get-tuple-element.27), channel_id=1, source_target_pairs={{0,12},{2,14},{4,8},{6,10},{8,4},{10,6},{12,0},{14,2},{1,13},{3,15... | collective-permute-start | bytes 36872 | tf_op jit(solution)/shard_map/ppermute | solution.py:270
  40.2 6.6 %copy-start.15 = (f32[24,128]{1,0:T(8,128)}, f32[24,128]{1,0:T(8,128)S(1)}, u32[]{:S(2)}) copy-start(f32[24,128]{1,0:T(8,128)S(1)} %collective-permute-done.4.refs_3_) | copy-start | bytes 36868
  40.2 6.6 %collective-permute-start.8 = (f32[24,128]{1,0:T(8,128)}, f32[24,128]{1,0:T(8,128)S(1)}, u32[]{:S(2)}, u32[]{:S(2)}) collective-permute-start(f32[24,128]{1,0:T(8,128)} %get-tuple-element.28), channel_id=1, source_target_pairs={{0,14},{2,12},{4,10},{6,8},{8,6},{10,4},{12,2},{14,0},{1,15},{3,13... | collective-permute-start | bytes 36872 | tf_op jit(solution)/shard_map/ppermute | solution.py:270
  40.4 6.4 %copy-start.16 = (f32[24,128]{1,0:T(8,128)}, f32[24,128]{1,0:T(8,128)S(1)}, u32[]{:S(2)}) copy-start(f32[24,128]{1,0:T(8,128)S(1)} %collective-permute-done.5.refs_4_) | copy-start | bytes 36868
  41.0 5.8 %copy-start.17 = (f32[24,128]{1,0:T(8,128)}, f32[24,128]{1,0:T(8,128)S(1)}, u32[]{:S(2)}) copy-start(f32[24,128]{1,0:T(8,128)S(1)} %collective-permute-done.6.refs_5_) | copy-start | bytes 36868
  42.4 4.5 %copy-start.18 = (f32[24,128]{1,0:T(8,128)}, f32[24,128]{1,0:T(8,128)S(1)}, u32[]{:S(2)}) copy-start(f32[24,128]{1,0:T(8,128)S(1)} %collective-permute-done.7.refs_6_) | copy-start | bytes 36868
  46.8 0.6 copy-start.19
  46.8 0.9 %copy-start.11 = (bf16[512,768]{1,0:T(8,128)(2,1)}, bf16[512,768]{1,0:T(8,128)(2,1)S(1)}, u32[]{:S(2)}) copy-start(bf16[512,768]{1,0:T(8,128)(2,1)S(1)} %collective-permute-done.swapped) | copy-start | bytes 2359300
  50.4 6.4 %collective-permute-start.9 = (f32[1,512]{1,0:T(1,128)}, f32[1,512]{1,0:T(1,128)S(1)}, u32[]{:S(2)}, u32[]{:S(2)}) collective-permute-start(f32[1,512]{1,0:T(1,128)} %get-tuple-element.30), channel_id=1, source_target_pairs={{0,2},{2,0},{4,6},{6,4},{8,10},{10,8},{12,14},{14,12},{1,3},{3,1},... | collective-permute-start | bytes 6152 | tf_op jit(solution)/shard_map/ppermute | solution.py:270
  50.9 6.2 %collective-permute-start.10 = (f32[1,512]{1,0:T(1,128)}, f32[1,512]{1,0:T(1,128)S(1)}, u32[]{:S(2)}, u32[]{:S(2)}) collective-permute-start(f32[1,512]{1,0:T(1,128)} %get-tuple-element.31), channel_id=1, source_target_pairs={{0,4},{2,6},{4,0},{6,2},{8,12},{10,14},{12,8},{14,10},{1,5},{3,7},... | collective-permute-start | bytes 6152 | tf_op jit(solution)/shard_map/ppermute | solution.py:270
  50.9 10.6 %collective-permute-start.11 = (f32[1,512]{1,0:T(1,128)}, f32[1,512]{1,0:T(1,128)S(1)}, u32[]{:S(2)}, u32[]{:S(2)}) collective-permute-start(f32[1,512]{1,0:T(1,128)} %get-tuple-element.32), channel_id=1, source_target_pairs={{0,6},{2,4},{4,2},{6,0},{8,14},{10,12},{12,10},{14,8},{1,7},{3,5},... | collective-permute-start | bytes 6152 | tf_op jit(solution)/shard_map/ppermute | solution.py:270
  53.9 7.7 %collective-permute-start.12 = (f32[1,512]{1,0:T(1,128)}, f32[1,512]{1,0:T(1,128)S(1)}, u32[]{:S(2)}, u32[]{:S(2)}) collective-permute-start(f32[1,512]{1,0:T(1,128)} %get-tuple-element.33), channel_id=1, source_target_pairs={{0,8},{2,10},{4,12},{6,14},{8,0},{10,2},{12,4},{14,6},{1,9},{3,11}... | collective-permute-start | bytes 6152 | tf_op jit(solution)/shard_map/ppermute | solution.py:270
  53.9 7.7 %collective-permute-start.13 = (f32[1,512]{1,0:T(1,128)}, f32[1,512]{1,0:T(1,128)S(1)}, u32[]{:S(2)}, u32[]{:S(2)}) collective-permute-start(f32[1,512]{1,0:T(1,128)} %get-tuple-element.34), channel_id=1, source_target_pairs={{0,10},{2,8},{4,14},{6,12},{8,2},{10,0},{12,6},{14,4},{1,11},{3,9}... | collective-permute-start | bytes 6152 | tf_op jit(solution)/shard_map/ppermute | solution.py:270
  56.8 5.6 %collective-permute-start.14 = (f32[1,512]{1,0:T(1,128)}, f32[1,512]{1,0:T(1,128)S(1)}, u32[]{:S(2)}, u32[]{:S(2)}) collective-permute-start(f32[1,512]{1,0:T(1,128)} %get-tuple-element.35), channel_id=1, source_target_pairs={{0,12},{2,14},{4,8},{6,10},{8,4},{10,6},{12,0},{14,2},{1,13},{3,15... | collective-permute-start | bytes 6152 | tf_op jit(solution)/shard_map/ppermute | solution.py:270
  57.1 6.5 %collective-permute-start.15 = (f32[1,512]{1,0:T(1,128)}, f32[1,512]{1,0:T(1,128)S(1)}, u32[]{:S(2)}, u32[]{:S(2)}) collective-permute-start(f32[1,512]{1,0:T(1,128)} %get-tuple-element.36), channel_id=1, source_target_pairs={{0,14},{2,12},{4,10},{6,8},{8,6},{10,4},{12,2},{14,0},{1,15},{3,13... | collective-permute-start | bytes 6152 | tf_op jit(solution)/shard_map/ppermute | solution.py:270

commit v4 on v3

v4 whole, which is shorter than its diff:
```python
import functools

import jax
import jax.numpy as jnp
from jax import lax
from jax.experimental import pallas as pl
from jax.experimental.pallas import tpu as pltpu
from jax.sharding import PartitionSpec as P

NT = (((1,), (1,)), ((), ()))
STEP = 1024
PART = 512
ROWS = 16
AHEAD = 3


def project(
    inputs,
    gate_pre,
    up_pre,
    hidden_grad,
    out_grad,
    gate_in,
    gate_out,
    up_in,
    up_out,
    down_in,
    down_out,
    out,
    v_inputs,
    v_gate,
    v_up,
    v_back,
    v_out_grad,
    v_in,
    v_gate_out,
    v_up_out,
    v_down_in,
    v_down_out,
    made_hidden,
    made_up,
    made_gate,
    sems,
):
    width = gate_in.shape[0]
    tokens = inputs.shape[0]
    hidden_steps = gate_pre.shape[1] // STEP
    model_steps = inputs.shape[1] // STEP
    copies = []

    def plan(pairs):
        made_here = []
        for source, target in pairs:
            copy = pltpu.make_async_copy(source, target, sems.at[sum(map(len, copies)) + len(made_here)])
            made_here.append(copy)
        copies.append(made_here)

    for step in range(hidden_steps):
        at = pl.ds(step * STEP, STEP)
        pairs = [
            (gate_pre.at[:, at], v_gate.at[:, at]),
            (up_pre.at[:, at], v_up.at[:, at]),
            (hidden_grad.at[:, at], v_back.at[:, at]),
            (gate_out.at[:, at], v_gate_out.at[:, at]),
            (up_out.at[:, at], v_up_out.at[:, at]),
            (down_in.at[:, at], v_down_in.at[:, at]),
        ]
        if step < model_steps:
            pairs += [
                (inputs.at[:, at], v_inputs.at[:, at]),
                (gate_in.at[:, at], v_in.at[pl.ds(0, width), at]),
                (up_in.at[:, at], v_in.at[pl.ds(width, width), at]),
                (out_grad.at[:, at], v_out_grad.at[:, at]),
                (down_out.at[:, at], v_down_out.at[:, at]),
            ]
        plan(pairs)

    def elementwise(step, part):
        target = step % 2
        for top in range(0, tokens, ROWS):
            for left in range(part * PART, (part + 1) * PART, 256):
                at = (slice(top, top + ROWS), slice(step * STEP + left, step * STEP + left + 256))
                put = (slice(top, top + ROWS), slice(left, left + 256))
                gate = v_gate[at].astype(jnp.float32)
                up = v_up[at].astype(jnp.float32)
                back = v_back[at].astype(jnp.float32)
                sig = 0.5 * jnp.tanh(0.5 * gate) + 0.5
                silu = gate * sig
                made_hidden[(target,) + put] = (silu * up).astype(jnp.bfloat16)
                made_up[(target,) + put] = (back * silu).astype(jnp.bfloat16)
                slope = sig + silu * (1.0 - sig)
                made_gate[(target,) + put] = (back * up * slope).astype(jnp.bfloat16)

    def add(low, high, base, values, first):
        value = lax.dot_general(base, values, NT, preferred_element_type=jnp.float32)
        if first:
            out[low * width : high * width, :] = value
        else:
            out[low * width : high * width, :] += value

    def hidden_dots(step, part):
        at = slice(step * STEP + part * PART, step * STEP + (part + 1) * PART)
        inner = (step % 2, slice(None), slice(part * PART, (part + 1) * PART))
        first = step == 0 and part == 0
        add(2, 3, v_gate_out[:, at], made_gate[inner], first)
        add(3, 4, v_up_out[:, at], made_up[inner], first)
        add(4, 5, v_down_in[:, at], made_hidden[inner], first)

    def model_dots(step, part):
        at = slice(step * STEP + part * PART, step * STEP + (part + 1) * PART)
        first = step == 0 and part == 0
        add(0, 2, v_in[:, at], v_inputs[:, at], first)
        add(5, 6, v_down_out[:, at], v_out_grad[:, at], first)

    for step in range(min(AHEAD, hidden_steps)):
        for copy in copies[step]:
            copy.start()
    for step in range(hidden_steps):
        if step + AHEAD < hidden_steps:
            for copy in copies[step + AHEAD]:
                copy.start()
        for copy in copies[step]:
            copy.wait()
        for part in range(STEP // PART):
            elementwise(step, part)
            if step >= 1:
                hidden_dots(step - 1, part)
            if step < model_steps:
                model_dots(step, part)
    for part in range(STEP // PART):
        hidden_dots(hidden_steps - 1, part)


def projections(*operands):
    inputs, gate_pre = operands[:2]
    width = operands[5].shape[0]
    tokens, model = inputs.shape
    hidden = gate_pre.shape[1]
    assert hidden % STEP == 0 and model % STEP == 0 and model <= hidden
    assert tokens % ROWS == 0
    steps = 6 * (hidden // STEP) + 5 * (model // STEP)
    bf16 = jnp.bfloat16
    return pl.pallas_call(
        project,
        out_shape=jax.ShapeDtypeStruct((6 * width, tokens), jnp.float32),
        in_specs=[pl.BlockSpec(memory_space=pltpu.HBM)] * len(operands),
        out_specs=pl.BlockSpec(memory_space=pltpu.VMEM),
        scratch_shapes=[
            pltpu.VMEM((tokens, model), bf16),
            pltpu.VMEM((tokens, hidden), bf16),
            pltpu.VMEM((tokens, hidden), bf16),
            pltpu.VMEM((tokens, hidden), bf16),
            pltpu.VMEM((tokens, model), bf16),
            pltpu.VMEM((2 * width, model), bf16),
            pltpu.VMEM((width, hidden), bf16),
            pltpu.VMEM((width, hidden), bf16),
            pltpu.VMEM((width, hidden), bf16),
            pltpu.VMEM((width, model), bf16),
            pltpu.VMEM((2, tokens, STEP), bf16),
            pltpu.VMEM((2, tokens, STEP), bf16),
            pltpu.VMEM((2, tokens, STEP), bf16),
            pltpu.SemaphoreType.DMA((steps,)),
        ],
        compiler_params=pltpu.CompilerParams(vmem_limit_bytes=60 * 2**20),
        cost_estimate=pl.CostEstimate(
            flops=6 * tokens * width * (model + hidden),
            bytes_accessed=2 * (2 * tokens * model + 3 * tokens * hidden),
            transcendentals=tokens * hidden,
        ),
        name="project",
    )(*operands)


def two_terms(value):
    high = value.astype(jnp.bfloat16)
    return high, (value - high.astype(jnp.float32)).astype(jnp.bfloat16)


def outer(chips, own, other, ids, out, summed, products):
    chip, core = lax.axis_index("dp"), lax.axis_index("mp")
    width = own.shape[0] // 6
    half = width // 2
    span = 3 * half // chips
    summed[...] = own[...] + other[...]
    own_label = 2 * chip + core
    tail_label = jnp.where(core == 1, 2 * chip - 1, -1)
    masks = [(ids[...] == label).astype(jnp.float32) for label in (tail_label, own_label)]
    lane = lax.broadcasted_iota(jnp.int32, (half, 2 * width), 1)
    for module, (left, right) in enumerate(((0, 2), (1, 3), (4, 5))):
        factor = summed[left * width : (left + 1) * width, :]
        high, low = two_terms(jnp.concatenate([factor * mask for mask in masks], axis=0))
        top, bottom = two_terms(summed[right * width : (right + 1) * width, :])
        product = None
        for one, two in ((high, top), (high, bottom), (low, top)):
            both = jnp.concatenate([two, two], axis=0)
            term = lax.dot_general(one, both, NT, preferred_element_type=jnp.float32)
            product = term if product is None else product + term
        products[module] = product
        for label in range(2):
            even = products[module, pl.ds(label * width, half, stride=2), :]
            odd = products[module, pl.ds(label * width + 1, half, stride=2), :]
            packed = jnp.where(lane < width, even, odd)
            row = 0
            while row < half:
                chip_to, inside = divmod(module * half + row, span)
                count = min(span - inside, half - row)
                put = slice(label * span + inside, label * span + inside + count)
                out[chip_to, put, :] = packed[row : row + count]
                row += count


def example_blocks(chips, own, other, ids):
    width = own.shape[0] // 6
    block = (3 * width // chips, 2 * width)
    return pl.pallas_call(
        functools.partial(outer, chips),
        out_shape=jax.ShapeDtypeStruct((chips,) + block, jnp.float32),
        in_specs=[pl.BlockSpec(memory_space=pltpu.VMEM)] * 3,
        out_specs=pl.BlockSpec(memory_space=pltpu.VMEM),
        scratch_shapes=[
            pltpu.VMEM(own.shape, jnp.float32),
            pltpu.VMEM((3, 2 * width, 2 * width), jnp.float32),
        ],
        compiler_params=pltpu.CompilerParams(vmem_limit_bytes=6 * 2**20),
        name="outer",
    )(own, other, ids)


def score(queries, swapped, received, out, rows):
    core = lax.axis_index("mp")
    chips, height, lanes = received.shape
    span = height // 2
    rows[: chips * height, :] = received[...].reshape(chips * height, lanes)
    rows[chips * height :, :] = jnp.zeros((8, lanes), jnp.float32)
    grads = []
    for at in range(span):
        own = rows[pl.ds(span + at, chips, stride=height), :]
        tail = rows[pl.ds(at, chips, stride=height), :]
        tail = jnp.concatenate([tail[1:], jnp.zeros_like(tail[:1])], axis=0)
        grads.append(own + tail)
    terms = jnp.concatenate(two_terms(jnp.concatenate(grads, axis=1)), axis=0)
    coords = queries.shape[1]
    first = core == 0
    mine = jnp.where(first, terms[:, :coords], terms[:, coords:])
    theirs = jnp.where(first, terms[:, coords:], terms[:, :coords])
    scores = lax.dot_general(mine, queries[...], NT, preferred_element_type=jnp.float32)
    scores += lax.dot_general(theirs, swapped[...], NT, preferred_element_type=jnp.float32)
    out[...] = scores[:chips] + scores[chips:]


def partial_scores(queries, swapped, received):
    chips, height, lanes = received.shape
    return pl.pallas_call(
        score,
        out_shape=jax.ShapeDtypeStruct((chips, queries.shape[0]), jnp.float32),
        in_specs=[pl.BlockSpec(memory_space=pltpu.VMEM)] * 3,
        out_specs=pl.BlockSpec(memory_space=pltpu.VMEM),
        scratch_shapes=[pltpu.VMEM((chips * height + 8, lanes), jnp.float32)],
        compiler_params=pltpu.CompilerParams(vmem_limit_bytes=6 * 2**20),
        name="score",
    )(queries, swapped, received)


def body(
    inputs,
    gate_pre,
    up_pre,
    hidden_grad,
    out_grad,
    example_ids,
    gate_in,
    gate_out,
    up_in,
    up_out,
    down_in,
    down_out,
    queries,
):
    chips = lax.axis_size("dp")
    swap = [(0, 1), (1, 0)]
    swapped = lax.ppermute(queries, "mp", swap)
    bases = [base.T for base in (gate_in, gate_out, up_in, up_out, down_in, down_out)]
    own = projections(inputs, gate_pre, up_pre, hidden_grad, out_grad, *bases)
    other = lax.ppermute(own, "mp", swap)
    blocks = example_blocks(chips, own, other, example_ids.reshape(1, -1))
    received = lax.all_to_all(blocks, "dp", split_axis=0, concat_axis=0, tiled=True)
    scores = lax.psum(partial_scores(queries, swapped, received), "dp")
    return lax.dynamic_slice_in_dim(scores, lax.axis_index("dp"), 1, 0)


def solution(mesh):
    placed = (
        P(("parts", "dp"), "mp"),
        P(("parts", "dp"), "mp"),
        P(("parts", "dp"), "mp"),
        P(("parts", "dp"), "mp"),
        P(("parts", "dp"), "mp"),
        P(("parts", "dp")),
        P("mp", None),
        P("mp", None),
        P("mp", None),
        P("mp", None),
        P("mp", None),
        P("mp", None),
        P(None, ("dp", "mp")),
    )
    return jax.shard_map(
        body, mesh=mesh, in_specs=placed, out_specs=P(("parts", "dp", "mp"), None), check_vma=False
    )
```

time: 65.4 us -> 63.9 us (0.977)
  blocking collectives: 0 us -> 34 us
  starting transfers between devices: 24.1 us -> 7.55 us
  local copies, waits for them, and re-layouts: 14.6 us -> 1.59 us
  Pallas kernels: 14.7 us -> 11.5 us
  other arithmetic: 1.27 us -> 0 us
  waiting for transfers between devices: 10 us -> 9 us
    psum x0 -> x1, blocking collectives: none -> 34 us  [body(): scores = lax.psum(partial_scores(queries, swapped, received), 'dp')]
    ppermute x14 -> x0, starting transfers between devices: 23.6 us -> none  [exchanged(): lax.ppermute(blocks[flip], 'dp', [(i, i ^ flip) for i in range(chips)])]
    unnamed x40 -> x6, local copies, waits for them, and re-layouts: 14.6 us -> 1 us
    ppermute x14 -> x0, waiting for transfers between devices: 8.38 us -> none  [exchanged(): lax.ppermute(blocks[flip], 'dp', [(i, i ^ flip) for i in range(chips)])]
    all_to_all x0 -> x1, waiting for transfers between devices: none -> 7.12 us  [body(): lax.all_to_all(blocks, 'dp', split_axis=0, concat_axis=0, tiled=True)]
    all_to_all x0 -> x1, starting transfers between devices: none -> 6.98 us  [body(): lax.all_to_all(blocks, 'dp', split_axis=0, concat_axis=0, tiled=True)]
    pallas_call x2, Pallas kernels: 4.97 us -> 1.52 us  [the longest x1 1.02 us: example_blocks(): pl.pallas_call(functools.partial(outer, chips), out_shape=jax.ShapeDtypeS...]
    add x1 -> x0, other arithmetic: 1.27 us -> none  [body(): return functools.reduce(jnp.add, pieces)]
  transfers between devices with their start and end apart: 16 -> 3, of which waited for: 6 -> 2; matrix products, arithmetic and copies ran while one was open for 0% -> 0% of each run, Pallas kernels for 19% -> 17%
where the time goes in v4:
time: 63.9 us; the launch traced here: 63.6 us
  blocking collectives  34 us (53%)
  Pallas kernels  11.5 us (18%)
  waiting for transfers between devices  9 us (14%)
  starting transfers between devices  7.55 us (12%)
  local copies, waits for them, and re-layouts  1.59 us (2%)
    psum x1, blocking collectives, body(): scores = lax.psum(partial_scores(queries, swapped, received), 'dp')  34 us
    pallas_call x1, Pallas kernels, projections(): pl.pallas_call(project, out_shape=jax.ShapeDtypeStruct((6 * width, tokens...  9.97 us
    all_to_all x1, waiting for transfers between devices, body(): lax.all_to_all(blocks, 'dp', split_axis=0, concat_axis=0, tiled=True)  7.12 us
    all_to_all x1, starting transfers between devices, body(): lax.all_to_all(blocks, 'dp', split_axis=0, concat_axis=0, tiled=True)  6.98 us
    ppermute x1, waiting for transfers between devices, body(): other = lax.ppermute(own, 'mp', swap)  1.88 us
  transfers between devices with their start and end apart: 3, of which 2 were waited for; matrix products, arithmetic and copies ran while one was open for 0% of the time, Pallas kernels for 17%

profile of v4, /device:TPU:0, one launch (start us, length us, event | category | flops | bytes accessed | tf_op | source)
XLA Modules:
  0.0 63.6 jit_solution(1107799093245564553)
XLA Ops:
  0.0 0.5 collective-permute-start
  0.5 0.0 copy-start.2
  0.5 0.0 copy-start.1
  0.5 10.0 %project.1.own = f32[384,192]{1,0:T(8,128)} custom-call(bf16[192,4096]{1,0:T(8,128)(2,1)} %inputs.1, bf16[192,7168]{1,0:T(8,128)(2,1)} %gate_pre.1, bf16[192,7168]{1,0:T(8,128)(2,1)} %up_pre.1, bf16[192,7168]{1,0:T(8,128)(2,1)} %hidden_grad.1, bf16[192,4096]{1,0:T(8,128)(2,1)} %out_grad.1, bf16[64,4096]{1,0:T(8,128)(2,1)} %bitcast.11, ...), custom_call_target="tpu_custom_call" | custom-call | flops 830472192 | bytes 11403264 | tf_op jit(solution)/shard_map/project/pallas_call | solution.py:143
  10.4 0.1 collective-permute-start.1
  10.6 1.9 %collective-permute-done.1.other = f32[384,192]{1,0:T(8,128)S(1)} collective-permute-done((f32[384,192]{1,0:T(8,128)}, f32[384,192]{1,0:T(8,128)S(1)}, u32[]{:S(2)}, u32[]{:S(2)}) %collective-permute-start.1) | collective-permute-done | bytes 294944 | tf_op jit(solution)/shard_map/ppermute | solution.py:284
  12.4 0.0 copy-done.2
  12.4 0.0 copy-start
  12.4 1.0 %copy-done = f32[384,192]{1,0:T(8,128)S(1)} copy-done((f32[384,192]{1,0:T(8,128)S(1)}, f32[384,192]{1,0:T(8,128)}, u32[]{:S(2)}) %copy-start) | copy-done | bytes 294936
  13.4 1.0 %outer.1 = f32[8,24,128]{2,1,0:T(8,128)} custom-call(f32[384,192]{1,0:T(8,128)S(1)} %copy-done, f32[384,192]{1,0:T(8,128)S(1)} %collective-permute-done.1.other, s32[1,192]{1,0:T(1,128)S(1)} %bitcast.7), custom_call_target="tpu_custom_call" | custom-call | tf_op jit(solution)/shard_map/outer/pallas_call | solution.py:215
  14.5 7.0 %all-to-all-start = ((f32[8,24,128]{2,1,0:T(8,128)}), f32[8,24,128]{2,1,0:T(8,128)S(1)}, u32[]{:S(2)}, u32[]{:S(2)}) async-start(f32[8,24,128]{2,1,0:T(8,128)} %outer.1), calls=%async_computation | async-start | bytes 196608 | tf_op jit(solution)/shard_map/all_to_all | solution.py:286
  21.4 7.1 %all-to-all-done.received = f32[8,24,128]{2,1,0:T(8,128)S(1)} async-done(((f32[8,24,128]{2,1,0:T(8,128)}), f32[8,24,128]{2,1,0:T(8,128)S(1)}, u32[]{:S(2)}, u32[]{:S(2)}) %all-to-all-start) | async-done | bytes 98336 | tf_op jit(solution)/shard_map/all_to_all | solution.py:286
  28.6 0.0 collective-permute-done.swapped
  28.6 0.0 copy-done.1
  28.6 0.5 score.1
  29.1 34.0 %psum.7 = f32[8,512]{1,0:T(8,128)S(1)} all-reduce(f32[8,512]{1,0:T(8,128)S(1)} %score.1), channel_id=1, replica_groups=mesh['parts'=2,'dp'=8,'mp'=2] {'dp'}, use_global_device_ids=true, to_apply=%region_0.0 | all-reduce | flops 4096 | bytes 32768 | tf_op jit(solution)/shard_map/psum | solution.py:287
  63.0 0.6 constant_dynamic-slice_fusion
Async XLA Ops:
  0.0 28.6 %collective-permute-start = (bf16[512,768]{1,0:T(8,128)(2,1)}, bf16[512,768]{1,0:T(8,128)(2,1)S(1)}, u32[]{:S(2)}, u32[]{:S(2)}) collective-permute-start(bf16[512,768]{1,0:T(8,128)(2,1)} %queries.1), channel_id=1, source_target_pairs={{0,1},{1,0},{2,3},{3,2},{4,5},{5,4},{6,7},{7,6},{8,9},{9,8},{10,11... | collective-permute-start | bytes 2359304 | tf_op jit(solution)/shard_map/ppermute | solution.py:281
  0.5 12.0 %copy-start.2 = (s32[192]{0:T(256)S(1)}, s32[192]{0:T(256)}, u32[]{:S(2)}) copy-start(s32[192]{0:T(256)} %param.18) | copy-start | bytes 2308
  0.5 28.1 %copy-start.1 = (bf16[512,768]{1,0:T(8,128)(2,1)S(1)}, bf16[512,768]{1,0:T(8,128)(2,1)}, u32[]{:S(2)}) copy-start(bf16[512,768]{1,0:T(8,128)(2,1)} %queries.1) | copy-start | bytes 2359300
  10.4 2.0 %collective-permute-start.1 = (f32[384,192]{1,0:T(8,128)}, f32[384,192]{1,0:T(8,128)S(1)}, u32[]{:S(2)}, u32[]{:S(2)}) collective-permute-start(f32[384,192]{1,0:T(8,128)} %project.1.own), channel_id=1, source_target_pairs={{0,1},{1,0},{2,3},{3,2},{4,5},{5,4},{6,7},{7,6},{8,9},{9,8},{10,11... | collective-permute-start | bytes 884744 | tf_op jit(solution)/shard_map/ppermute | solution.py:284
  12.4 1.0 %copy-start = (f32[384,192]{1,0:T(8,128)S(1)}, f32[384,192]{1,0:T(8,128)}, u32[]{:S(2)}) copy-start(f32[384,192]{1,0:T(8,128)} %project.1.own) | copy-start | bytes 884740
  14.5 14.1 %all-to-all-start = ((f32[8,24,128]{2,1,0:T(8,128)}), f32[8,24,128]{2,1,0:T(8,128)S(1)}, u32[]{:S(2)}, u32[]{:S(2)}) async-start(f32[8,24,128]{2,1,0:T(8,128)} %outer.1), calls=%async_computation | async-start | bytes 196608 | tf_op jit(solution)/shard_map/all_to_all | solution.py:286

commit v5 on v4

--- a/solution.py
+++ b/solution.py
@@ -40,6 +40,8 @@
     made_hidden,
     made_up,
     made_gate,
+    sum_in,
+    sums,
     sems,
 ):
     width = gate_in.shape[0]
@@ -91,26 +93,26 @@
                 slope = sig + silu * (1.0 - sig)
                 made_gate[(target,) + put] = (back * up * slope).astype(jnp.bfloat16)
 
-    def add(low, high, base, values, first):
-        value = lax.dot_general(base, values, NT, preferred_element_type=jnp.float32)
+    def add(total, values, base, first):
+        value = lax.dot_general(values, base, NT, preferred_element_type=jnp.float32)
         if first:
-            out[low * width : high * width, :] = value
+            total[...] = value
         else:
-            out[low * width : high * width, :] += value
+            total[...] += value
 
     def hidden_dots(step, part):
         at = slice(step * STEP + part * PART, step * STEP + (part + 1) * PART)
         inner = (step % 2, slice(None), slice(part * PART, (part + 1) * PART))
         first = step == 0 and part == 0
-        add(2, 3, v_gate_out[:, at], made_gate[inner], first)
-        add(3, 4, v_up_out[:, at], made_up[inner], first)
-        add(4, 5, v_down_in[:, at], made_hidden[inner], first)
+        add(sums.at[0], made_gate[inner], v_gate_out[:, at], first)
+        add(sums.at[1], made_up[inner], v_up_out[:, at], first)
+        add(sums.at[2], made_hidden[inner], v_down_in[:, at], first)
 
     def model_dots(step, part):
         at = slice(step * STEP + part * PART, step * STEP + (part + 1) * PART)
         first = step == 0 and part == 0
-        add(0, 2, v_in[:, at], v_inputs[:, at], first)
-        add(5, 6, v_down_out[:, at], v_out_grad[:, at], first)
+        add(sum_in, v_inputs[:, at], v_in[:, at], first)
+        add(sums.at[3], v_out_grad[:, at], v_down_out[:, at], first)
 
     for step in range(min(AHEAD, hidden_steps)):
         for copy in copies[step]:
@@ -129,6 +131,9 @@
                 model_dots(step, part)
     for part in range(STEP // PART):
         hidden_dots(hidden_steps - 1, part)
+    out[:, : 2 * width] = sum_in[...]
+    out[:, 2 * width : 4 * width] = jnp.concatenate([sums[0], sums[1]], axis=1)
+    out[:, 4 * width :] = jnp.concatenate([sums[2], sums[3]], axis=1)
 
 
 def projections(*operands):
@@ -142,7 +147,7 @@
     bf16 = jnp.bfloat16
     return pl.pallas_call(
         project,
-        out_shape=jax.ShapeDtypeStruct((6 * width, tokens), jnp.float32),
+        out_shape=jax.ShapeDtypeStruct((tokens, 6 * width), jnp.float32),
         in_specs=[pl.BlockSpec(memory_space=pltpu.HBM)] * len(operands),
         out_specs=pl.BlockSpec(memory_space=pltpu.VMEM),
         scratch_shapes=[
@@ -159,9 +164,11 @@
             pltpu.VMEM((2, tokens, STEP), bf16),
             pltpu.VMEM((2, tokens, STEP), bf16),
             pltpu.VMEM((2, tokens, STEP), bf16),
+            pltpu.VMEM((tokens, 2 * width), jnp.float32),
+            pltpu.VMEM((4, tokens, width), jnp.float32),
             pltpu.SemaphoreType.DMA((steps,)),
         ],
-        compiler_params=pltpu.CompilerParams(vmem_limit_bytes=60 * 2**20),
+        compiler_params=pltpu.CompilerParams(vmem_limit_bytes=427 * 2**17),
         cost_estimate=pl.CostEstimate(
             flops=6 * tokens * width * (model + hidden),
             bytes_accessed=2 * (2 * tokens * model + 3 * tokens * hidden),
@@ -178,10 +185,10 @@
 
 def outer(chips, own, other, ids, out, summed, products):
     chip, core = lax.axis_index("dp"), lax.axis_index("mp")
-    width = own.shape[0] // 6
+    width = own.shape[1] // 6
     half = width // 2
     span = 3 * half // chips
-    summed[...] = own[...] + other[...]
+    summed[...] = (own[...] + other[...]).T
     own_label = 2 * chip + core
     tail_label = jnp.where(core == 1, 2 * chip - 1, -1)
     masks = [(ids[...] == label).astype(jnp.float32) for label in (tail_label, own_label)]
@@ -210,7 +217,7 @@
 
 
 def example_blocks(chips, own, other, ids):
-    width = own.shape[0] // 6
+    width = own.shape[1] // 6
     block = (3 * width // chips, 2 * width)
     return pl.pallas_call(
         functools.partial(outer, chips),
@@ -218,7 +225,7 @@
         in_specs=[pl.BlockSpec(memory_space=pltpu.VMEM)] * 3,
         out_specs=pl.BlockSpec(memory_space=pltpu.VMEM),
         scratch_shapes=[
-            pltpu.VMEM(own.shape, jnp.float32),
+            pltpu.VMEM(own.shape[::-1], jnp.float32),
             pltpu.VMEM((3, 2 * width, 2 * width), jnp.float32),
         ],
         compiler_params=pltpu.CompilerParams(vmem_limit_bytes=6 * 2**20),
@@ -284,8 +291,9 @@
     other = lax.ppermute(own, "mp", swap)
     blocks = example_blocks(chips, own, other, example_ids.reshape(1, -1))
     received = lax.all_to_all(blocks, "dp", split_axis=0, concat_axis=0, tiled=True)
-    scores = lax.psum(partial_scores(queries, swapped, received), "dp")
-    return lax.dynamic_slice_in_dim(scores, lax.axis_index("dp"), 1, 0)
+    scores = partial_scores(queries, swapped, received)[:, None]
+    pieces = lax.all_to_all(scores, "dp", split_axis=0, concat_axis=0, tiled=True)
+    return jnp.sum(pieces, axis=0)
 
 
 def solution(mesh):

time: 63.9 us -> 35.7 us (0.56)
  blocking collectives: 34 us -> 22.8 us
  waiting for transfers between devices: 9 us -> 1.53 us
  starting transfers between devices: 7.55 us -> 0.57 us
  Pallas kernels: 11.5 us -> 9.91 us
  local copies, waits for them, and re-layouts: 1.59 us -> 0.05 us
    psum x1 -> x0, blocking collectives: 34 us -> none  [body(): scores = lax.psum(partial_scores(queries, swapped, received), 'dp')]
    all_to_all x0 -> x2, blocking collectives: none -> 22.8 us  [the longest x1 13.9 us: body(): lax.all_to_all(blocks, 'dp', split_axis=0, concat_axis=0, tiled=True)]
    all_to_all x1 -> x0, waiting for transfers between devices: 7.12 us -> none  [body(): lax.all_to_all(blocks, 'dp', split_axis=0, concat_axis=0, tiled=True)]
    all_to_all x1 -> x0, starting transfers between devices: 6.98 us -> none  [body(): lax.all_to_all(blocks, 'dp', split_axis=0, concat_axis=0, tiled=True)]
    pallas_call x1, Pallas kernels: 9.97 us -> 8.93 us  [projections(): pl.pallas_call(project, out_shape=jax.ShapeDtypeStruct((tokens, 6 * width...]
    unnamed x6 -> x4, local copies, waits for them, and re-layouts: 1 us -> 0.01 us
  transfers between devices with their start and end apart: 3 -> 2, of which waited for: 2 -> 1; matrix products, arithmetic and copies ran while one was open for 0% -> 0% of each run, Pallas kernels for 17% -> 26%
where the time goes in v5:
time: 35.7 us; the launch traced here: 35.5 us
  blocking collectives  22.8 us (64%)
  Pallas kernels  9.91 us (28%)
  waiting for transfers between devices  1.53 us (4%)
  other arithmetic  0.61 us (2%)
  starting transfers between devices  0.57 us (2%)
    all_to_all x1, blocking collectives, body(): lax.all_to_all(blocks, 'dp', split_axis=0, concat_axis=0, tiled=True)  13.9 us
    all_to_all x1, blocking collectives, body(): lax.all_to_all(scores, 'dp', split_axis=0, concat_axis=0, tiled=True)  8.94 us
    pallas_call x1, Pallas kernels, projections(): pl.pallas_call(project, out_shape=jax.ShapeDtypeStruct((tokens, 6 * width...  8.93 us
    ppermute x1, waiting for transfers between devices, body(): other = lax.ppermute(own, 'mp', swap)  1.53 us
  transfers between devices with their start and end apart: 2, of which 1 were waited for; matrix products, arithmetic and copies ran while one was open for 0% of the time, Pallas kernels for 26%

profile of v5, /device:TPU:0, one launch (start us, length us, event | category | flops | bytes accessed | tf_op | source)
XLA Modules:
  0.0 35.5 jit_solution(5051933317817182461)
XLA Ops:
  0.0 0.5 %collective-permute-start = (bf16[512,768]{1,0:T(8,128)(2,1)}, bf16[512,768]{1,0:T(8,128)(2,1)S(1)}, u32[]{:S(2)}, u32[]{:S(2)}) collective-permute-start(bf16[512,768]{1,0:T(8,128)(2,1)} %queries.1), channel_id=1, source_target_pairs={{0,1},{1,0},{2,3},{3,2},{4,5},{5,4},{6,7},{7,6},{8,9},{9,8},{10,11... | collective-permute-start | bytes 2359304 | tf_op jit(solution)/shard_map/ppermute | solution.py:288
  0.5 0.0 copy-start.1
  0.5 0.0 copy-start
  0.5 8.9 %project.1.own = f32[192,384]{1,0:T(8,128)S(1)} custom-call(bf16[192,4096]{1,0:T(8,128)(2,1)} %inputs.1, bf16[192,7168]{1,0:T(8,128)(2,1)} %gate_pre.1, bf16[192,7168]{1,0:T(8,128)(2,1)} %up_pre.1, bf16[192,7168]{1,0:T(8,128)(2,1)} %hidden_grad.1, bf16[192,4096]{1,0:T(8,128)(2,1)} %out_grad.1, bf16[64,4096]{1,0:T(8,128)(2,1)} %bitcast.14, ...), custom_call_target="tpu_custom_call" | custom-call | flops 830472192 | bytes 11403264 | tf_op jit(solution)/shard_map/project/pallas_call | solution.py:148
  9.4 0.1 collective-permute-start.1
  9.5 1.5 %collective-permute-done.1.other = f32[192,384]{1,0:T(8,128)S(1)} collective-permute-done((f32[192,384]{1,0:T(8,128)S(1)}, f32[192,384]{1,0:T(8,128)S(1)}, u32[]{:S(2)}, u32[]{:S(2)}) %collective-permute-start.1) | collective-permute-done | bytes 294944 | tf_op jit(solution)/shard_map/ppermute | solution.py:291
  11.0 0.0 copy-done.1
  11.0 0.5 %outer.1 = f32[8,24,128]{2,1,0:T(8,128)S(1)} custom-call(f32[192,384]{1,0:T(8,128)S(1)} %project.1.own, f32[192,384]{1,0:T(8,128)S(1)} %collective-permute-done.1.other, s32[1,192]{1,0:T(1,128)S(1)} %bitcast.10), custom_call_target="tpu_custom_call" | custom-call | tf_op jit(solution)/shard_map/outer/pallas_call | solution.py:222
  11.5 13.9 %all_to_all.10.received = f32[8,24,128]{2,1,0:T(8,128)S(1)} all-to-all(f32[8,24,128]{2,1,0:T(8,128)S(1)} %outer.1), channel_id=1, replica_groups=mesh['parts'=2,'dp'=8,'mp'=2] {'dp'}, dimensions={0} | all-to-all | bytes 196608 | tf_op jit(solution)/shard_map/all_to_all | solution.py:293
  25.4 0.0 collective-permute-done.swapped
  25.4 0.0 copy-done
  25.4 0.5 %score.1 = f32[8,512]{1,0:T(8,128)S(1)} custom-call(bf16[512,768]{1,0:T(8,128)(2,1)S(1)} %copy-done, bf16[512,768]{1,0:T(8,128)(2,1)S(1)} %collective-permute-done.swapped, f32[8,24,128]{2,1,0:T(8,128)S(1)} %all_to_all.10.received), custom_call_target="tpu_custom_call" | custom-call | tf_op jit(solution)/shard_map/score/pallas_call | solution.py:260
  26.0 8.9 %all_to_all.11 = f32[8,1,512]{2,1,0:T(1,128)S(1)} all-to-all(f32[8,1,512]{2,1,0:T(1,128)S(1)} %copy.14), channel_id=1, replica_groups=mesh['parts'=2,'dp'=8,'mp'=2] {'dp'}, dimensions={0} | all-to-all | bytes 32768 | tf_op jit(solution)/shard_map/all_to_all | solution.py:295
  34.9 0.6 %reduce_sum.11 = f32[512]{0:T(512)} reduce(f32[8,1,512]{2,1,0:T(1,128)S(1)} %all_to_all.11, f32[]{:T(128)} %constant.0.clone.1), dimensions={0,1}, to_apply=%region_0.0 | reduce | flops 3584 | bytes 18436 | tf_op jit(solution)/shard_map/reduce_sum | solution.py:296
  (1 shorter events, 0.0 us)
Async XLA Ops:
  0.0 25.4 %collective-permute-start = (bf16[512,768]{1,0:T(8,128)(2,1)}, bf16[512,768]{1,0:T(8,128)(2,1)S(1)}, u32[]{:S(2)}, u32[]{:S(2)}) collective-permute-start(bf16[512,768]{1,0:T(8,128)(2,1)} %queries.1), channel_id=1, source_target_pairs={{0,1},{1,0},{2,3},{3,2},{4,5},{5,4},{6,7},{7,6},{8,9},{9,8},{10,11... | collective-permute-start | bytes 2359304 | tf_op jit(solution)/shard_map/ppermute | solution.py:288
  0.5 10.6 %copy-start.1 = (s32[192]{0:T(256)S(1)}, s32[192]{0:T(256)}, u32[]{:S(2)}) copy-start(s32[192]{0:T(256)} %param.18) | copy-start | bytes 2308
  0.5 25.0 %copy-start = (bf16[512,768]{1,0:T(8,128)(2,1)S(1)}, bf16[512,768]{1,0:T(8,128)(2,1)}, u32[]{:S(2)}) copy-start(bf16[512,768]{1,0:T(8,128)(2,1)} %queries.1) | copy-start | bytes 2359300
  9.4 1.6 %collective-permute-start.1 = (f32[192,384]{1,0:T(8,128)S(1)}, f32[192,384]{1,0:T(8,128)S(1)}, u32[]{:S(2)}, u32[]{:S(2)}) collective-permute-start(f32[192,384]{1,0:T(8,128)S(1)} %project.1.own), channel_id=1, source_target_pairs={{0,1},{1,0},{2,3},{3,2},{4,5},{5,4},{6,7},{7,6},{8,9},{9,8},{10,11... | collective-permute-start | bytes 884744 | tf_op jit(solution)/shard_map/ppermute | solution.py:291

commit v6 on v5

--- a/solution.py
+++ b/solution.py
@@ -8,10 +8,9 @@
 from jax.sharding import PartitionSpec as P
 
 NT = (((1,), (1,)), ((), ()))
-STEP = 1024
-PART = 512
+STEP = 512
 ROWS = 16
-AHEAD = 3
+AHEAD = 6
 
 
 def project(
@@ -37,6 +36,7 @@
     v_up_out,
     v_down_in,
     v_down_out,
+    tanhs,
     made_hidden,
     made_up,
     made_gate,
@@ -49,49 +49,52 @@
     hidden_steps = gate_pre.shape[1] // STEP
     model_steps = inputs.shape[1] // STEP
     copies = []
-
-    def plan(pairs):
-        made_here = []
-        for source, target in pairs:
-            copy = pltpu.make_async_copy(source, target, sems.at[sum(map(len, copies)) + len(made_here)])
-            made_here.append(copy)
-        copies.append(made_here)
-
-    for step in range(hidden_steps):
-        at = pl.ds(step * STEP, STEP)
-        pairs = [
-            (gate_pre.at[:, at], v_gate.at[:, at]),
-            (up_pre.at[:, at], v_up.at[:, at]),
-            (hidden_grad.at[:, at], v_back.at[:, at]),
-            (gate_out.at[:, at], v_gate_out.at[:, at]),
-            (up_out.at[:, at], v_up_out.at[:, at]),
-            (down_in.at[:, at], v_down_in.at[:, at]),
-        ]
-        if step < model_steps:
-            pairs += [
+    for step in range(hidden_steps + model_steps):
+        if step < hidden_steps:
+            at = pl.ds(step * STEP, STEP)
+            pairs = [
+                (gate_pre.at[:, at], v_gate.at[:, at]),
+                (up_pre.at[:, at], v_up.at[:, at]),
+                (hidden_grad.at[:, at], v_back.at[:, at]),
+                (gate_out.at[:, at], v_gate_out.at[:, at]),
+                (up_out.at[:, at], v_up_out.at[:, at]),
+                (down_in.at[:, at], v_down_in.at[:, at]),
+            ]
+        else:
+            at = pl.ds((step - hidden_steps) * STEP, STEP)
+            pairs = [
                 (inputs.at[:, at], v_inputs.at[:, at]),
                 (gate_in.at[:, at], v_in.at[pl.ds(0, width), at]),
                 (up_in.at[:, at], v_in.at[pl.ds(width, width), at]),
                 (out_grad.at[:, at], v_out_grad.at[:, at]),
                 (down_out.at[:, at], v_down_out.at[:, at]),
             ]
-        plan(pairs)
-
-    def elementwise(step, part):
-        target = step % 2
-        for top in range(0, tokens, ROWS):
-            for left in range(part * PART, (part + 1) * PART, 256):
-                at = (slice(top, top + ROWS), slice(step * STEP + left, step * STEP + left + 256))
-                put = (slice(top, top + ROWS), slice(left, left + 256))
-                gate = v_gate[at].astype(jnp.float32)
-                up = v_up[at].astype(jnp.float32)
-                back = v_back[at].astype(jnp.float32)
-                sig = 0.5 * jnp.tanh(0.5 * gate) + 0.5
-                silu = gate * sig
-                made_hidden[(target,) + put] = (silu * up).astype(jnp.bfloat16)
-                made_up[(target,) + put] = (back * silu).astype(jnp.bfloat16)
-                slope = sig + silu * (1.0 - sig)
-                made_gate[(target,) + put] = (back * up * slope).astype(jnp.bfloat16)
+        first = sum(map(len, copies))
+        copies.append(
+            [
+                pltpu.make_async_copy(source, target, sems.at[first + i])
+                for i, (source, target) in enumerate(pairs)
+            ]
+        )
+
+    def columns(step):
+        return slice(step * STEP, (step + 1) * STEP)
+
+    def squash(step, rows):
+        half = 0.5 * v_gate[rows, columns(step)].astype(jnp.float32)
+        tanhs[step % 2, rows, :] = jnp.tanh(half)
+
+    def products(step, rows):
+        at = (rows, columns(step))
+        put = (step % 2, rows, slice(None))
+        tanh = tanhs[put]
+        up = v_up[at].astype(jnp.float32)
+        back = v_back[at].astype(jnp.float32)
+        plus = 1.0 + tanh
+        silu = 0.5 * v_gate[at].astype(jnp.float32) * plus
+        made_hidden[put] = (silu * up).astype(jnp.bfloat16)
+        made_up[put] = (back * silu).astype(jnp.bfloat16)
+        made_gate[put] = (back * up * (plus + silu * (1.0 - tanh))).astype(jnp.bfloat16)
 
     def add(total, values, base, first):
         value = lax.dot_general(values, base, NT, preferred_element_type=jnp.float32)
@@ -100,39 +103,39 @@
         else:
             total[...] += value
 
-    def hidden_dots(step, part):
-        at = slice(step * STEP + part * PART, step * STEP + (part + 1) * PART)
-        inner = (step % 2, slice(None), slice(part * PART, (part + 1) * PART))
-        first = step == 0 and part == 0
-        add(sums.at[0], made_gate[inner], v_gate_out[:, at], first)
-        add(sums.at[1], made_up[inner], v_up_out[:, at], first)
-        add(sums.at[2], made_hidden[inner], v_down_in[:, at], first)
-
-    def model_dots(step, part):
-        at = slice(step * STEP + part * PART, step * STEP + (part + 1) * PART)
-        first = step == 0 and part == 0
-        add(sum_in, v_inputs[:, at], v_in[:, at], first)
-        add(sums.at[3], v_out_grad[:, at], v_down_out[:, at], first)
-
-    for step in range(min(AHEAD, hidden_steps)):
+    def hidden_dot(step, which):
+        made = (made_gate, made_up, made_hidden)[which]
+        base = (v_gate_out, v_up_out, v_down_in)[which]
+        add(sums.at[which], made[step % 2], base[:, columns(step)], step == 0)
+
+    def model_dots(step):
+        at = columns(step)
+        add(sum_in, v_inputs[:, at], v_in[:, at], step == 0)
+        add(sums.at[3], v_out_grad[:, at], v_down_out[:, at], step == 0)
+
+    steps = hidden_steps + model_steps
+    for step in range(AHEAD):
         for copy in copies[step]:
             copy.start()
-    for step in range(hidden_steps):
-        if step + AHEAD < hidden_steps:
-            for copy in copies[step + AHEAD]:
+    for block in range(steps):
+        if block + AHEAD < steps:
+            for copy in copies[block + AHEAD]:
                 copy.start()
-        for copy in copies[step]:
+        for copy in copies[block]:
             copy.wait()
-        for part in range(STEP // PART):
-            elementwise(step, part)
-            if step >= 1:
-                hidden_dots(step - 1, part)
-            if step < model_steps:
-                model_dots(step, part)
-    for part in range(STEP // PART):
-        hidden_dots(hidden_steps - 1, part)
+        groups = tokens // ROWS
+        for group in range(groups):
+            rows = slice(group * ROWS, (group + 1) * ROWS)
+            if 0 <= block - 2 < hidden_steps and group % (groups // 3) == 0:
+                hidden_dot(block - 2, group // (groups // 3))
+            if 0 <= block - 1 < hidden_steps:
+                products(block - 1, rows)
+            if block < hidden_steps:
+                squash(block, rows)
+        if block >= hidden_steps:
+            model_dots(block - hidden_steps)
     out[:, : 2 * width] = sum_in[...]
-    out[:, 2 * width : 4 * width] = jnp.concatenate([sums[0], sums[1]], axis=1)
+    out[:, 2 * width : 4 * width] = jnp.concatenate([0.5 * sums[0], sums[1]], axis=1)
     out[:, 4 * width :] = jnp.concatenate([sums[2], sums[3]], axis=1)
 
 
@@ -141,8 +144,8 @@
     width = operands[5].shape[0]
     tokens, model = inputs.shape
     hidden = gate_pre.shape[1]
-    assert hidden % STEP == 0 and model % STEP == 0 and model <= hidden
-    assert tokens % ROWS == 0
+    assert hidden % STEP == 0 and model % STEP == 0 and model >= 2 * STEP
+    assert tokens % (3 * ROWS) == 0
     steps = 6 * (hidden // STEP) + 5 * (model // STEP)
     bf16 = jnp.bfloat16
     return pl.pallas_call(
@@ -161,6 +164,7 @@
             pltpu.VMEM((width, hidden), bf16),
             pltpu.VMEM((width, hidden), bf16),
             pltpu.VMEM((width, model), bf16),
+            pltpu.VMEM((2, tokens, STEP), jnp.float32),
             pltpu.VMEM((2, tokens, STEP), bf16),
             pltpu.VMEM((2, tokens, STEP), bf16),
             pltpu.VMEM((2, tokens, STEP), bf16),

time: 35.7 us -> 38.6 us (1.081)
  Pallas kernels: 9.91 us -> 12.7 us
    pallas_call x1, Pallas kernels: 8.93 us -> 11.8 us  [projections(): pl.pallas_call(project, out_shape=jax.ShapeDtypeStruct((tokens, 6 * width...]
  transfers between devices with their start and end apart: 2 -> 2, of which waited for: 1 -> 1; matrix products, arithmetic and copies ran while one was open for 0% -> 0% of each run, Pallas kernels for 26% -> 32%
where the time goes in v6:
time: 38.6 us; the launch traced here: 38.4 us
  blocking collectives  22.9 us (59%)
  Pallas kernels  12.7 us (33%)
  waiting for transfers between devices  1.52 us (4%)
  other arithmetic  0.61 us (2%)
  starting transfers between devices  0.58 us (2%)
    all_to_all x1, blocking collectives, body(): lax.all_to_all(blocks, 'dp', split_axis=0, concat_axis=0, tiled=True)  13.9 us
    pallas_call x1, Pallas kernels, projections(): pl.pallas_call(project, out_shape=jax.ShapeDtypeStruct((tokens, 6 * width...  11.8 us
    all_to_all x1, blocking collectives, body(): lax.all_to_all(scores, 'dp', split_axis=0, concat_axis=0, tiled=True)  8.94 us
    ppermute x1, waiting for transfers between devices, body(): other = lax.ppermute(own, 'mp', swap)  1.52 us
  transfers between devices with their start and end apart: 2, of which 1 were waited for; matrix products, arithmetic and copies ran while one was open for 0% of the time, Pallas kernels for 32%

profile of v6, /device:TPU:0, one launch (start us, length us, event | category | flops | bytes accessed | tf_op | source)
XLA Modules:
  0.0 38.4 jit_solution(16673145283299546056)
XLA Ops:
  0.0 0.5 %collective-permute-start = (bf16[512,768]{1,0:T(8,128)(2,1)}, bf16[512,768]{1,0:T(8,128)(2,1)S(1)}, u32[]{:S(2)}, u32[]{:S(2)}) collective-permute-start(bf16[512,768]{1,0:T(8,128)(2,1)} %queries.1), channel_id=1, source_target_pairs={{0,1},{1,0},{2,3},{3,2},{4,5},{5,4},{6,7},{7,6},{8,9},{9,8},{10,11... | collective-permute-start | bytes 2359304 | tf_op jit(solution)/shard_map/ppermute | solution.py:292
  0.5 0.0 copy-start.1
  0.5 0.0 copy-start
  0.5 11.8 %project.1.own = f32[192,384]{1,0:T(8,128)S(1)} custom-call(bf16[192,4096]{1,0:T(8,128)(2,1)} %inputs.1, bf16[192,7168]{1,0:T(8,128)(2,1)} %gate_pre.1, bf16[192,7168]{1,0:T(8,128)(2,1)} %up_pre.1, bf16[192,7168]{1,0:T(8,128)(2,1)} %hidden_grad.1, bf16[192,4096]{1,0:T(8,128)(2,1)} %out_grad.1, bf16[64,4096]{1,0:T(8,128)(2,1)} %bitcast.14, ...), custom_call_target="tpu_custom_call" | custom-call | flops 830472192 | bytes 11403264 | tf_op jit(solution)/shard_map/project/pallas_call | solution.py:151
  12.2 0.1 collective-permute-start.1
  12.4 1.5 %collective-permute-done.1.other = f32[192,384]{1,0:T(8,128)S(1)} collective-permute-done((f32[192,384]{1,0:T(8,128)S(1)}, f32[192,384]{1,0:T(8,128)S(1)}, u32[]{:S(2)}, u32[]{:S(2)}) %collective-permute-start.1) | collective-permute-done | bytes 294944 | tf_op jit(solution)/shard_map/ppermute | solution.py:295
  13.9 0.0 copy-done.1
  13.9 0.5 %outer.1 = f32[8,24,128]{2,1,0:T(8,128)S(1)} custom-call(f32[192,384]{1,0:T(8,128)S(1)} %project.1.own, f32[192,384]{1,0:T(8,128)S(1)} %collective-permute-done.1.other, s32[1,192]{1,0:T(1,128)S(1)} %bitcast.10), custom_call_target="tpu_custom_call" | custom-call | tf_op jit(solution)/shard_map/outer/pallas_call | solution.py:226
  14.4 13.9 %all_to_all.10.received = f32[8,24,128]{2,1,0:T(8,128)S(1)} all-to-all(f32[8,24,128]{2,1,0:T(8,128)S(1)} %outer.1), channel_id=1, replica_groups=mesh['parts'=2,'dp'=8,'mp'=2] {'dp'}, dimensions={0} | all-to-all | bytes 196608 | tf_op jit(solution)/shard_map/all_to_all | solution.py:297
  28.3 0.0 collective-permute-done.swapped
  28.3 0.0 copy-done
  28.3 0.5 %score.1 = f32[8,512]{1,0:T(8,128)S(1)} custom-call(bf16[512,768]{1,0:T(8,128)(2,1)S(1)} %copy-done, bf16[512,768]{1,0:T(8,128)(2,1)S(1)} %collective-permute-done.swapped, f32[8,24,128]{2,1,0:T(8,128)S(1)} %all_to_all.10.received), custom_call_target="tpu_custom_call" | custom-call | tf_op jit(solution)/shard_map/score/pallas_call | solution.py:264
  28.8 8.9 %all_to_all.11 = f32[8,1,512]{2,1,0:T(1,128)S(1)} all-to-all(f32[8,1,512]{2,1,0:T(1,128)S(1)} %copy.14), channel_id=1, replica_groups=mesh['parts'=2,'dp'=8,'mp'=2] {'dp'}, dimensions={0} | all-to-all | bytes 32768 | tf_op jit(solution)/shard_map/all_to_all | solution.py:299
  37.8 0.6 %reduce_sum.11 = f32[512]{0:T(512)} reduce(f32[8,1,512]{2,1,0:T(1,128)S(1)} %all_to_all.11, f32[]{:T(128)} %constant.0.clone.1), dimensions={0,1}, to_apply=%region_0.0 | reduce | flops 3584 | bytes 18436 | tf_op jit(solution)/shard_map/reduce_sum | solution.py:300
  (1 shorter events, 0.0 us)
Async XLA Ops:
  0.0 28.3 %collective-permute-start = (bf16[512,768]{1,0:T(8,128)(2,1)}, bf16[512,768]{1,0:T(8,128)(2,1)S(1)}, u32[]{:S(2)}, u32[]{:S(2)}) collective-permute-start(bf16[512,768]{1,0:T(8,128)(2,1)} %queries.1), channel_id=1, source_target_pairs={{0,1},{1,0},{2,3},{3,2},{4,5},{5,4},{6,7},{7,6},{8,9},{9,8},{10,11... | collective-permute-start | bytes 2359304 | tf_op jit(solution)/shard_map/ppermute | solution.py:292
  0.5 13.4 %copy-start.1 = (s32[192]{0:T(256)S(1)}, s32[192]{0:T(256)}, u32[]{:S(2)}) copy-start(s32[192]{0:T(256)} %param.18) | copy-start | bytes 2308
  0.5 27.8 %copy-start = (bf16[512,768]{1,0:T(8,128)(2,1)S(1)}, bf16[512,768]{1,0:T(8,128)(2,1)}, u32[]{:S(2)}) copy-start(bf16[512,768]{1,0:T(8,128)(2,1)} %queries.1) | copy-start | bytes 2359300
  12.2 1.6 %collective-permute-start.1 = (f32[192,384]{1,0:T(8,128)S(1)}, f32[192,384]{1,0:T(8,128)S(1)}, u32[]{:S(2)}, u32[]{:S(2)}) collective-permute-start(f32[192,384]{1,0:T(8,128)S(1)} %project.1.own), channel_id=1, source_target_pairs={{0,1},{1,0},{2,3},{3,2},{4,5},{5,4},{6,7},{7,6},{8,9},{9,8},{10,11... | collective-permute-start | bytes 884744 | tf_op jit(solution)/shard_map/ppermute | solution.py:295

commit v7 on v6

--- a/solution.py
+++ b/solution.py
@@ -8,9 +8,9 @@
 from jax.sharding import PartitionSpec as P
 
 NT = (((1,), (1,)), ((), ()))
-STEP = 512
+PIECE = 2048
 ROWS = 16
-AHEAD = 6
+DEPTH = 512
 
 
 def project(
@@ -36,7 +36,6 @@
     v_up_out,
     v_down_in,
     v_down_out,
-    tanhs,
     made_hidden,
     made_up,
     made_gate,
@@ -46,94 +45,94 @@
 ):
     width = gate_in.shape[0]
     tokens = inputs.shape[0]
-    hidden_steps = gate_pre.shape[1] // STEP
-    model_steps = inputs.shape[1] // STEP
+    hidden, model = gate_pre.shape[1], inputs.shape[1]
     copies = []
-    for step in range(hidden_steps + model_steps):
-        if step < hidden_steps:
-            at = pl.ds(step * STEP, STEP)
-            pairs = [
-                (gate_pre.at[:, at], v_gate.at[:, at]),
-                (up_pre.at[:, at], v_up.at[:, at]),
-                (hidden_grad.at[:, at], v_back.at[:, at]),
-                (gate_out.at[:, at], v_gate_out.at[:, at]),
-                (up_out.at[:, at], v_up_out.at[:, at]),
-                (down_in.at[:, at], v_down_in.at[:, at]),
-            ]
-        else:
-            at = pl.ds((step - hidden_steps) * STEP, STEP)
-            pairs = [
-                (inputs.at[:, at], v_inputs.at[:, at]),
-                (gate_in.at[:, at], v_in.at[pl.ds(0, width), at]),
-                (up_in.at[:, at], v_in.at[pl.ds(width, width), at]),
-                (out_grad.at[:, at], v_out_grad.at[:, at]),
-                (down_out.at[:, at], v_down_out.at[:, at]),
-            ]
-        first = sum(map(len, copies))
-        copies.append(
-            [
-                pltpu.make_async_copy(source, target, sems.at[first + i])
-                for i, (source, target) in enumerate(pairs)
-            ]
-        )
-
-    def columns(step):
-        return slice(step * STEP, (step + 1) * STEP)
-
-    def squash(step, rows):
-        half = 0.5 * v_gate[rows, columns(step)].astype(jnp.float32)
-        tanhs[step % 2, rows, :] = jnp.tanh(half)
-
-    def products(step, rows):
-        at = (rows, columns(step))
-        put = (step % 2, rows, slice(None))
-        tanh = tanhs[put]
+
+    def copy(source, target):
+        copies.append(pltpu.make_async_copy(source, target, sems.at[len(copies)]))
+        return copies[-1]
+
+    def whole(*pairs):
+        return [copy(source, target) for source, target in pairs]
+
+    def piece(at, *pairs):
+        return [copy(source.at[:, at], target.at[:, at]) for source, target in pairs]
+
+    edges = [0] + list(range(PIECE // 2, hidden, PIECE)) + [hidden]
+    pieces = [slice(low, high) for low, high in zip(edges, edges[1:])]
+    activations = ((gate_pre, v_gate), (up_pre, v_up), (hidden_grad, v_back))
+    arrivals = [piece(pl.ds(0, pieces[0].stop), *activations)]
+    hidden_bases = whole((gate_out, v_gate_out), (up_out, v_up_out), (down_in, v_down_in))
+    for at in pieces[1:]:
+        arrivals.append(piece(pl.ds(at.start, at.stop - at.start), *activations))
+    for_inputs = whole(
+        (gate_in, v_in.at[pl.ds(0, width), :]),
+        (up_in, v_in.at[pl.ds(width, width), :]),
+        (inputs, v_inputs),
+    )
+    for_out_grad = whole((down_out, v_down_out))
+    halves = [slice(0, model // 2), slice(model // 2, model)]
+    for_halves = [piece(pl.ds(at.start, model // 2), (out_grad, v_out_grad)) for at in halves]
+
+    def products(top, low, slot, left):
+        rows = slice(top, top + ROWS)
+        at = (rows, slice(low, low + 256))
+        put = (slot, rows, slice(left, left + 256))
+        half = 0.5 * v_gate[at].astype(jnp.float32)
         up = v_up[at].astype(jnp.float32)
         back = v_back[at].astype(jnp.float32)
+        tanh = jnp.tanh(half)
         plus = 1.0 + tanh
-        silu = 0.5 * v_gate[at].astype(jnp.float32) * plus
+        silu = half * plus
         made_hidden[put] = (silu * up).astype(jnp.bfloat16)
         made_up[put] = (back * silu).astype(jnp.bfloat16)
         made_gate[put] = (back * up * (plus + silu * (1.0 - tanh))).astype(jnp.bfloat16)
 
-    def add(total, values, base, first):
+    started = set()
+
+    def add(name, total, values, base):
         value = lax.dot_general(values, base, NT, preferred_element_type=jnp.float32)
-        if first:
+        if name in started:
+            total[...] += value
+        else:
             total[...] = value
-        else:
-            total[...] += value
-
-    def hidden_dot(step, which):
-        made = (made_gate, made_up, made_hidden)[which]
-        base = (v_gate_out, v_up_out, v_down_in)[which]
-        add(sums.at[which], made[step % 2], base[:, columns(step)], step == 0)
-
-    def model_dots(step):
-        at = columns(step)
-        add(sum_in, v_inputs[:, at], v_in[:, at], step == 0)
-        add(sums.at[3], v_out_grad[:, at], v_down_out[:, at], step == 0)
-
-    steps = hidden_steps + model_steps
-    for step in range(AHEAD):
-        for copy in copies[step]:
-            copy.start()
-    for block in range(steps):
-        if block + AHEAD < steps:
-            for copy in copies[block + AHEAD]:
-                copy.start()
-        for copy in copies[block]:
-            copy.wait()
-        groups = tokens // ROWS
-        for group in range(groups):
-            rows = slice(group * ROWS, (group + 1) * ROWS)
-            if 0 <= block - 2 < hidden_steps and group % (groups // 3) == 0:
-                hidden_dot(block - 2, group // (groups // 3))
-            if 0 <= block - 1 < hidden_steps:
-                products(block - 1, rows)
-            if block < hidden_steps:
-                squash(block, rows)
-        if block >= hidden_steps:
-            model_dots(block - hidden_steps)
+        started.add(name)
+
+    def hidden_dots(low, slot, left):
+        at = slice(low, low + DEPTH)
+        inner = (slot, slice(None), slice(left, left + DEPTH))
+        add("gate", sums.at[0], made_gate[inner], v_gate_out[:, at])
+        add("up", sums.at[1], made_up[inner], v_up_out[:, at])
+        add("hidden", sums.at[2], made_hidden[inner], v_down_in[:, at])
+
+    for each in copies:
+        each.start()
+    for index, at in enumerate(pieces):
+        for each in arrivals[index]:
+            each.wait()
+        if index == 1:
+            for each in hidden_bases:
+                each.wait()
+        length = at.stop - at.start
+        before = pieces[index - 1] if index > 0 else slice(0, 0)
+        for left in range(0, length, DEPTH):
+            for top in range(0, tokens, ROWS):
+                for inner in range(left, left + DEPTH, 256):
+                    products(top, at.start + inner, index % 2, inner)
+            if before.start + left < before.stop:
+                hidden_dots(before.start + left, (index - 1) % 2, left)
+    for each in for_inputs:
+        each.wait()
+    last = pieces[-1]
+    for left in range(0, last.stop - last.start, DEPTH):
+        hidden_dots(last.start + left, (len(pieces) - 1) % 2, left)
+    add("inputs", sum_in, v_inputs[...], v_in[...])
+    for each in for_out_grad:
+        each.wait()
+    for arrival, at in zip(for_halves, halves):
+        for each in arrival:
+            each.wait()
+        add("out_grad", sums.at[3], v_out_grad[:, at], v_down_out[:, at])
     out[:, : 2 * width] = sum_in[...]
     out[:, 2 * width : 4 * width] = jnp.concatenate([0.5 * sums[0], sums[1]], axis=1)
     out[:, 4 * width :] = jnp.concatenate([sums[2], sums[3]], axis=1)
@@ -144,9 +143,8 @@
     width = operands[5].shape[0]
     tokens, model = inputs.shape
     hidden = gate_pre.shape[1]
-    assert hidden % STEP == 0 and model % STEP == 0 and model >= 2 * STEP
-    assert tokens % (3 * ROWS) == 0
-    steps = 6 * (hidden // STEP) + 5 * (model // STEP)
+    assert hidden % PIECE == PIECE // 2 and model % (2 * DEPTH) == 0 and tokens % ROWS == 0
+    copies = 3 * (hidden // PIECE + 1) + 9
     bf16 = jnp.bfloat16
     return pl.pallas_call(
         project,
@@ -164,13 +162,12 @@
             pltpu.VMEM((width, hidden), bf16),
             pltpu.VMEM((width, hidden), bf16),
             pltpu.VMEM((width, model), bf16),
-            pltpu.VMEM((2, tokens, STEP), jnp.float32),
-            pltpu.VMEM((2, tokens, STEP), bf16),
-            pltpu.VMEM((2, tokens, STEP), bf16),
-            pltpu.VMEM((2, tokens, STEP), bf16),
+            pltpu.VMEM((2, tokens, PIECE), bf16),
+            pltpu.VMEM((2, tokens, PIECE), bf16),
+            pltpu.VMEM((2, tokens, PIECE), bf16),
             pltpu.VMEM((tokens, 2 * width), jnp.float32),
             pltpu.VMEM((4, tokens, width), jnp.float32),
-            pltpu.SemaphoreType.DMA((steps,)),
+            pltpu.SemaphoreType.DMA((copies,)),
         ],
         compiler_params=pltpu.CompilerParams(vmem_limit_bytes=427 * 2**17),
         cost_estimate=pl.CostEstimate(

time: 38.6 us -> 37 us (0.959)
  Pallas kernels: 12.7 us -> 11.2 us
    pallas_call x1, Pallas kernels: 11.8 us -> 10.2 us  [projections(): pl.pallas_call(project, out_shape=jax.ShapeDtypeStruct((tokens, 6 * width...]
  transfers between devices with their start and end apart: 2 -> 2, of which waited for: 1 -> 1; matrix products, arithmetic and copies ran while one was open for 0% -> 0% of each run, Pallas kernels for 32% -> 29%
where the time goes in v7:
time: 37 us; the launch traced here: 36.8 us
  blocking collectives  22.8 us (62%)
  Pallas kernels  11.2 us (30%)
  waiting for transfers between devices  1.52 us (4%)
  other arithmetic  0.61 us (2%)
  starting transfers between devices  0.58 us (2%)
    all_to_all x1, blocking collectives, body(): lax.all_to_all(blocks, 'dp', split_axis=0, concat_axis=0, tiled=True)  13.9 us
    pallas_call x1, Pallas kernels, projections(): pl.pallas_call(project, out_shape=jax.ShapeDtypeStruct((tokens, 6 * width...  10.2 us
    all_to_all x1, blocking collectives, body(): lax.all_to_all(scores, 'dp', split_axis=0, concat_axis=0, tiled=True)  8.94 us
    ppermute x1, waiting for transfers between devices, body(): other = lax.ppermute(own, 'mp', swap)  1.52 us
  transfers between devices with their start and end apart: 2, of which 1 were waited for; matrix products, arithmetic and copies ran while one was open for 0% of the time, Pallas kernels for 29%

profile of v7, /device:TPU:0, one launch (start us, length us, event | category | flops | bytes accessed | tf_op | source)
XLA Modules:
  0.0 36.8 jit_solution(3244466191778695640)
XLA Ops:
  0.0 0.5 %collective-permute-start = (bf16[512,768]{1,0:T(8,128)(2,1)}, bf16[512,768]{1,0:T(8,128)(2,1)S(1)}, u32[]{:S(2)}, u32[]{:S(2)}) collective-permute-start(bf16[512,768]{1,0:T(8,128)(2,1)} %queries.1), channel_id=1, source_target_pairs={{0,1},{1,0},{2,3},{3,2},{4,5},{5,4},{6,7},{7,6},{8,9},{9,8},{10,11... | collective-permute-start | bytes 2359304 | tf_op jit(solution)/shard_map/ppermute | solution.py:289
  0.5 0.0 copy-start.1
  0.5 0.0 copy-start
  0.5 10.2 %project.1.own = f32[192,384]{1,0:T(8,128)S(1)} custom-call(bf16[192,4096]{1,0:T(8,128)(2,1)} %inputs.1, bf16[192,7168]{1,0:T(8,128)(2,1)} %gate_pre.1, bf16[192,7168]{1,0:T(8,128)(2,1)} %up_pre.1, bf16[192,7168]{1,0:T(8,128)(2,1)} %hidden_grad.1, bf16[192,4096]{1,0:T(8,128)(2,1)} %out_grad.1, bf16[64,4096]{1,0:T(8,128)(2,1)} %bitcast.14, ...), custom_call_target="tpu_custom_call" | custom-call | flops 830472192 | bytes 11403264 | tf_op jit(solution)/shard_map/project/pallas_call | solution.py:149
  10.6 0.1 collective-permute-start.1
  10.8 1.5 %collective-permute-done.1.other = f32[192,384]{1,0:T(8,128)S(1)} collective-permute-done((f32[192,384]{1,0:T(8,128)S(1)}, f32[192,384]{1,0:T(8,128)S(1)}, u32[]{:S(2)}, u32[]{:S(2)}) %collective-permute-start.1) | collective-permute-done | bytes 294944 | tf_op jit(solution)/shard_map/ppermute | solution.py:292
  12.3 0.0 copy-done.1
  12.3 0.5 %outer.1 = f32[8,24,128]{2,1,0:T(8,128)S(1)} custom-call(f32[192,384]{1,0:T(8,128)S(1)} %project.1.own, f32[192,384]{1,0:T(8,128)S(1)} %collective-permute-done.1.other, s32[1,192]{1,0:T(1,128)S(1)} %bitcast.10), custom_call_target="tpu_custom_call" | custom-call | tf_op jit(solution)/shard_map/outer/pallas_call | solution.py:223
  12.8 13.9 %all_to_all.10.received = f32[8,24,128]{2,1,0:T(8,128)S(1)} all-to-all(f32[8,24,128]{2,1,0:T(8,128)S(1)} %outer.1), channel_id=1, replica_groups=mesh['parts'=2,'dp'=8,'mp'=2] {'dp'}, dimensions={0} | all-to-all | bytes 196608 | tf_op jit(solution)/shard_map/all_to_all | solution.py:294
  26.7 0.0 collective-permute-done.swapped
  26.7 0.0 copy-done
  26.7 0.5 %score.1 = f32[8,512]{1,0:T(8,128)S(1)} custom-call(bf16[512,768]{1,0:T(8,128)(2,1)S(1)} %copy-done, bf16[512,768]{1,0:T(8,128)(2,1)S(1)} %collective-permute-done.swapped, f32[8,24,128]{2,1,0:T(8,128)S(1)} %all_to_all.10.received), custom_call_target="tpu_custom_call" | custom-call | tf_op jit(solution)/shard_map/score/pallas_call | solution.py:261
  27.2 8.9 %all_to_all.11 = f32[8,1,512]{2,1,0:T(1,128)S(1)} all-to-all(f32[8,1,512]{2,1,0:T(1,128)S(1)} %copy.14), channel_id=1, replica_groups=mesh['parts'=2,'dp'=8,'mp'=2] {'dp'}, dimensions={0} | all-to-all | bytes 32768 | tf_op jit(solution)/shard_map/all_to_all | solution.py:296
  36.2 0.6 %reduce_sum.11 = f32[512]{0:T(512)} reduce(f32[8,1,512]{2,1,0:T(1,128)S(1)} %all_to_all.11, f32[]{:T(128)} %constant.0.clone.1), dimensions={0,1}, to_apply=%region_0.0 | reduce | flops 3584 | bytes 18436 | tf_op jit(solution)/shard_map/reduce_sum | solution.py:297
  (1 shorter events, 0.0 us)
Async XLA Ops:
  0.0 26.7 %collective-permute-start = (bf16[512,768]{1,0:T(8,128)(2,1)}, bf16[512,768]{1,0:T(8,128)(2,1)S(1)}, u32[]{:S(2)}, u32[]{:S(2)}) collective-permute-start(bf16[512,768]{1,0:T(8,128)(2,1)} %queries.1), channel_id=1, source_target_pairs={{0,1},{1,0},{2,3},{3,2},{4,5},{5,4},{6,7},{7,6},{8,9},{9,8},{10,11... | collective-permute-start | bytes 2359304 | tf_op jit(solution)/shard_map/ppermute | solution.py:289
  0.5 11.8 %copy-start.1 = (s32[192]{0:T(256)S(1)}, s32[192]{0:T(256)}, u32[]{:S(2)}) copy-start(s32[192]{0:T(256)} %param.18) | copy-start | bytes 2308
  0.5 26.2 %copy-start = (bf16[512,768]{1,0:T(8,128)(2,1)S(1)}, bf16[512,768]{1,0:T(8,128)(2,1)}, u32[]{:S(2)}) copy-start(bf16[512,768]{1,0:T(8,128)(2,1)} %queries.1) | copy-start | bytes 2359300
  10.6 1.6 %collective-permute-start.1 = (f32[192,384]{1,0:T(8,128)S(1)}, f32[192,384]{1,0:T(8,128)S(1)}, u32[]{:S(2)}, u32[]{:S(2)}) collective-permute-start(f32[192,384]{1,0:T(8,128)S(1)} %project.1.own), channel_id=1, source_target_pairs={{0,1},{1,0},{2,3},{3,2},{4,5},{5,4},{6,7},{7,6},{8,9},{9,8},{10,11... | collective-permute-start | bytes 884744 | tf_op jit(solution)/shard_map/ppermute | solution.py:292

commit v8 on v5

--- a/solution.py
+++ b/solution.py
@@ -11,7 +11,7 @@
 STEP = 1024
 PART = 512
 ROWS = 16
-AHEAD = 3
+AHEAD = 2
 
 
 def project(
@@ -86,11 +86,13 @@
                 gate = v_gate[at].astype(jnp.float32)
                 up = v_up[at].astype(jnp.float32)
                 back = v_back[at].astype(jnp.float32)
-                sig = 0.5 * jnp.tanh(0.5 * gate) + 0.5
-                silu = gate * sig
+                half = 0.5 * gate
+                tanh = jnp.tanh(half)
+                plus = 1.0 + tanh
+                silu = half * plus
                 made_hidden[(target,) + put] = (silu * up).astype(jnp.bfloat16)
                 made_up[(target,) + put] = (back * silu).astype(jnp.bfloat16)
-                slope = sig + silu * (1.0 - sig)
+                slope = plus + silu * (1.0 - tanh)
                 made_gate[(target,) + put] = (back * up * slope).astype(jnp.bfloat16)
 
     def add(total, values, base, first):
@@ -132,7 +134,7 @@
     for part in range(STEP // PART):
         hidden_dots(hidden_steps - 1, part)
     out[:, : 2 * width] = sum_in[...]
-    out[:, 2 * width : 4 * width] = jnp.concatenate([sums[0], sums[1]], axis=1)
+    out[:, 2 * width : 4 * width] = jnp.concatenate([0.5 * sums[0], sums[1]], axis=1)
     out[:, 4 * width :] = jnp.concatenate([sums[2], sums[3]], axis=1)
 
 

time: 35.7 us -> 35.7 us (level)
  transfers between devices with their start and end apart: 2 -> 2, of which waited for: 1 -> 1; matrix products, arithmetic and copies ran while one was open for 0% -> 0% of each run, Pallas kernels for 26% -> 27%
where the time goes in v8:
time: 35.7 us; the launch traced here: 35.5 us
  blocking collectives  22.9 us (64%)
  Pallas kernels  9.92 us (28%)
  waiting for transfers between devices  1.53 us (4%)
  other arithmetic  0.61 us (2%)
  starting transfers between devices  0.57 us (2%)
    all_to_all x1, blocking collectives, body(): lax.all_to_all(blocks, 'dp', split_axis=0, concat_axis=0, tiled=True)  13.9 us
    all_to_all x1, blocking collectives, body(): lax.all_to_all(scores, 'dp', split_axis=0, concat_axis=0, tiled=True)  8.94 us
    pallas_call x1, Pallas kernels, projections(): pl.pallas_call(project, out_shape=jax.ShapeDtypeStruct((tokens, 6 * width...  8.94 us
    ppermute x1, waiting for transfers between devices, body(): other = lax.ppermute(own, 'mp', swap)  1.53 us
  transfers between devices with their start and end apart: 2, of which 1 were waited for; matrix products, arithmetic and copies ran while one was open for 0% of the time, Pallas kernels for 27%

profile of v8, /device:TPU:0, one launch (start us, length us, event | category | flops | bytes accessed | tf_op | source)
XLA Modules:
  0.0 35.5 jit_solution(15916820597567402765)
XLA Ops:
  0.0 0.5 %collective-permute-start = (bf16[512,768]{1,0:T(8,128)(2,1)}, bf16[512,768]{1,0:T(8,128)(2,1)S(1)}, u32[]{:S(2)}, u32[]{:S(2)}) collective-permute-start(bf16[512,768]{1,0:T(8,128)(2,1)} %queries.1), channel_id=1, source_target_pairs={{0,1},{1,0},{2,3},{3,2},{4,5},{5,4},{6,7},{7,6},{8,9},{9,8},{10,11... | collective-permute-start | bytes 2359304 | tf_op jit(solution)/shard_map/ppermute | solution.py:290
  0.5 0.0 copy-start.1
  0.5 0.0 copy-start
  0.5 8.9 %project.1.own = f32[192,384]{1,0:T(8,128)S(1)} custom-call(bf16[192,4096]{1,0:T(8,128)(2,1)} %inputs.1, bf16[192,7168]{1,0:T(8,128)(2,1)} %gate_pre.1, bf16[192,7168]{1,0:T(8,128)(2,1)} %up_pre.1, bf16[192,7168]{1,0:T(8,128)(2,1)} %hidden_grad.1, bf16[192,4096]{1,0:T(8,128)(2,1)} %out_grad.1, bf16[64,4096]{1,0:T(8,128)(2,1)} %bitcast.14, ...), custom_call_target="tpu_custom_call" | custom-call | flops 830472192 | bytes 11403264 | tf_op jit(solution)/shard_map/project/pallas_call | solution.py:150
  9.4 0.1 collective-permute-start.1
  9.5 1.5 %collective-permute-done.1.other = f32[192,384]{1,0:T(8,128)S(1)} collective-permute-done((f32[192,384]{1,0:T(8,128)S(1)}, f32[192,384]{1,0:T(8,128)S(1)}, u32[]{:S(2)}, u32[]{:S(2)}) %collective-permute-start.1) | collective-permute-done | bytes 294944 | tf_op jit(solution)/shard_map/ppermute | solution.py:293
  11.1 0.0 copy-done.1
  11.1 0.5 %outer.1 = f32[8,24,128]{2,1,0:T(8,128)S(1)} custom-call(f32[192,384]{1,0:T(8,128)S(1)} %project.1.own, f32[192,384]{1,0:T(8,128)S(1)} %collective-permute-done.1.other, s32[1,192]{1,0:T(1,128)S(1)} %bitcast.10), custom_call_target="tpu_custom_call" | custom-call | tf_op jit(solution)/shard_map/outer/pallas_call | solution.py:224
  11.5 13.9 %all_to_all.10.received = f32[8,24,128]{2,1,0:T(8,128)S(1)} all-to-all(f32[8,24,128]{2,1,0:T(8,128)S(1)} %outer.1), channel_id=1, replica_groups=mesh['parts'=2,'dp'=8,'mp'=2] {'dp'}, dimensions={0} | all-to-all | bytes 196608 | tf_op jit(solution)/shard_map/all_to_all | solution.py:295
  25.4 0.0 collective-permute-done.swapped
  25.4 0.0 copy-done
  25.4 0.5 %score.1 = f32[8,512]{1,0:T(8,128)S(1)} custom-call(bf16[512,768]{1,0:T(8,128)(2,1)S(1)} %copy-done, bf16[512,768]{1,0:T(8,128)(2,1)S(1)} %collective-permute-done.swapped, f32[8,24,128]{2,1,0:T(8,128)S(1)} %all_to_all.10.received), custom_call_target="tpu_custom_call" | custom-call | tf_op jit(solution)/shard_map/score/pallas_call | solution.py:262
  26.0 8.9 %all_to_all.11 = f32[8,1,512]{2,1,0:T(1,128)S(1)} all-to-all(f32[8,1,512]{2,1,0:T(1,128)S(1)} %copy.14), channel_id=1, replica_groups=mesh['parts'=2,'dp'=8,'mp'=2] {'dp'}, dimensions={0} | all-to-all | bytes 32768 | tf_op jit(solution)/shard_map/all_to_all | solution.py:297
  34.9 0.6 %reduce_sum.11 = f32[512]{0:T(512)} reduce(f32[8,1,512]{2,1,0:T(1,128)S(1)} %all_to_all.11, f32[]{:T(128)} %constant.0.clone.1), dimensions={0,1}, to_apply=%region_0.0 | reduce | flops 3584 | bytes 18436 | tf_op jit(solution)/shard_map/reduce_sum | solution.py:298
  (1 shorter events, 0.0 us)
Async XLA Ops:
  0.0 25.4 %collective-permute-start = (bf16[512,768]{1,0:T(8,128)(2,1)}, bf16[512,768]{1,0:T(8,128)(2,1)S(1)}, u32[]{:S(2)}, u32[]{:S(2)}) collective-permute-start(bf16[512,768]{1,0:T(8,128)(2,1)} %queries.1), channel_id=1, source_target_pairs={{0,1},{1,0},{2,3},{3,2},{4,5},{5,4},{6,7},{7,6},{8,9},{9,8},{10,11... | collective-permute-start | bytes 2359304 | tf_op jit(solution)/shard_map/ppermute | solution.py:290
  0.5 10.6 %copy-start.1 = (s32[192]{0:T(256)S(1)}, s32[192]{0:T(256)}, u32[]{:S(2)}) copy-start(s32[192]{0:T(256)} %param.18) | copy-start | bytes 2308
  0.5 25.0 %copy-start = (bf16[512,768]{1,0:T(8,128)(2,1)S(1)}, bf16[512,768]{1,0:T(8,128)(2,1)}, u32[]{:S(2)}) copy-start(bf16[512,768]{1,0:T(8,128)(2,1)} %queries.1) | copy-start | bytes 2359300
  9.4 1.6 %collective-permute-start.1 = (f32[192,384]{1,0:T(8,128)S(1)}, f32[192,384]{1,0:T(8,128)S(1)}, u32[]{:S(2)}, u32[]{:S(2)}) collective-permute-start(f32[192,384]{1,0:T(8,128)S(1)} %project.1.own), channel_id=1, source_target_pairs={{0,1},{1,0},{2,3},{3,2},{4,5},{5,4},{6,7},{7,6},{8,9},{9,8},{10,11... | collective-permute-start | bytes 884744 | tf_op jit(solution)/shard_map/ppermute | solution.py:293

commit v9 on v8

--- a/solution.py
+++ b/solution.py
@@ -9,7 +9,7 @@
 
 NT = (((1,), (1,)), ((), ()))
 STEP = 1024
-PART = 512
+PART = 1024
 ROWS = 16
 AHEAD = 2
 

time: 35.7 us -> 35.8 us (level)
  no operation moved by 1% of the time
where the time goes in v9:
time: 35.8 us; the launch traced here: 35.6 us
  blocking collectives  22.8 us (64%)
  Pallas kernels  9.95 us (28%)
  waiting for transfers between devices  1.52 us (4%)
  other arithmetic  0.61 us (2%)
  starting transfers between devices  0.59 us (2%)
    all_to_all x1, blocking collectives, body(): lax.all_to_all(blocks, 'dp', split_axis=0, concat_axis=0, tiled=True)  13.9 us
    pallas_call x1, Pallas kernels, projections(): pl.pallas_call(project, out_shape=jax.ShapeDtypeStruct((tokens, 6 * width...  8.97 us
    all_to_all x1, blocking collectives, body(): lax.all_to_all(scores, 'dp', split_axis=0, concat_axis=0, tiled=True)  8.94 us
    ppermute x1, waiting for transfers between devices, body(): other = lax.ppermute(own, 'mp', swap)  1.51 us
  transfers between devices with their start and end apart: 2, of which 1 were waited for; matrix products, arithmetic and copies ran while one was open for 0% of the time, Pallas kernels for 27%

profile of v9, /device:TPU:0, one launch (start us, length us, event | category | flops | bytes accessed | tf_op | source)
XLA Modules:
  0.0 35.6 jit_solution(4998893629180757086)
XLA Ops:
  0.0 0.5 %collective-permute-start = (bf16[512,768]{1,0:T(8,128)(2,1)}, bf16[512,768]{1,0:T(8,128)(2,1)S(1)}, u32[]{:S(2)}, u32[]{:S(2)}) collective-permute-start(bf16[512,768]{1,0:T(8,128)(2,1)} %queries.1), channel_id=1, source_target_pairs={{0,1},{1,0},{2,3},{3,2},{4,5},{5,4},{6,7},{7,6},{8,9},{9,8},{10,11... | collective-permute-start | bytes 2359304 | tf_op jit(solution)/shard_map/ppermute | solution.py:290
  0.5 0.0 copy-start.1
  0.5 0.0 copy-start
  0.5 9.0 %project.1.own = f32[192,384]{1,0:T(8,128)S(1)} custom-call(bf16[192,4096]{1,0:T(8,128)(2,1)} %inputs.1, bf16[192,7168]{1,0:T(8,128)(2,1)} %gate_pre.1, bf16[192,7168]{1,0:T(8,128)(2,1)} %up_pre.1, bf16[192,7168]{1,0:T(8,128)(2,1)} %hidden_grad.1, bf16[192,4096]{1,0:T(8,128)(2,1)} %out_grad.1, bf16[64,4096]{1,0:T(8,128)(2,1)} %bitcast.14, ...), custom_call_target="tpu_custom_call" | custom-call | flops 830472192 | bytes 11403264 | tf_op jit(solution)/shard_map/project/pallas_call | solution.py:150
  9.4 0.1 collective-permute-start.1
  9.6 1.5 %collective-permute-done.1.other = f32[192,384]{1,0:T(8,128)S(1)} collective-permute-done((f32[192,384]{1,0:T(8,128)S(1)}, f32[192,384]{1,0:T(8,128)S(1)}, u32[]{:S(2)}, u32[]{:S(2)}) %collective-permute-start.1) | collective-permute-done | bytes 294944 | tf_op jit(solution)/shard_map/ppermute | solution.py:293
  11.1 0.0 copy-done.1
  11.1 0.5 %outer.1 = f32[8,24,128]{2,1,0:T(8,128)S(1)} custom-call(f32[192,384]{1,0:T(8,128)S(1)} %project.1.own, f32[192,384]{1,0:T(8,128)S(1)} %collective-permute-done.1.other, s32[1,192]{1,0:T(1,128)S(1)} %bitcast.10), custom_call_target="tpu_custom_call" | custom-call | tf_op jit(solution)/shard_map/outer/pallas_call | solution.py:224
  11.6 13.9 %all_to_all.10.received = f32[8,24,128]{2,1,0:T(8,128)S(1)} all-to-all(f32[8,24,128]{2,1,0:T(8,128)S(1)} %outer.1), channel_id=1, replica_groups=mesh['parts'=2,'dp'=8,'mp'=2] {'dp'}, dimensions={0} | all-to-all | bytes 196608 | tf_op jit(solution)/shard_map/all_to_all | solution.py:295
  25.5 0.0 collective-permute-done.swapped
  25.5 0.0 copy-done
  25.5 0.5 %score.1 = f32[8,512]{1,0:T(8,128)S(1)} custom-call(bf16[512,768]{1,0:T(8,128)(2,1)S(1)} %copy-done, bf16[512,768]{1,0:T(8,128)(2,1)S(1)} %collective-permute-done.swapped, f32[8,24,128]{2,1,0:T(8,128)S(1)} %all_to_all.10.received), custom_call_target="tpu_custom_call" | custom-call | tf_op jit(solution)/shard_map/score/pallas_call | solution.py:262
  26.0 8.9 %all_to_all.11 = f32[8,1,512]{2,1,0:T(1,128)S(1)} all-to-all(f32[8,1,512]{2,1,0:T(1,128)S(1)} %copy.14), channel_id=1, replica_groups=mesh['parts'=2,'dp'=8,'mp'=2] {'dp'}, dimensions={0} | all-to-all | bytes 32768 | tf_op jit(solution)/shard_map/all_to_all | solution.py:297
  35.0 0.6 %reduce_sum.11 = f32[512]{0:T(512)} reduce(f32[8,1,512]{2,1,0:T(1,128)S(1)} %all_to_all.11, f32[]{:T(128)} %constant.0.clone.1), dimensions={0,1}, to_apply=%region_0.0 | reduce | flops 3584 | bytes 18436 | tf_op jit(solution)/shard_map/reduce_sum | solution.py:298
  (1 shorter events, 0.0 us)
Async XLA Ops:
  0.0 25.5 %collective-permute-start = (bf16[512,768]{1,0:T(8,128)(2,1)}, bf16[512,768]{1,0:T(8,128)(2,1)S(1)}, u32[]{:S(2)}, u32[]{:S(2)}) collective-permute-start(bf16[512,768]{1,0:T(8,128)(2,1)} %queries.1), channel_id=1, source_target_pairs={{0,1},{1,0},{2,3},{3,2},{4,5},{5,4},{6,7},{7,6},{8,9},{9,8},{10,11... | collective-permute-start | bytes 2359304 | tf_op jit(solution)/shard_map/ppermute | solution.py:290
  0.5 10.6 %copy-start.1 = (s32[192]{0:T(256)S(1)}, s32[192]{0:T(256)}, u32[]{:S(2)}) copy-start(s32[192]{0:T(256)} %param.18) | copy-start | bytes 2308
  0.5 25.0 %copy-start = (bf16[512,768]{1,0:T(8,128)(2,1)S(1)}, bf16[512,768]{1,0:T(8,128)(2,1)}, u32[]{:S(2)}) copy-start(bf16[512,768]{1,0:T(8,128)(2,1)} %queries.1) | copy-start | bytes 2359300
  9.4 1.6 %collective-permute-start.1 = (f32[192,384]{1,0:T(8,128)S(1)}, f32[192,384]{1,0:T(8,128)S(1)}, u32[]{:S(2)}, u32[]{:S(2)}) collective-permute-start(f32[192,384]{1,0:T(8,128)S(1)} %project.1.own), channel_id=1, source_target_pairs={{0,1},{1,0},{2,3},{3,2},{4,5},{5,4},{6,7},{7,6},{8,9},{9,8},{10,11... | collective-permute-start | bytes 884744 | tf_op jit(solution)/shard_map/ppermute | solution.py:293

commit v10 on v9

--- a/solution.py
+++ b/solution.py
@@ -9,7 +9,7 @@
 
 NT = (((1,), (1,)), ((), ()))
 STEP = 1024
-PART = 1024
+TILE = 256
 ROWS = 16
 AHEAD = 2
 
@@ -37,9 +37,6 @@
     v_up_out,
     v_down_in,
     v_down_out,
-    made_hidden,
-    made_up,
-    made_gate,
     sum_in,
     sums,
     sems,
@@ -77,23 +74,20 @@
             ]
         plan(pairs)
 
-    def elementwise(step, part):
-        target = step % 2
+    def products(step, left):
+        parts = []
         for top in range(0, tokens, ROWS):
-            for left in range(part * PART, (part + 1) * PART, 256):
-                at = (slice(top, top + ROWS), slice(step * STEP + left, step * STEP + left + 256))
-                put = (slice(top, top + ROWS), slice(left, left + 256))
-                gate = v_gate[at].astype(jnp.float32)
-                up = v_up[at].astype(jnp.float32)
-                back = v_back[at].astype(jnp.float32)
-                half = 0.5 * gate
-                tanh = jnp.tanh(half)
-                plus = 1.0 + tanh
-                silu = half * plus
-                made_hidden[(target,) + put] = (silu * up).astype(jnp.bfloat16)
-                made_up[(target,) + put] = (back * silu).astype(jnp.bfloat16)
-                slope = plus + silu * (1.0 - tanh)
-                made_gate[(target,) + put] = (back * up * slope).astype(jnp.bfloat16)
+            at = (slice(top, top + ROWS), slice(step * STEP + left, step * STEP + left + TILE))
+            half = 0.5 * v_gate[at].astype(jnp.float32)
+            up = v_up[at].astype(jnp.float32)
+            back = v_back[at].astype(jnp.float32)
+            tanh = jnp.tanh(half)
+            plus = 1.0 + tanh
+            silu = half * plus
+            slope = plus + silu * (1.0 - tanh)
+            values = (back * up * slope, back * silu, silu * up)
+            parts.append([value.astype(jnp.bfloat16) for value in values])
+        return [jnp.concatenate(column, axis=0) for column in zip(*parts)]
 
     def add(total, values, base, first):
         value = lax.dot_general(values, base, NT, preferred_element_type=jnp.float32)
@@ -102,19 +96,16 @@
         else:
             total[...] += value
 
-    def hidden_dots(step, part):
-        at = slice(step * STEP + part * PART, step * STEP + (part + 1) * PART)
-        inner = (step % 2, slice(None), slice(part * PART, (part + 1) * PART))
-        first = step == 0 and part == 0
-        add(sums.at[0], made_gate[inner], v_gate_out[:, at], first)
-        add(sums.at[1], made_up[inner], v_up_out[:, at], first)
-        add(sums.at[2], made_hidden[inner], v_down_in[:, at], first)
-
-    def model_dots(step, part):
-        at = slice(step * STEP + part * PART, step * STEP + (part + 1) * PART)
-        first = step == 0 and part == 0
-        add(sum_in, v_inputs[:, at], v_in[:, at], first)
-        add(sums.at[3], v_out_grad[:, at], v_down_out[:, at], first)
+    def hidden_dots(step, left):
+        at = slice(step * STEP + left, step * STEP + left + TILE)
+        bases = (v_gate_out, v_up_out, v_down_in)
+        for which, value in enumerate(products(step, left)):
+            add(sums.at[which], value, bases[which][:, at], step == 0 and left == 0)
+
+    def model_dots(step):
+        at = slice(step * STEP, (step + 1) * STEP)
+        add(sum_in, v_inputs[:, at], v_in[:, at], step == 0)
+        add(sums.at[3], v_out_grad[:, at], v_down_out[:, at], step == 0)
 
     for step in range(min(AHEAD, hidden_steps)):
         for copy in copies[step]:
@@ -125,14 +116,10 @@
                 copy.start()
         for copy in copies[step]:
             copy.wait()
-        for part in range(STEP // PART):
-            elementwise(step, part)
-            if step >= 1:
-                hidden_dots(step - 1, part)
-            if step < model_steps:
-                model_dots(step, part)
-    for part in range(STEP // PART):
-        hidden_dots(hidden_steps - 1, part)
+        for left in range(0, STEP, TILE):
+            hidden_dots(step, left)
+        if step < model_steps:
+            model_dots(step)
     out[:, : 2 * width] = sum_in[...]
     out[:, 2 * width : 4 * width] = jnp.concatenate([0.5 * sums[0], sums[1]], axis=1)
     out[:, 4 * width :] = jnp.concatenate([sums[2], sums[3]], axis=1)
@@ -163,9 +150,6 @@
             pltpu.VMEM((width, hidden), bf16),
             pltpu.VMEM((width, hidden), bf16),
             pltpu.VMEM((width, model), bf16),
-            pltpu.VMEM((2, tokens, STEP), bf16),
-            pltpu.VMEM((2, tokens, STEP), bf16),
-            pltpu.VMEM((2, tokens, STEP), bf16),
             pltpu.VMEM((tokens, 2 * width), jnp.float32),
             pltpu.VMEM((4, tokens, width), jnp.float32),
             pltpu.SemaphoreType.DMA((steps,)),

time: 35.8 us -> 34.8 us (0.972)
  Pallas kernels: 9.95 us -> 8.96 us
    pallas_call x1, Pallas kernels: 8.97 us -> 7.98 us  [projections(): pl.pallas_call(project, out_shape=jax.ShapeDtypeStruct((tokens, 6 * width...]
  transfers between devices with their start and end apart: 2 -> 2, of which waited for: 1 -> 1; matrix products, arithmetic and copies ran while one was open for 0% -> 0% of each run, Pallas kernels for 27% -> 24%
where the time goes in v10:
time: 34.8 us; the launch traced here: 34.6 us
  blocking collectives  22.8 us (66%)
  Pallas kernels  8.96 us (26%)
  waiting for transfers between devices  1.53 us (4%)
  other arithmetic  0.61 us (2%)
  starting transfers between devices  0.57 us (2%)
    all_to_all x1, blocking collectives, body(): lax.all_to_all(blocks, 'dp', split_axis=0, concat_axis=0, tiled=True)  13.9 us
    all_to_all x1, blocking collectives, body(): lax.all_to_all(scores, 'dp', split_axis=0, concat_axis=0, tiled=True)  8.94 us
    pallas_call x1, Pallas kernels, projections(): pl.pallas_call(project, out_shape=jax.ShapeDtypeStruct((tokens, 6 * width...  7.98 us
    ppermute x1, waiting for transfers between devices, body(): other = lax.ppermute(own, 'mp', swap)  1.53 us
  transfers between devices with their start and end apart: 2, of which 1 were waited for; matrix products, arithmetic and copies ran while one was open for 0% of the time, Pallas kernels for 24%

profile of v10, /device:TPU:0, one launch (start us, length us, event | category | flops | bytes accessed | tf_op | source)
XLA Modules:
  0.0 34.6 jit_solution(7185532120378457812)
XLA Ops:
  0.0 0.5 %collective-permute-start = (bf16[512,768]{1,0:T(8,128)(2,1)}, bf16[512,768]{1,0:T(8,128)(2,1)S(1)}, u32[]{:S(2)}, u32[]{:S(2)}) collective-permute-start(bf16[512,768]{1,0:T(8,128)(2,1)} %queries.1), channel_id=1, source_target_pairs={{0,1},{1,0},{2,3},{3,2},{4,5},{5,4},{6,7},{7,6},{8,9},{9,8},{10,11... | collective-permute-start | bytes 2359304 | tf_op jit(solution)/shard_map/ppermute | solution.py:274
  0.5 0.0 copy-start.1
  0.5 0.0 copy-start
  0.5 8.0 %project.1.own = f32[192,384]{1,0:T(8,128)S(1)} custom-call(bf16[192,4096]{1,0:T(8,128)(2,1)} %inputs.1, bf16[192,7168]{1,0:T(8,128)(2,1)} %gate_pre.1, bf16[192,7168]{1,0:T(8,128)(2,1)} %up_pre.1, bf16[192,7168]{1,0:T(8,128)(2,1)} %hidden_grad.1, bf16[192,4096]{1,0:T(8,128)(2,1)} %out_grad.1, bf16[64,4096]{1,0:T(8,128)(2,1)} %bitcast.14, ...), custom_call_target="tpu_custom_call" | custom-call | flops 830472192 | bytes 11403264 | tf_op jit(solution)/shard_map/project/pallas_call | solution.py:137
  8.4 0.1 collective-permute-start.1
  8.6 1.5 %collective-permute-done.1.other = f32[192,384]{1,0:T(8,128)S(1)} collective-permute-done((f32[192,384]{1,0:T(8,128)S(1)}, f32[192,384]{1,0:T(8,128)S(1)}, u32[]{:S(2)}, u32[]{:S(2)}) %collective-permute-start.1) | collective-permute-done | bytes 294944 | tf_op jit(solution)/shard_map/ppermute | solution.py:277
  10.1 0.0 copy-done.1
  10.1 0.5 %outer.1 = f32[8,24,128]{2,1,0:T(8,128)S(1)} custom-call(f32[192,384]{1,0:T(8,128)S(1)} %project.1.own, f32[192,384]{1,0:T(8,128)S(1)} %collective-permute-done.1.other, s32[1,192]{1,0:T(1,128)S(1)} %bitcast.10), custom_call_target="tpu_custom_call" | custom-call | tf_op jit(solution)/shard_map/outer/pallas_call | solution.py:208
  10.6 13.9 %all_to_all.10.received = f32[8,24,128]{2,1,0:T(8,128)S(1)} all-to-all(f32[8,24,128]{2,1,0:T(8,128)S(1)} %outer.1), channel_id=1, replica_groups=mesh['parts'=2,'dp'=8,'mp'=2] {'dp'}, dimensions={0} | all-to-all | bytes 196608 | tf_op jit(solution)/shard_map/all_to_all | solution.py:279
  24.5 0.0 collective-permute-done.swapped
  24.5 0.0 copy-done
  24.5 0.5 %score.1 = f32[8,512]{1,0:T(8,128)S(1)} custom-call(bf16[512,768]{1,0:T(8,128)(2,1)S(1)} %copy-done, bf16[512,768]{1,0:T(8,128)(2,1)S(1)} %collective-permute-done.swapped, f32[8,24,128]{2,1,0:T(8,128)S(1)} %all_to_all.10.received), custom_call_target="tpu_custom_call" | custom-call | tf_op jit(solution)/shard_map/score/pallas_call | solution.py:246
  25.0 8.9 %all_to_all.11 = f32[8,1,512]{2,1,0:T(1,128)S(1)} all-to-all(f32[8,1,512]{2,1,0:T(1,128)S(1)} %copy.14), channel_id=1, replica_groups=mesh['parts'=2,'dp'=8,'mp'=2] {'dp'}, dimensions={0} | all-to-all | bytes 32768 | tf_op jit(solution)/shard_map/all_to_all | solution.py:281
  34.0 0.6 %reduce_sum.11 = f32[512]{0:T(512)} reduce(f32[8,1,512]{2,1,0:T(1,128)S(1)} %all_to_all.11, f32[]{:T(128)} %constant.0.clone.1), dimensions={0,1}, to_apply=%region_0.0 | reduce | flops 3584 | bytes 18436 | tf_op jit(solution)/shard_map/reduce_sum | solution.py:282
  (1 shorter events, 0.0 us)
Async XLA Ops:
  0.0 24.5 %collective-permute-start = (bf16[512,768]{1,0:T(8,128)(2,1)}, bf16[512,768]{1,0:T(8,128)(2,1)S(1)}, u32[]{:S(2)}, u32[]{:S(2)}) collective-permute-start(bf16[512,768]{1,0:T(8,128)(2,1)} %queries.1), channel_id=1, source_target_pairs={{0,1},{1,0},{2,3},{3,2},{4,5},{5,4},{6,7},{7,6},{8,9},{9,8},{10,11... | collective-permute-start | bytes 2359304 | tf_op jit(solution)/shard_map/ppermute | solution.py:274
  0.5 9.6 %copy-start.1 = (s32[192]{0:T(256)S(1)}, s32[192]{0:T(256)}, u32[]{:S(2)}) copy-start(s32[192]{0:T(256)} %param.18) | copy-start | bytes 2308
  0.5 24.0 %copy-start = (bf16[512,768]{1,0:T(8,128)(2,1)S(1)}, bf16[512,768]{1,0:T(8,128)(2,1)}, u32[]{:S(2)}) copy-start(bf16[512,768]{1,0:T(8,128)(2,1)} %queries.1) | copy-start | bytes 2359300
  8.4 1.6 %collective-permute-start.1 = (f32[192,384]{1,0:T(8,128)S(1)}, f32[192,384]{1,0:T(8,128)S(1)}, u32[]{:S(2)}, u32[]{:S(2)}) collective-permute-start(f32[192,384]{1,0:T(8,128)S(1)} %project.1.own), channel_id=1, source_target_pairs={{0,1},{1,0},{2,3},{3,2},{4,5},{5,4},{6,7},{7,6},{8,9},{9,8},{10,11... | collective-permute-start | bytes 884744 | tf_op jit(solution)/shard_map/ppermute | solution.py:277

commit v11 on v10

--- a/solution.py
+++ b/solution.py
@@ -11,7 +11,7 @@
 STEP = 1024
 TILE = 256
 ROWS = 16
-AHEAD = 2
+AHEAD = 3
 
 
 def project(
@@ -27,6 +27,7 @@
     down_in,
     down_out,
     out,
+    rounded,
     v_inputs,
     v_gate,
     v_up,
@@ -43,28 +44,26 @@
 ):
     width = gate_in.shape[0]
     tokens = inputs.shape[0]
-    hidden_steps = gate_pre.shape[1] // STEP
-    model_steps = inputs.shape[1] // STEP
+    hidden, model = gate_pre.shape[1], inputs.shape[1]
+    edges = [0, STEP // 2] + list(range(STEP, hidden - STEP + 1, STEP)) + [hidden - STEP // 2, hidden]
+    steps = [slice(low, high) for low, high in zip(edges, edges[1:])]
+    first_model = 2
     copies = []
-
-    def plan(pairs):
-        made_here = []
-        for source, target in pairs:
-            copy = pltpu.make_async_copy(source, target, sems.at[sum(map(len, copies)) + len(made_here)])
-            made_here.append(copy)
-        copies.append(made_here)
-
-    for step in range(hidden_steps):
-        at = pl.ds(step * STEP, STEP)
+    for step, at in enumerate(steps):
         pairs = [
-            (gate_pre.at[:, at], v_gate.at[:, at]),
-            (up_pre.at[:, at], v_up.at[:, at]),
-            (hidden_grad.at[:, at], v_back.at[:, at]),
-            (gate_out.at[:, at], v_gate_out.at[:, at]),
-            (up_out.at[:, at], v_up_out.at[:, at]),
-            (down_in.at[:, at], v_down_in.at[:, at]),
+            (gate_pre, v_gate),
+            (up_pre, v_up),
+            (hidden_grad, v_back),
+            (gate_out, v_gate_out),
+            (up_out, v_up_out),
+            (down_in, v_down_in),
         ]
-        if step < model_steps:
+        pairs = [
+            (source.at[:, pl.ds(at.start, at.stop - at.start)], target.at[:, pl.ds(at.start, at.stop - at.start)])
+            for source, target in pairs
+        ]
+        if 0 <= step - first_model < model // STEP:
+            at = pl.ds((step - first_model) * STEP, STEP)
             pairs += [
                 (inputs.at[:, at], v_inputs.at[:, at]),
                 (gate_in.at[:, at], v_in.at[pl.ds(0, width), at]),
@@ -72,12 +71,18 @@
                 (out_grad.at[:, at], v_out_grad.at[:, at]),
                 (down_out.at[:, at], v_down_out.at[:, at]),
             ]
-        plan(pairs)
-
-    def products(step, left):
+        known = sum(map(len, copies))
+        copies.append(
+            [
+                pltpu.make_async_copy(source, target, sems.at[known + i])
+                for i, (source, target) in enumerate(pairs)
+            ]
+        )
+
+    def products(left):
         parts = []
         for top in range(0, tokens, ROWS):
-            at = (slice(top, top + ROWS), slice(step * STEP + left, step * STEP + left + TILE))
+            at = (slice(top, top + ROWS), slice(left, left + TILE))
             half = 0.5 * v_gate[at].astype(jnp.float32)
             up = v_up[at].astype(jnp.float32)
             back = v_back[at].astype(jnp.float32)
@@ -96,33 +101,34 @@
         else:
             total[...] += value
 
-    def hidden_dots(step, left):
-        at = slice(step * STEP + left, step * STEP + left + TILE)
+    def hidden_dots(left):
+        at = slice(left, left + TILE)
         bases = (v_gate_out, v_up_out, v_down_in)
-        for which, value in enumerate(products(step, left)):
-            add(sums.at[which], value, bases[which][:, at], step == 0 and left == 0)
+        for which, value in enumerate(products(left)):
+            add(sums.at[which], value, bases[which][:, at], left == 0)
 
     def model_dots(step):
         at = slice(step * STEP, (step + 1) * STEP)
         add(sum_in, v_inputs[:, at], v_in[:, at], step == 0)
         add(sums.at[3], v_out_grad[:, at], v_down_out[:, at], step == 0)
 
-    for step in range(min(AHEAD, hidden_steps)):
+    for step in range(AHEAD):
         for copy in copies[step]:
             copy.start()
-    for step in range(hidden_steps):
-        if step + AHEAD < hidden_steps:
+    for step, at in enumerate(steps):
+        if step + AHEAD < len(steps):
             for copy in copies[step + AHEAD]:
                 copy.start()
         for copy in copies[step]:
             copy.wait()
-        for left in range(0, STEP, TILE):
-            hidden_dots(step, left)
-        if step < model_steps:
-            model_dots(step)
+        for left in range(at.start, at.stop, TILE):
+            hidden_dots(left)
+        if 0 <= step - first_model < model // STEP:
+            model_dots(step - first_model)
     out[:, : 2 * width] = sum_in[...]
     out[:, 2 * width : 4 * width] = jnp.concatenate([0.5 * sums[0], sums[1]], axis=1)
     out[:, 4 * width :] = jnp.concatenate([sums[2], sums[3]], axis=1)
+    rounded[...] = out[...].astype(jnp.bfloat16)
 
 
 def projections(*operands):
@@ -130,15 +136,15 @@
     width = operands[5].shape[0]
     tokens, model = inputs.shape
     hidden = gate_pre.shape[1]
-    assert hidden % STEP == 0 and model % STEP == 0 and model <= hidden
+    assert hidden % STEP == 0 and model % STEP == 0 and model + 2 * STEP <= hidden
     assert tokens % ROWS == 0
-    steps = 6 * (hidden // STEP) + 5 * (model // STEP)
+    copies = 6 * (hidden // STEP + 2) + 5 * (model // STEP)
     bf16 = jnp.bfloat16
     return pl.pallas_call(
         project,
-        out_shape=jax.ShapeDtypeStruct((tokens, 6 * width), jnp.float32),
+        out_shape=[jax.ShapeDtypeStruct((tokens, 6 * width), kind) for kind in (jnp.float32, bf16)],
         in_specs=[pl.BlockSpec(memory_space=pltpu.HBM)] * len(operands),
-        out_specs=pl.BlockSpec(memory_space=pltpu.VMEM),
+        out_specs=[pl.BlockSpec(memory_space=pltpu.VMEM)] * 2,
         scratch_shapes=[
             pltpu.VMEM((tokens, model), bf16),
             pltpu.VMEM((tokens, hidden), bf16),
@@ -152,7 +158,7 @@
             pltpu.VMEM((width, model), bf16),
             pltpu.VMEM((tokens, 2 * width), jnp.float32),
             pltpu.VMEM((4, tokens, width), jnp.float32),
-            pltpu.SemaphoreType.DMA((steps,)),
+            pltpu.SemaphoreType.DMA((copies,)),
         ],
         compiler_params=pltpu.CompilerParams(vmem_limit_bytes=427 * 2**17),
         cost_estimate=pl.CostEstimate(
@@ -169,12 +175,12 @@
     return high, (value - high.astype(jnp.float32)).astype(jnp.bfloat16)
 
 
-def outer(chips, own, other, ids, out, summed, products):
+def outer(chips, own, other, ids, out, summed, products, blocks):
     chip, core = lax.axis_index("dp"), lax.axis_index("mp")
     width = own.shape[1] // 6
     half = width // 2
     span = 3 * half // chips
-    summed[...] = (own[...] + other[...]).T
+    summed[...] = (own[...] + other[...].astype(jnp.float32)).T
     own_label = 2 * chip + core
     tail_label = jnp.where(core == 1, 2 * chip - 1, -1)
     masks = [(ids[...] == label).astype(jnp.float32) for label in (tail_label, own_label)]
@@ -198,8 +204,9 @@
                 chip_to, inside = divmod(module * half + row, span)
                 count = min(span - inside, half - row)
                 put = slice(label * span + inside, label * span + inside + count)
-                out[chip_to, put, :] = packed[row : row + count]
+                blocks[chip_to, put, :] = packed[row : row + count]
                 row += count
+    out[...] = blocks[...].astype(jnp.bfloat16)
 
 
 def example_blocks(chips, own, other, ids):
@@ -207,12 +214,13 @@
     block = (3 * width // chips, 2 * width)
     return pl.pallas_call(
         functools.partial(outer, chips),
-        out_shape=jax.ShapeDtypeStruct((chips,) + block, jnp.float32),
+        out_shape=jax.ShapeDtypeStruct((chips,) + block, jnp.bfloat16),
         in_specs=[pl.BlockSpec(memory_space=pltpu.VMEM)] * 3,
         out_specs=pl.BlockSpec(memory_space=pltpu.VMEM),
         scratch_shapes=[
             pltpu.VMEM(own.shape[::-1], jnp.float32),
             pltpu.VMEM((3, 2 * width, 2 * width), jnp.float32),
+            pltpu.VMEM((chips,) + block, jnp.float32),
         ],
         compiler_params=pltpu.CompilerParams(vmem_limit_bytes=6 * 2**20),
         name="outer",
@@ -223,7 +231,7 @@
     core = lax.axis_index("mp")
     chips, height, lanes = received.shape
     span = height // 2
-    rows[: chips * height, :] = received[...].reshape(chips * height, lanes)
+    rows[: chips * height, :] = received[...].astype(jnp.float32).reshape(chips * height, lanes)
     rows[chips * height :, :] = jnp.zeros((8, lanes), jnp.float32)
     grads = []
     for at in range(span):
@@ -273,8 +281,8 @@
     swap = [(0, 1), (1, 0)]
     swapped = lax.ppermute(queries, "mp", swap)
     bases = [base.T for base in (gate_in, gate_out, up_in, up_out, down_in, down_out)]
-    own = projections(inputs, gate_pre, up_pre, hidden_grad, out_grad, *bases)
-    other = lax.ppermute(own, "mp", swap)
+    own, rounded = projections(inputs, gate_pre, up_pre, hidden_grad, out_grad, *bases)
+    other = lax.ppermute(rounded, "mp", swap)
     blocks = example_blocks(chips, own, other, example_ids.reshape(1, -1))
     received = lax.all_to_all(blocks, "dp", split_axis=0, concat_axis=0, tiled=True)
     scores = partial_scores(queries, swapped, received)[:, None]

time: 34.8 us -> 34.4 us (0.989)
  transfers between devices with their start and end apart: 2 -> 2, of which waited for: 1 -> 1; matrix products, arithmetic and copies ran while one was open for 0% -> 0% of each run, Pallas kernels for 24% -> 25%
where the time goes in v11:
time: 34.4 us; the launch traced here: 34.3 us
  blocking collectives  22.5 us (65%)
  Pallas kernels  9.16 us (27%)
  waiting for transfers between devices  1.32 us (4%)
  other arithmetic  0.61 us (2%)
  starting transfers between devices  0.57 us (2%)
    all_to_all x1, blocking collectives, body(): lax.all_to_all(blocks, 'dp', split_axis=0, concat_axis=0, tiled=True)  13.6 us
    all_to_all x1, blocking collectives, body(): lax.all_to_all(scores, 'dp', split_axis=0, concat_axis=0, tiled=True)  8.94 us
    pallas_call x1, Pallas kernels, projections(): pl.pallas_call(project, out_shape=[jax.ShapeDtypeStruct((tokens, 6 * widt...  8.18 us
    ppermute x1, waiting for transfers between devices, body(): other = lax.ppermute(rounded, 'mp', swap)  1.32 us
  transfers between devices with their start and end apart: 2, of which 1 were waited for; matrix products, arithmetic and copies ran while one was open for 0% of the time, Pallas kernels for 25%

profile of v11, /device:TPU:0, one launch (start us, length us, event | category | flops | bytes accessed | tf_op | source)
XLA Modules:
  0.0 34.3 jit_solution(1016314554231939888)
XLA Ops:
  0.0 0.5 %collective-permute-start = (bf16[512,768]{1,0:T(8,128)(2,1)}, bf16[512,768]{1,0:T(8,128)(2,1)S(1)}, u32[]{:S(2)}, u32[]{:S(2)}) collective-permute-start(bf16[512,768]{1,0:T(8,128)(2,1)} %queries.1), channel_id=1, source_target_pairs={{0,1},{1,0},{2,3},{3,2},{4,5},{5,4},{6,7},{7,6},{8,9},{9,8},{10,11... | collective-permute-start | bytes 2359304 | tf_op jit(solution)/shard_map/ppermute | solution.py:282
  0.5 0.0 copy-start.1
  0.5 0.0 copy-start
  0.5 8.2 %project.1 = (f32[192,384]{1,0:T(8,128)S(1)}, bf16[192,384]{1,0:T(8,128)(2,1)S(1)}) custom-call(bf16[192,4096]{1,0:T(8,128)(2,1)} %inputs.1, bf16[192,7168]{1,0:T(8,128)(2,1)} %gate_pre.1, bf16[192,7168]{1,0:T(8,128)(2,1)} %up_pre.1, bf16[192,7168]{1,0:T(8,128)(2,1)} %hidden_grad.1, bf16[192,4096]{1,0:T(8,128)(2,1)} %out_grad.1, bf16[64,4096]{1,0:T(8,128)(2,1)} %bitcast.14, ...), custom_call_target="tpu_custom_call" | custom-call | flops 830472192 | bytes 11403264 | tf_op jit(solution)/shard_map/project/pallas_call | solution.py:143
  8.6 0.1 collective-permute-start.1
  8.8 1.3 %collective-permute-done.1.other = bf16[192,384]{1,0:T(8,128)(2,1)S(1)} collective-permute-done((bf16[192,384]{1,0:T(8,128)(2,1)S(1)}, bf16[192,384]{1,0:T(8,128)(2,1)S(1)}, u32[]{:S(2)}, u32[]{:S(2)}) %collective-permute-start.1) | collective-permute-done | bytes 147488 | tf_op jit(solution)/shard_map/ppermute | solution.py:285
  10.1 0.0 copy-done.1
  10.1 0.5 %outer.1 = bf16[8,24,128]{2,1,0:T(8,128)(2,1)S(1)} custom-call(f32[192,384]{1,0:T(8,128)S(1)} %get-tuple-element.7.own, bf16[192,384]{1,0:T(8,128)(2,1)S(1)} %collective-permute-done.1.other, s32[1,192]{1,0:T(1,128)S(1)} %bitcast.10), custom_call_target="tpu_custom_call" | custom-call | tf_op jit(solution)/shard_map/outer/pallas_call | solution.py:215
  10.6 13.6 %all_to_all.10.received = bf16[8,24,128]{2,1,0:T(8,128)(2,1)S(1)} all-to-all(bf16[8,24,128]{2,1,0:T(8,128)(2,1)S(1)} %outer.1), channel_id=1, replica_groups=mesh['parts'=2,'dp'=8,'mp'=2] {'dp'}, dimensions={0} | all-to-all | bytes 98304 | tf_op jit(solution)/shard_map/all_to_all | solution.py:287
  24.1 0.0 collective-permute-done.swapped
  24.1 0.0 copy-done
  24.2 0.5 %score.1 = f32[8,512]{1,0:T(8,128)S(1)} custom-call(bf16[512,768]{1,0:T(8,128)(2,1)S(1)} %copy-done, bf16[512,768]{1,0:T(8,128)(2,1)S(1)} %collective-permute-done.swapped, bf16[8,24,128]{2,1,0:T(8,128)(2,1)S(1)} %all_to_all.10.received), custom_call_target="tpu_custom_call" | custom-call | tf_op jit(solution)/shard_map/score/pallas_call | solution.py:254
  24.7 8.9 %all_to_all.11 = f32[8,1,512]{2,1,0:T(1,128)S(1)} all-to-all(f32[8,1,512]{2,1,0:T(1,128)S(1)} %copy.14), channel_id=1, replica_groups=mesh['parts'=2,'dp'=8,'mp'=2] {'dp'}, dimensions={0} | all-to-all | bytes 32768 | tf_op jit(solution)/shard_map/all_to_all | solution.py:289
  33.6 0.6 %reduce_sum.11 = f32[512]{0:T(512)} reduce(f32[8,1,512]{2,1,0:T(1,128)S(1)} %all_to_all.11, f32[]{:T(128)} %constant.0.clone.1), dimensions={0,1}, to_apply=%region_0.0 | reduce | flops 3584 | bytes 18436 | tf_op jit(solution)/shard_map/reduce_sum | solution.py:290
  (1 shorter events, 0.0 us)
Async XLA Ops:
  0.0 24.1 %collective-permute-start = (bf16[512,768]{1,0:T(8,128)(2,1)}, bf16[512,768]{1,0:T(8,128)(2,1)S(1)}, u32[]{:S(2)}, u32[]{:S(2)}) collective-permute-start(bf16[512,768]{1,0:T(8,128)(2,1)} %queries.1), channel_id=1, source_target_pairs={{0,1},{1,0},{2,3},{3,2},{4,5},{5,4},{6,7},{7,6},{8,9},{9,8},{10,11... | collective-permute-start | bytes 2359304 | tf_op jit(solution)/shard_map/ppermute | solution.py:282
  0.5 9.6 %copy-start.1 = (s32[192]{0:T(256)S(1)}, s32[192]{0:T(256)}, u32[]{:S(2)}) copy-start(s32[192]{0:T(256)} %param.18) | copy-start | bytes 2308
  0.5 23.7 %copy-start = (bf16[512,768]{1,0:T(8,128)(2,1)S(1)}, bf16[512,768]{1,0:T(8,128)(2,1)}, u32[]{:S(2)}) copy-start(bf16[512,768]{1,0:T(8,128)(2,1)} %queries.1) | copy-start | bytes 2359300
  8.6 1.4 %collective-permute-start.1 = (bf16[192,384]{1,0:T(8,128)(2,1)S(1)}, bf16[192,384]{1,0:T(8,128)(2,1)S(1)}, u32[]{:S(2)}, u32[]{:S(2)}) collective-permute-start(bf16[192,384]{1,0:T(8,128)(2,1)S(1)} %get-tuple-element.8), channel_id=1, source_target_pairs={{0,1},{1,0},{2,3},{3,2},{4,5},{5,4},{6,7},{7,6},{8,9},{9,8},{10,11... | collective-permute-start | bytes 442376 | tf_op jit(solution)/shard_map/ppermute | solution.py:285

commit v12 on v10

--- a/solution.py
+++ b/solution.py
@@ -11,7 +11,7 @@
 STEP = 1024
 TILE = 256
 ROWS = 16
-AHEAD = 2
+AHEAD = 4
 
 
 def project(
@@ -43,41 +43,47 @@
 ):
     width = gate_in.shape[0]
     tokens = inputs.shape[0]
-    hidden_steps = gate_pre.shape[1] // STEP
-    model_steps = inputs.shape[1] // STEP
-    copies = []
-
-    def plan(pairs):
-        made_here = []
+    hidden, model = gate_pre.shape[1], inputs.shape[1]
+    edges = [0] + list(range(STEP // 2, hidden, STEP)) + [hidden]
+    pieces = [slice(low, high) for low, high in zip(edges, edges[1:])]
+    sides = [slice(0, hidden // 2), slice(hidden // 2, hidden)]
+    known = []
+
+    def copies(pairs, at=None):
+        group = []
         for source, target in pairs:
-            copy = pltpu.make_async_copy(source, target, sems.at[sum(map(len, copies)) + len(made_here)])
-            made_here.append(copy)
-        copies.append(made_here)
-
-    for step in range(hidden_steps):
-        at = pl.ds(step * STEP, STEP)
-        pairs = [
-            (gate_pre.at[:, at], v_gate.at[:, at]),
-            (up_pre.at[:, at], v_up.at[:, at]),
-            (hidden_grad.at[:, at], v_back.at[:, at]),
-            (gate_out.at[:, at], v_gate_out.at[:, at]),
-            (up_out.at[:, at], v_up_out.at[:, at]),
-            (down_in.at[:, at], v_down_in.at[:, at]),
-        ]
-        if step < model_steps:
-            pairs += [
-                (inputs.at[:, at], v_inputs.at[:, at]),
-                (gate_in.at[:, at], v_in.at[pl.ds(0, width), at]),
-                (up_in.at[:, at], v_in.at[pl.ds(width, width), at]),
-                (out_grad.at[:, at], v_out_grad.at[:, at]),
-                (down_out.at[:, at], v_down_out.at[:, at]),
-            ]
-        plan(pairs)
-
-    def products(step, left):
+            if at is not None:
+                window = pl.ds(at.start, at.stop - at.start)
+                source, target = source.at[:, window], target.at[:, window]
+            group.append(pltpu.make_async_copy(source, target, sems.at[len(known)]))
+            known.append(group[-1])
+        return group
+
+    activations = ((gate_pre, v_gate), (up_pre, v_up), (hidden_grad, v_back))
+    bases = ((gate_out, v_gate_out), (up_out, v_up_out), (down_in, v_down_in))
+    for_inputs = (
+        (gate_in, v_in.at[pl.ds(0, width), :]),
+        (up_in, v_in.at[pl.ds(width, width), :]),
+        (inputs, v_inputs),
+    )
+    for_out_grad = ((down_out, v_down_out), (out_grad, v_out_grad))
+    groups = []
+    for index, at in enumerate(pieces):
+        groups.append((copies(activations, at), ("hidden", at)))
+        if index == 0:
+            groups.append((copies(bases, sides[0]), None))
+        if index == 2:
+            groups.append((copies(bases, sides[1]), None))
+        if index == 3:
+            groups.append((copies(for_inputs), ("inputs", None)))
+        if index == 5:
+            groups.append((copies(for_out_grad), ("out_grad", None)))
+    groups[0], groups[1] = (groups[0][0], None), (groups[1][0], groups[0][1])
+
+    def products(left):
         parts = []
         for top in range(0, tokens, ROWS):
-            at = (slice(top, top + ROWS), slice(step * STEP + left, step * STEP + left + TILE))
+            at = (slice(top, top + ROWS), slice(left, left + TILE))
             half = 0.5 * v_gate[at].astype(jnp.float32)
             up = v_up[at].astype(jnp.float32)
             back = v_back[at].astype(jnp.float32)
@@ -96,30 +102,30 @@
         else:
             total[...] += value
 
-    def hidden_dots(step, left):
-        at = slice(step * STEP + left, step * STEP + left + TILE)
-        bases = (v_gate_out, v_up_out, v_down_in)
-        for which, value in enumerate(products(step, left)):
-            add(sums.at[which], value, bases[which][:, at], step == 0 and left == 0)
-
-    def model_dots(step):
-        at = slice(step * STEP, (step + 1) * STEP)
-        add(sum_in, v_inputs[:, at], v_in[:, at], step == 0)
-        add(sums.at[3], v_out_grad[:, at], v_down_out[:, at], step == 0)
-
-    for step in range(min(AHEAD, hidden_steps)):
-        for copy in copies[step]:
+    def hidden_dots(left):
+        at = slice(left, left + TILE)
+        for which, value in enumerate(products(left)):
+            add(sums.at[which], value, bases[which][1][:, at], left == 0)
+
+    for group, _ in groups[:AHEAD]:
+        for copy in group:
             copy.start()
-    for step in range(hidden_steps):
-        if step + AHEAD < hidden_steps:
-            for copy in copies[step + AHEAD]:
+    for index, (group, work) in enumerate(groups):
+        for later, _ in groups[index + AHEAD : index + AHEAD + 1]:
+            for copy in later:
                 copy.start()
-        for copy in copies[step]:
+        for copy in group:
             copy.wait()
-        for left in range(0, STEP, TILE):
-            hidden_dots(step, left)
-        if step < model_steps:
-            model_dots(step)
+        if work is None:
+            continue
+        kind, at = work
+        if kind == "hidden":
+            for left in range(at.start, at.stop, TILE):
+                hidden_dots(left)
+        if kind == "inputs":
+            add(sum_in, v_inputs[...], v_in[...], True)
+        if kind == "out_grad":
+            add(sums.at[3], v_out_grad[...], v_down_out[...], True)
     out[:, : 2 * width] = sum_in[...]
     out[:, 2 * width : 4 * width] = jnp.concatenate([0.5 * sums[0], sums[1]], axis=1)
     out[:, 4 * width :] = jnp.concatenate([sums[2], sums[3]], axis=1)
@@ -130,9 +136,8 @@
     width = operands[5].shape[0]
     tokens, model = inputs.shape
     hidden = gate_pre.shape[1]
-    assert hidden % STEP == 0 and model % STEP == 0 and model <= hidden
-    assert tokens % ROWS == 0
-    steps = 6 * (hidden // STEP) + 5 * (model // STEP)
+    assert hidden % STEP == 0 and hidden >= 6 * STEP and tokens % ROWS == 0
+    copies = 3 * (hidden // STEP + 1) + 11
     bf16 = jnp.bfloat16
     return pl.pallas_call(
         project,
@@ -152,7 +157,7 @@
             pltpu.VMEM((width, model), bf16),
             pltpu.VMEM((tokens, 2 * width), jnp.float32),
             pltpu.VMEM((4, tokens, width), jnp.float32),
-            pltpu.SemaphoreType.DMA((steps,)),
+            pltpu.SemaphoreType.DMA((copies,)),
         ],
         compiler_params=pltpu.CompilerParams(vmem_limit_bytes=427 * 2**17),
         cost_estimate=pl.CostEstimate(

time: 34.8 us -> 36.2 us (1.040)
  Pallas kernels: 8.96 us -> 10.4 us
    pallas_call x1, Pallas kernels: 7.98 us -> 9.4 us  [projections(): pl.pallas_call(project, out_shape=jax.ShapeDtypeStruct((tokens, 6 * width...]
  transfers between devices with their start and end apart: 2 -> 2, of which waited for: 1 -> 1; matrix products, arithmetic and copies ran while one was open for 0% -> 0% of each run, Pallas kernels for 24% -> 27%
where the time goes in v12:
time: 36.2 us; the launch traced here: 36 us
  blocking collectives  22.8 us (63%)
  Pallas kernels  10.4 us (29%)
  waiting for transfers between devices  1.53 us (4%)
  other arithmetic  0.61 us (2%)
  starting transfers between devices  0.58 us (2%)
    all_to_all x1, blocking collectives, body(): lax.all_to_all(blocks, 'dp', split_axis=0, concat_axis=0, tiled=True)  13.9 us
    pallas_call x1, Pallas kernels, projections(): pl.pallas_call(project, out_shape=jax.ShapeDtypeStruct((tokens, 6 * width...  9.4 us
    all_to_all x1, blocking collectives, body(): lax.all_to_all(scores, 'dp', split_axis=0, concat_axis=0, tiled=True)  8.94 us
    ppermute x1, waiting for transfers between devices, body(): other = lax.ppermute(own, 'mp', swap)  1.52 us
  transfers between devices with their start and end apart: 2, of which 1 were waited for; matrix products, arithmetic and copies ran while one was open for 0% of the time, Pallas kernels for 27%

profile of v12, /device:TPU:0, one launch (start us, length us, event | category | flops | bytes accessed | tf_op | source)
XLA Modules:
  0.0 36.0 jit_solution(14460729028086660307)
XLA Ops:
  0.0 0.5 %collective-permute-start = (bf16[512,768]{1,0:T(8,128)(2,1)}, bf16[512,768]{1,0:T(8,128)(2,1)S(1)}, u32[]{:S(2)}, u32[]{:S(2)}) collective-permute-start(bf16[512,768]{1,0:T(8,128)(2,1)} %queries.1), channel_id=1, source_target_pairs={{0,1},{1,0},{2,3},{3,2},{4,5},{5,4},{6,7},{7,6},{8,9},{9,8},{10,11... | collective-permute-start | bytes 2359304 | tf_op jit(solution)/shard_map/ppermute | solution.py:279
  0.5 0.0 copy-start.1
  0.5 0.0 copy-start
  0.5 9.4 %project.1.own = f32[192,384]{1,0:T(8,128)S(1)} custom-call(bf16[192,4096]{1,0:T(8,128)(2,1)} %inputs.1, bf16[192,7168]{1,0:T(8,128)(2,1)} %gate_pre.1, bf16[192,7168]{1,0:T(8,128)(2,1)} %up_pre.1, bf16[192,7168]{1,0:T(8,128)(2,1)} %hidden_grad.1, bf16[192,4096]{1,0:T(8,128)(2,1)} %out_grad.1, bf16[64,4096]{1,0:T(8,128)(2,1)} %bitcast.14, ...), custom_call_target="tpu_custom_call" | custom-call | flops 830472192 | bytes 11403264 | tf_op jit(solution)/shard_map/project/pallas_call | solution.py:142
  9.9 0.1 collective-permute-start.1
  10.0 1.5 %collective-permute-done.1.other = f32[192,384]{1,0:T(8,128)S(1)} collective-permute-done((f32[192,384]{1,0:T(8,128)S(1)}, f32[192,384]{1,0:T(8,128)S(1)}, u32[]{:S(2)}, u32[]{:S(2)}) %collective-permute-start.1) | collective-permute-done | bytes 294944 | tf_op jit(solution)/shard_map/ppermute | solution.py:282
  11.5 0.0 copy-done.1
  11.5 0.5 %outer.1 = f32[8,24,128]{2,1,0:T(8,128)S(1)} custom-call(f32[192,384]{1,0:T(8,128)S(1)} %project.1.own, f32[192,384]{1,0:T(8,128)S(1)} %collective-permute-done.1.other, s32[1,192]{1,0:T(1,128)S(1)} %bitcast.10), custom_call_target="tpu_custom_call" | custom-call | tf_op jit(solution)/shard_map/outer/pallas_call | solution.py:213
  12.0 13.9 %all_to_all.10.received = f32[8,24,128]{2,1,0:T(8,128)S(1)} all-to-all(f32[8,24,128]{2,1,0:T(8,128)S(1)} %outer.1), channel_id=1, replica_groups=mesh['parts'=2,'dp'=8,'mp'=2] {'dp'}, dimensions={0} | all-to-all | bytes 196608 | tf_op jit(solution)/shard_map/all_to_all | solution.py:284
  25.9 0.0 collective-permute-done.swapped
  25.9 0.0 copy-done
  25.9 0.5 %score.1 = f32[8,512]{1,0:T(8,128)S(1)} custom-call(bf16[512,768]{1,0:T(8,128)(2,1)S(1)} %copy-done, bf16[512,768]{1,0:T(8,128)(2,1)S(1)} %collective-permute-done.swapped, f32[8,24,128]{2,1,0:T(8,128)S(1)} %all_to_all.10.received), custom_call_target="tpu_custom_call" | custom-call | tf_op jit(solution)/shard_map/score/pallas_call | solution.py:251
  26.5 8.9 %all_to_all.11 = f32[8,1,512]{2,1,0:T(1,128)S(1)} all-to-all(f32[8,1,512]{2,1,0:T(1,128)S(1)} %copy.14), channel_id=1, replica_groups=mesh['parts'=2,'dp'=8,'mp'=2] {'dp'}, dimensions={0} | all-to-all | bytes 32768 | tf_op jit(solution)/shard_map/all_to_all | solution.py:286
  35.4 0.6 %reduce_sum.11 = f32[512]{0:T(512)} reduce(f32[8,1,512]{2,1,0:T(1,128)S(1)} %all_to_all.11, f32[]{:T(128)} %constant.0.clone.1), dimensions={0,1}, to_apply=%region_0.0 | reduce | flops 3584 | bytes 18436 | tf_op jit(solution)/shard_map/reduce_sum | solution.py:287
  (1 shorter events, 0.0 us)
Async XLA Ops:
  0.0 25.9 %collective-permute-start = (bf16[512,768]{1,0:T(8,128)(2,1)}, bf16[512,768]{1,0:T(8,128)(2,1)S(1)}, u32[]{:S(2)}, u32[]{:S(2)}) collective-permute-start(bf16[512,768]{1,0:T(8,128)(2,1)} %queries.1), channel_id=1, source_target_pairs={{0,1},{1,0},{2,3},{3,2},{4,5},{5,4},{6,7},{7,6},{8,9},{9,8},{10,11... | collective-permute-start | bytes 2359304 | tf_op jit(solution)/shard_map/ppermute | solution.py:279
  0.5 11.1 %copy-start.1 = (s32[192]{0:T(256)S(1)}, s32[192]{0:T(256)}, u32[]{:S(2)}) copy-start(s32[192]{0:T(256)} %param.18) | copy-start | bytes 2308
  0.5 25.4 %copy-start = (bf16[512,768]{1,0:T(8,128)(2,1)S(1)}, bf16[512,768]{1,0:T(8,128)(2,1)}, u32[]{:S(2)}) copy-start(bf16[512,768]{1,0:T(8,128)(2,1)} %queries.1) | copy-start | bytes 2359300
  9.9 1.6 %collective-permute-start.1 = (f32[192,384]{1,0:T(8,128)S(1)}, f32[192,384]{1,0:T(8,128)S(1)}, u32[]{:S(2)}, u32[]{:S(2)}) collective-permute-start(f32[192,384]{1,0:T(8,128)S(1)} %project.1.own), channel_id=1, source_target_pairs={{0,1},{1,0},{2,3},{3,2},{4,5},{5,4},{6,7},{7,6},{8,9},{9,8},{10,11... | collective-permute-start | bytes 884744 | tf_op jit(solution)/shard_map/ppermute | solution.py:282

commit v13 on v10

--- a/solution.py
+++ b/solution.py
@@ -102,10 +102,10 @@
         for which, value in enumerate(products(step, left)):
             add(sums.at[which], value, bases[which][:, at], step == 0 and left == 0)
 
-    def model_dots(step):
-        at = slice(step * STEP, (step + 1) * STEP)
-        add(sum_in, v_inputs[:, at], v_in[:, at], step == 0)
-        add(sums.at[3], v_out_grad[:, at], v_down_out[:, at], step == 0)
+    def model_dots(left):
+        at = slice(left, left + TILE)
+        add(sum_in, v_inputs[:, at], v_in[:, at], left == 0)
+        add(sums.at[3], v_out_grad[:, at], v_down_out[:, at], left == 0)
 
     for step in range(min(AHEAD, hidden_steps)):
         for copy in copies[step]:
@@ -118,8 +118,8 @@
             copy.wait()
         for left in range(0, STEP, TILE):
             hidden_dots(step, left)
-        if step < model_steps:
-            model_dots(step)
+            if step < model_steps:
+                model_dots(step * STEP + left)
     out[:, : 2 * width] = sum_in[...]
     out[:, 2 * width : 4 * width] = jnp.concatenate([0.5 * sums[0], sums[1]], axis=1)
     out[:, 4 * width :] = jnp.concatenate([sums[2], sums[3]], axis=1)

time: 34.8 us -> 34.7 us (level)
  no operation moved by 1% of the time
where the time goes in v13:
time: 34.7 us; the launch traced here: 34.5 us
  blocking collectives  22.8 us (66%)
  Pallas kernels  8.88 us (26%)
  waiting for transfers between devices  1.53 us (4%)
  other arithmetic  0.61 us (2%)
  starting transfers between devices  0.57 us (2%)
    all_to_all x1, blocking collectives, body(): lax.all_to_all(blocks, 'dp', split_axis=0, concat_axis=0, tiled=True)  13.9 us
    all_to_all x1, blocking collectives, body(): lax.all_to_all(scores, 'dp', split_axis=0, concat_axis=0, tiled=True)  8.94 us
    pallas_call x1, Pallas kernels, projections(): pl.pallas_call(project, out_shape=jax.ShapeDtypeStruct((tokens, 6 * width...  7.91 us
    ppermute x1, waiting for transfers between devices, body(): other = lax.ppermute(own, 'mp', swap)  1.53 us
  transfers between devices with their start and end apart: 2, of which 1 were waited for; matrix products, arithmetic and copies ran while one was open for 0% of the time, Pallas kernels for 24%

profile of v13, /device:TPU:0, one launch (start us, length us, event | category | flops | bytes accessed | tf_op | source)
XLA Modules:
  0.0 34.5 jit_solution(12508355165399449045)
XLA Ops:
  0.0 0.5 %collective-permute-start = (bf16[512,768]{1,0:T(8,128)(2,1)}, bf16[512,768]{1,0:T(8,128)(2,1)S(1)}, u32[]{:S(2)}, u32[]{:S(2)}) collective-permute-start(bf16[512,768]{1,0:T(8,128)(2,1)} %queries.1), channel_id=1, source_target_pairs={{0,1},{1,0},{2,3},{3,2},{4,5},{5,4},{6,7},{7,6},{8,9},{9,8},{10,11... | collective-permute-start | bytes 2359304 | tf_op jit(solution)/shard_map/ppermute | solution.py:274
  0.5 0.0 copy-start.1
  0.5 0.0 copy-start
  0.5 7.9 %project.1.own = f32[192,384]{1,0:T(8,128)S(1)} custom-call(bf16[192,4096]{1,0:T(8,128)(2,1)} %inputs.1, bf16[192,7168]{1,0:T(8,128)(2,1)} %gate_pre.1, bf16[192,7168]{1,0:T(8,128)(2,1)} %up_pre.1, bf16[192,7168]{1,0:T(8,128)(2,1)} %hidden_grad.1, bf16[192,4096]{1,0:T(8,128)(2,1)} %out_grad.1, bf16[64,4096]{1,0:T(8,128)(2,1)} %bitcast.14, ...), custom_call_target="tpu_custom_call" | custom-call | flops 830472192 | bytes 11403264 | tf_op jit(solution)/shard_map/project/pallas_call | solution.py:137
  8.4 0.1 collective-permute-start.1
  8.5 1.5 %collective-permute-done.1.other = f32[192,384]{1,0:T(8,128)S(1)} collective-permute-done((f32[192,384]{1,0:T(8,128)S(1)}, f32[192,384]{1,0:T(8,128)S(1)}, u32[]{:S(2)}, u32[]{:S(2)}) %collective-permute-start.1) | collective-permute-done | bytes 294944 | tf_op jit(solution)/shard_map/ppermute | solution.py:277
  10.0 0.0 copy-done.1
  10.0 0.5 %outer.1 = f32[8,24,128]{2,1,0:T(8,128)S(1)} custom-call(f32[192,384]{1,0:T(8,128)S(1)} %project.1.own, f32[192,384]{1,0:T(8,128)S(1)} %collective-permute-done.1.other, s32[1,192]{1,0:T(1,128)S(1)} %bitcast.10), custom_call_target="tpu_custom_call" | custom-call | tf_op jit(solution)/shard_map/outer/pallas_call | solution.py:208
  10.5 13.9 %all_to_all.10.received = f32[8,24,128]{2,1,0:T(8,128)S(1)} all-to-all(f32[8,24,128]{2,1,0:T(8,128)S(1)} %outer.1), channel_id=1, replica_groups=mesh['parts'=2,'dp'=8,'mp'=2] {'dp'}, dimensions={0} | all-to-all | bytes 196608 | tf_op jit(solution)/shard_map/all_to_all | solution.py:279
  24.4 0.0 collective-permute-done.swapped
  24.4 0.0 copy-done
  24.4 0.5 %score.1 = f32[8,512]{1,0:T(8,128)S(1)} custom-call(bf16[512,768]{1,0:T(8,128)(2,1)S(1)} %copy-done, bf16[512,768]{1,0:T(8,128)(2,1)S(1)} %collective-permute-done.swapped, f32[8,24,128]{2,1,0:T(8,128)S(1)} %all_to_all.10.received), custom_call_target="tpu_custom_call" | custom-call | tf_op jit(solution)/shard_map/score/pallas_call | solution.py:246
  25.0 8.9 %all_to_all.11 = f32[8,1,512]{2,1,0:T(1,128)S(1)} all-to-all(f32[8,1,512]{2,1,0:T(1,128)S(1)} %copy.14), channel_id=1, replica_groups=mesh['parts'=2,'dp'=8,'mp'=2] {'dp'}, dimensions={0} | all-to-all | bytes 32768 | tf_op jit(solution)/shard_map/all_to_all | solution.py:281
  33.9 0.6 %reduce_sum.11 = f32[512]{0:T(512)} reduce(f32[8,1,512]{2,1,0:T(1,128)S(1)} %all_to_all.11, f32[]{:T(128)} %constant.0.clone.1), dimensions={0,1}, to_apply=%region_0.0 | reduce | flops 3584 | bytes 18436 | tf_op jit(solution)/shard_map/reduce_sum | solution.py:282
  (1 shorter events, 0.0 us)
Async XLA Ops:
  0.0 24.4 %collective-permute-start = (bf16[512,768]{1,0:T(8,128)(2,1)}, bf16[512,768]{1,0:T(8,128)(2,1)S(1)}, u32[]{:S(2)}, u32[]{:S(2)}) collective-permute-start(bf16[512,768]{1,0:T(8,128)(2,1)} %queries.1), channel_id=1, source_target_pairs={{0,1},{1,0},{2,3},{3,2},{4,5},{5,4},{6,7},{7,6},{8,9},{9,8},{10,11... | collective-permute-start | bytes 2359304 | tf_op jit(solution)/shard_map/ppermute | solution.py:274
  0.5 9.6 %copy-start.1 = (s32[192]{0:T(256)S(1)}, s32[192]{0:T(256)}, u32[]{:S(2)}) copy-start(s32[192]{0:T(256)} %param.18) | copy-start | bytes 2308
  0.5 23.9 %copy-start = (bf16[512,768]{1,0:T(8,128)(2,1)S(1)}, bf16[512,768]{1,0:T(8,128)(2,1)}, u32[]{:S(2)}) copy-start(bf16[512,768]{1,0:T(8,128)(2,1)} %queries.1) | copy-start | bytes 2359300
  8.4 1.6 %collective-permute-start.1 = (f32[192,384]{1,0:T(8,128)S(1)}, f32[192,384]{1,0:T(8,128)S(1)}, u32[]{:S(2)}, u32[]{:S(2)}) collective-permute-start(f32[192,384]{1,0:T(8,128)S(1)} %project.1.own), channel_id=1, source_target_pairs={{0,1},{1,0},{2,3},{3,2},{4,5},{5,4},{6,7},{7,6},{8,9},{9,8},{10,11... | collective-permute-start | bytes 884744 | tf_op jit(solution)/shard_map/ppermute | solution.py:277

commit v14 on v13

--- a/solution.py
+++ b/solution.py
@@ -9,7 +9,7 @@
 
 NT = (((1,), (1,)), ((), ()))
 STEP = 1024
-TILE = 256
+TILE = 512
 ROWS = 16
 AHEAD = 2
 

time: 34.7 us -> 34.9 us (level)
  transfers between devices with their start and end apart: 2 -> 2, of which waited for: 1 -> 1; matrix products, arithmetic and copies ran while one was open for 0% -> 0% of each run, Pallas kernels for 24% -> 25%
where the time goes in v14:
time: 34.9 us; the launch traced here: 34.7 us
  blocking collectives  22.8 us (65%)
  Pallas kernels  9.03 us (26%)
  waiting for transfers between devices  1.53 us (4%)
  other arithmetic  0.61 us (2%)
  starting transfers between devices  0.57 us (2%)
    all_to_all x1, blocking collectives, body(): lax.all_to_all(blocks, 'dp', split_axis=0, concat_axis=0, tiled=True)  13.9 us
    all_to_all x1, blocking collectives, body(): lax.all_to_all(scores, 'dp', split_axis=0, concat_axis=0, tiled=True)  8.94 us
    pallas_call x1, Pallas kernels, projections(): pl.pallas_call(project, out_shape=jax.ShapeDtypeStruct((tokens, 6 * width...  8.05 us
    ppermute x1, waiting for transfers between devices, body(): other = lax.ppermute(own, 'mp', swap)  1.53 us
  transfers between devices with their start and end apart: 2, of which 1 were waited for; matrix products, arithmetic and copies ran while one was open for 0% of the time, Pallas kernels for 25%

profile of v14, /device:TPU:0, one launch (start us, length us, event | category | flops | bytes accessed | tf_op | source)
XLA Modules:
  0.0 34.7 jit_solution(2702380803068097195)
XLA Ops:
  0.0 0.5 %collective-permute-start = (bf16[512,768]{1,0:T(8,128)(2,1)}, bf16[512,768]{1,0:T(8,128)(2,1)S(1)}, u32[]{:S(2)}, u32[]{:S(2)}) collective-permute-start(bf16[512,768]{1,0:T(8,128)(2,1)} %queries.1), channel_id=1, source_target_pairs={{0,1},{1,0},{2,3},{3,2},{4,5},{5,4},{6,7},{7,6},{8,9},{9,8},{10,11... | collective-permute-start | bytes 2359304 | tf_op jit(solution)/shard_map/ppermute | solution.py:274
  0.5 0.0 copy-start.1
  0.5 0.0 copy-start
  0.5 8.1 %project.1.own = f32[192,384]{1,0:T(8,128)S(1)} custom-call(bf16[192,4096]{1,0:T(8,128)(2,1)} %inputs.1, bf16[192,7168]{1,0:T(8,128)(2,1)} %gate_pre.1, bf16[192,7168]{1,0:T(8,128)(2,1)} %up_pre.1, bf16[192,7168]{1,0:T(8,128)(2,1)} %hidden_grad.1, bf16[192,4096]{1,0:T(8,128)(2,1)} %out_grad.1, bf16[64,4096]{1,0:T(8,128)(2,1)} %bitcast.14, ...), custom_call_target="tpu_custom_call" | custom-call | flops 830472192 | bytes 11403264 | tf_op jit(solution)/shard_map/project/pallas_call | solution.py:137
  8.5 0.1 collective-permute-start.1
  8.6 1.5 %collective-permute-done.1.other = f32[192,384]{1,0:T(8,128)S(1)} collective-permute-done((f32[192,384]{1,0:T(8,128)S(1)}, f32[192,384]{1,0:T(8,128)S(1)}, u32[]{:S(2)}, u32[]{:S(2)}) %collective-permute-start.1) | collective-permute-done | bytes 294944 | tf_op jit(solution)/shard_map/ppermute | solution.py:277
  10.2 0.0 copy-done.1
  10.2 0.5 %outer.1 = f32[8,24,128]{2,1,0:T(8,128)S(1)} custom-call(f32[192,384]{1,0:T(8,128)S(1)} %project.1.own, f32[192,384]{1,0:T(8,128)S(1)} %collective-permute-done.1.other, s32[1,192]{1,0:T(1,128)S(1)} %bitcast.10), custom_call_target="tpu_custom_call" | custom-call | tf_op jit(solution)/shard_map/outer/pallas_call | solution.py:208
  10.6 13.9 %all_to_all.10.received = f32[8,24,128]{2,1,0:T(8,128)S(1)} all-to-all(f32[8,24,128]{2,1,0:T(8,128)S(1)} %outer.1), channel_id=1, replica_groups=mesh['parts'=2,'dp'=8,'mp'=2] {'dp'}, dimensions={0} | all-to-all | bytes 196608 | tf_op jit(solution)/shard_map/all_to_all | solution.py:279
  24.5 0.0 collective-permute-done.swapped
  24.6 0.0 copy-done
  24.6 0.5 %score.1 = f32[8,512]{1,0:T(8,128)S(1)} custom-call(bf16[512,768]{1,0:T(8,128)(2,1)S(1)} %copy-done, bf16[512,768]{1,0:T(8,128)(2,1)S(1)} %collective-permute-done.swapped, f32[8,24,128]{2,1,0:T(8,128)S(1)} %all_to_all.10.received), custom_call_target="tpu_custom_call" | custom-call | tf_op jit(solution)/shard_map/score/pallas_call | solution.py:246
  25.1 8.9 %all_to_all.11 = f32[8,1,512]{2,1,0:T(1,128)S(1)} all-to-all(f32[8,1,512]{2,1,0:T(1,128)S(1)} %copy.14), channel_id=1, replica_groups=mesh['parts'=2,'dp'=8,'mp'=2] {'dp'}, dimensions={0} | all-to-all | bytes 32768 | tf_op jit(solution)/shard_map/all_to_all | solution.py:281
  34.0 0.6 %reduce_sum.11 = f32[512]{0:T(512)} reduce(f32[8,1,512]{2,1,0:T(1,128)S(1)} %all_to_all.11, f32[]{:T(128)} %constant.0.clone.1), dimensions={0,1}, to_apply=%region_0.0 | reduce | flops 3584 | bytes 18436 | tf_op jit(solution)/shard_map/reduce_sum | solution.py:282
  (1 shorter events, 0.0 us)
Async XLA Ops:
  0.0 24.6 %collective-permute-start = (bf16[512,768]{1,0:T(8,128)(2,1)}, bf16[512,768]{1,0:T(8,128)(2,1)S(1)}, u32[]{:S(2)}, u32[]{:S(2)}) collective-permute-start(bf16[512,768]{1,0:T(8,128)(2,1)} %queries.1), channel_id=1, source_target_pairs={{0,1},{1,0},{2,3},{3,2},{4,5},{5,4},{6,7},{7,6},{8,9},{9,8},{10,11... | collective-permute-start | bytes 2359304 | tf_op jit(solution)/shard_map/ppermute | solution.py:274
  0.5 9.7 %copy-start.1 = (s32[192]{0:T(256)S(1)}, s32[192]{0:T(256)}, u32[]{:S(2)}) copy-start(s32[192]{0:T(256)} %param.18) | copy-start | bytes 2308
  0.5 24.1 %copy-start = (bf16[512,768]{1,0:T(8,128)(2,1)S(1)}, bf16[512,768]{1,0:T(8,128)(2,1)}, u32[]{:S(2)}) copy-start(bf16[512,768]{1,0:T(8,128)(2,1)} %queries.1) | copy-start | bytes 2359300
  8.5 1.6 %collective-permute-start.1 = (f32[192,384]{1,0:T(8,128)S(1)}, f32[192,384]{1,0:T(8,128)S(1)}, u32[]{:S(2)}, u32[]{:S(2)}) collective-permute-start(f32[192,384]{1,0:T(8,128)S(1)} %project.1.own), channel_id=1, source_target_pairs={{0,1},{1,0},{2,3},{3,2},{4,5},{5,4},{6,7},{7,6},{8,9},{9,8},{10,11... | collective-permute-start | bytes 884744 | tf_op jit(solution)/shard_map/ppermute | solution.py:277

commit v15 on v13

--- a/solution.py
+++ b/solution.py
@@ -271,10 +271,11 @@
 ):
     chips = lax.axis_size("dp")
     swap = [(0, 1), (1, 0)]
-    swapped = lax.ppermute(queries, "mp", swap)
     bases = [base.T for base in (gate_in, gate_out, up_in, up_out, down_in, down_out)]
     own = projections(inputs, gate_pre, up_pre, hidden_grad, out_grad, *bases)
+    own, queries = lax.optimization_barrier((own, queries))
     other = lax.ppermute(own, "mp", swap)
+    swapped = lax.ppermute(queries, "mp", swap)
     blocks = example_blocks(chips, own, other, example_ids.reshape(1, -1))
     received = lax.all_to_all(blocks, "dp", split_axis=0, concat_axis=0, tiled=True)
     scores = partial_scores(queries, swapped, received)[:, None]

time: 34.7 us -> 35.9 us (1.035)
  waiting for transfers between devices: 1.53 us -> 2.26 us
    ppermute x1, waiting for transfers between devices: 1.53 us -> 2.25 us  [body(): other = lax.ppermute(own, 'mp', swap)]
  transfers between devices with their start and end apart: 2 -> 2, of which waited for: 1 -> 1; matrix products, arithmetic and copies ran while one was open for 0% -> 0% of each run, Pallas kernels for 24% -> 1%
where the time goes in v15:
time: 35.9 us; the launch traced here: 35.7 us
  blocking collectives  23.1 us (64%)
  Pallas kernels  9.06 us (25%)
  waiting for transfers between devices  2.26 us (6%)
  other arithmetic  0.61 us (2%)
  starting transfers between devices  0.59 us (2%)
    all_to_all x1, blocking collectives, body(): lax.all_to_all(blocks, 'dp', split_axis=0, concat_axis=0, tiled=True)  14.1 us
    all_to_all x1, blocking collectives, body(): lax.all_to_all(scores, 'dp', split_axis=0, concat_axis=0, tiled=True)  8.94 us
    pallas_call x1, Pallas kernels, projections(): pl.pallas_call(project, out_shape=jax.ShapeDtypeStruct((tokens, 6 * width...  8.08 us
    ppermute x1, waiting for transfers between devices, body(): other = lax.ppermute(own, 'mp', swap)  2.25 us
  transfers between devices with their start and end apart: 2, of which 1 were waited for; matrix products, arithmetic and copies ran while one was open for 0% of the time, Pallas kernels for 1%

profile of v15, /device:TPU:0, one launch (start us, length us, event | category | flops | bytes accessed | tf_op | source)
XLA Modules:
  0.0 35.7 jit_solution(4932969304540461534)
XLA Ops:
  0.0 0.0 copy-start
  0.0 0.0 copy-start.1
  0.0 8.1 %project.1.own = f32[192,384]{1,0:T(8,128)S(1)} custom-call(bf16[192,4096]{1,0:T(8,128)(2,1)} %inputs.1, bf16[192,7168]{1,0:T(8,128)(2,1)} %gate_pre.1, bf16[192,7168]{1,0:T(8,128)(2,1)} %up_pre.1, bf16[192,7168]{1,0:T(8,128)(2,1)} %hidden_grad.1, bf16[192,4096]{1,0:T(8,128)(2,1)} %out_grad.1, bf16[64,4096]{1,0:T(8,128)(2,1)} %bitcast.14, ...), custom_call_target="tpu_custom_call" | custom-call | flops 830472192 | bytes 11403264 | tf_op jit(solution)/shard_map/project/pallas_call | solution.py:137
  8.1 0.0 copy-done
  8.1 0.5 %collective-permute-start = (bf16[512,768]{1,0:T(8,128)(2,1)S(1)}, bf16[512,768]{1,0:T(8,128)(2,1)S(1)}, u32[]{:S(2)}, u32[]{:S(2)}) collective-permute-start(bf16[512,768]{1,0:T(8,128)(2,1)S(1)} %copy-done), channel_id=1, source_target_pairs={{0,1},{1,0},{2,3},{3,2},{4,5},{5,4},{6,7},{7,6},{8,9},{9,8},{10,11... | collective-permute-start | bytes 2359304 | tf_op jit(solution)/shard_map/ppermute | solution.py:278
  8.6 0.1 collective-permute-start.1
  8.7 2.3 %collective-permute-done.1.other = f32[192,384]{1,0:T(8,128)S(1)} collective-permute-done((f32[192,384]{1,0:T(8,128)S(1)}, f32[192,384]{1,0:T(8,128)S(1)}, u32[]{:S(2)}, u32[]{:S(2)}) %collective-permute-start.1) | collective-permute-done | bytes 294944 | tf_op jit(solution)/shard_map/ppermute | solution.py:277
  11.0 0.0 copy-done.1
  11.0 0.5 %outer.1 = f32[8,24,128]{2,1,0:T(8,128)S(1)} custom-call(f32[192,384]{1,0:T(8,128)S(1)} %project.1.own, f32[192,384]{1,0:T(8,128)S(1)} %collective-permute-done.1.other, s32[1,192]{1,0:T(1,128)S(1)} %bitcast.10), custom_call_target="tpu_custom_call" | custom-call | tf_op jit(solution)/shard_map/outer/pallas_call | solution.py:208
  11.4 14.1 %all_to_all.10.received = f32[8,24,128]{2,1,0:T(8,128)S(1)} all-to-all(f32[8,24,128]{2,1,0:T(8,128)S(1)} %outer.1), channel_id=1, replica_groups=mesh['parts'=2,'dp'=8,'mp'=2] {'dp'}, dimensions={0} | all-to-all | bytes 196608 | tf_op jit(solution)/shard_map/all_to_all | solution.py:280
  25.6 0.0 collective-permute-done.swapped
  25.6 0.5 %score.1 = f32[8,512]{1,0:T(8,128)S(1)} custom-call(bf16[512,768]{1,0:T(8,128)(2,1)S(1)} %copy-done, bf16[512,768]{1,0:T(8,128)(2,1)S(1)} %collective-permute-done.swapped, f32[8,24,128]{2,1,0:T(8,128)S(1)} %all_to_all.10.received), custom_call_target="tpu_custom_call" | custom-call | tf_op jit(solution)/shard_map/score/pallas_call | solution.py:246
  26.1 8.9 %all_to_all.11 = f32[8,1,512]{2,1,0:T(1,128)S(1)} all-to-all(f32[8,1,512]{2,1,0:T(1,128)S(1)} %copy.14), channel_id=1, replica_groups=mesh['parts'=2,'dp'=8,'mp'=2] {'dp'}, dimensions={0} | all-to-all | bytes 32768 | tf_op jit(solution)/shard_map/all_to_all | solution.py:282
  35.1 0.6 %reduce_sum.11 = f32[512]{0:T(512)} reduce(f32[8,1,512]{2,1,0:T(1,128)S(1)} %all_to_all.11, f32[]{:T(128)} %constant.0.clone.1), dimensions={0,1}, to_apply=%region_0.0 | reduce | flops 3584 | bytes 18436 | tf_op jit(solution)/shard_map/reduce_sum | solution.py:283
  (1 shorter events, 0.0 us)
Async XLA Ops:
  0.0 8.1 %copy-start = (bf16[512,768]{1,0:T(8,128)(2,1)S(1)}, bf16[512,768]{1,0:T(8,128)(2,1)}, u32[]{:S(2)}) copy-start(bf16[512,768]{1,0:T(8,128)(2,1)} %queries) | copy-start | bytes 2359300
  0.0 11.0 %copy-start.1 = (s32[192]{0:T(256)S(1)}, s32[192]{0:T(256)}, u32[]{:S(2)}) copy-start(s32[192]{0:T(256)} %param.18) | copy-start | bytes 2308
  8.1 17.5 %collective-permute-start = (bf16[512,768]{1,0:T(8,128)(2,1)S(1)}, bf16[512,768]{1,0:T(8,128)(2,1)S(1)}, u32[]{:S(2)}, u32[]{:S(2)}) collective-permute-start(bf16[512,768]{1,0:T(8,128)(2,1)S(1)} %copy-done), channel_id=1, source_target_pairs={{0,1},{1,0},{2,3},{3,2},{4,5},{5,4},{6,7},{7,6},{8,9},{9,8},{10,11... | collective-permute-start | bytes 2359304 | tf_op jit(solution)/shard_map/ppermute | solution.py:278
  8.6 2.3 %collective-permute-start.1 = (f32[192,384]{1,0:T(8,128)S(1)}, f32[192,384]{1,0:T(8,128)S(1)}, u32[]{:S(2)}, u32[]{:S(2)}) collective-permute-start(f32[192,384]{1,0:T(8,128)S(1)} %project.1.own), channel_id=1, source_target_pairs={{0,1},{1,0},{2,3},{3,2},{4,5},{5,4},{6,7},{7,6},{8,9},{9,8},{10,11... | collective-permute-start | bytes 884744 | tf_op jit(solution)/shard_map/ppermute | solution.py:277

commit v16 on v13

--- a/solution.py
+++ b/solution.py
@@ -43,36 +43,41 @@
 ):
     width = gate_in.shape[0]
     tokens = inputs.shape[0]
-    hidden_steps = gate_pre.shape[1] // STEP
-    model_steps = inputs.shape[1] // STEP
-    copies = []
-
-    def plan(pairs):
-        made_here = []
-        for source, target in pairs:
-            copy = pltpu.make_async_copy(source, target, sems.at[sum(map(len, copies)) + len(made_here)])
-            made_here.append(copy)
-        copies.append(made_here)
-
-    for step in range(hidden_steps):
-        at = pl.ds(step * STEP, STEP)
-        pairs = [
-            (gate_pre.at[:, at], v_gate.at[:, at]),
-            (up_pre.at[:, at], v_up.at[:, at]),
-            (hidden_grad.at[:, at], v_back.at[:, at]),
-            (gate_out.at[:, at], v_gate_out.at[:, at]),
-            (up_out.at[:, at], v_up_out.at[:, at]),
-            (down_in.at[:, at], v_down_in.at[:, at]),
-        ]
-        if step < model_steps:
-            pairs += [
-                (inputs.at[:, at], v_inputs.at[:, at]),
-                (gate_in.at[:, at], v_in.at[pl.ds(0, width), at]),
-                (up_in.at[:, at], v_in.at[pl.ds(width, width), at]),
-                (out_grad.at[:, at], v_out_grad.at[:, at]),
-                (down_out.at[:, at], v_down_out.at[:, at]),
-            ]
-        plan(pairs)
+    hidden, model = gate_pre.shape[1], inputs.shape[1]
+    steps = hidden // STEP
+    activations = ((gate_pre, v_gate), (up_pre, v_up), (hidden_grad, v_back))
+    hidden_bases = ((gate_out, v_gate_out), (up_out, v_up_out), (down_in, v_down_in))
+    model_bases = (
+        (gate_in, v_in.at[pl.ds(0, width), :]),
+        (up_in, v_in.at[pl.ds(width, width), :]),
+        (down_out, v_down_out),
+    )
+    tokens_wide = ((inputs, v_inputs), (out_grad, v_out_grad))
+    first_model = 2
+    groups = []
+    for step in range(steps):
+        pairs = [(pair, step * STEP, STEP) for pair in activations]
+        if step == 0:
+            pairs += [(pair, 0, hidden // 2) for pair in hidden_bases]
+        if step == steps // 2:
+            pairs += [(pair, hidden // 2, hidden // 2) for pair in hidden_bases]
+        if step == first_model - 1:
+            pairs += [(pair, 0, model) for pair in model_bases]
+        if step == first_model:
+            pairs += [(pair, 0, model // 2) for pair in tokens_wide]
+        if step == first_model + model // STEP // 2:
+            pairs += [(pair, model // 2, model // 2) for pair in tokens_wide]
+        groups.append(pairs)
+
+    def start(step):
+        for (source, target), low, length in groups[step]:
+            at = pl.ds(low, length)
+            pltpu.make_async_copy(source.at[:, at], target.at[:, at], sems.at[step]).start()
+
+    def wait(step):
+        count = sum(source.shape[0] * length for (source, _), _, length in groups[step])
+        at = pl.ds(0, count // tokens)
+        pltpu.make_async_copy(gate_pre.at[:, at], v_gate.at[:, at], sems.at[step]).wait()
 
     def products(step, left):
         parts = []
@@ -107,19 +112,17 @@
         add(sum_in, v_inputs[:, at], v_in[:, at], left == 0)
         add(sums.at[3], v_out_grad[:, at], v_down_out[:, at], left == 0)
 
-    for step in range(min(AHEAD, hidden_steps)):
-        for copy in copies[step]:
-            copy.start()
-    for step in range(hidden_steps):
-        if step + AHEAD < hidden_steps:
-            for copy in copies[step + AHEAD]:
-                copy.start()
-        for copy in copies[step]:
-            copy.wait()
+    for step in range(AHEAD):
+        start(step)
+    for step in range(steps):
+        if step + AHEAD < steps:
+            start(step + AHEAD)
+        wait(step)
         for left in range(0, STEP, TILE):
             hidden_dots(step, left)
-            if step < model_steps:
-                model_dots(step * STEP + left)
+            model_left = (step - first_model) * STEP + left
+            if 0 <= model_left < model:
+                model_dots(model_left)
     out[:, : 2 * width] = sum_in[...]
     out[:, 2 * width : 4 * width] = jnp.concatenate([0.5 * sums[0], sums[1]], axis=1)
     out[:, 4 * width :] = jnp.concatenate([sums[2], sums[3]], axis=1)
@@ -130,9 +133,8 @@
     width = operands[5].shape[0]
     tokens, model = inputs.shape
     hidden = gate_pre.shape[1]
-    assert hidden % STEP == 0 and model % STEP == 0 and model <= hidden
-    assert tokens % ROWS == 0
-    steps = 6 * (hidden // STEP) + 5 * (model // STEP)
+    assert hidden % STEP == 0 and model % (2 * STEP) == 0 and tokens % ROWS == 0
+    assert 2 * STEP + model <= hidden and hidden % 256 == 0 and tokens == 3 * width
     bf16 = jnp.bfloat16
     return pl.pallas_call(
         project,
@@ -152,7 +154,7 @@
             pltpu.VMEM((width, model), bf16),
             pltpu.VMEM((tokens, 2 * width), jnp.float32),
             pltpu.VMEM((4, tokens, width), jnp.float32),
-            pltpu.SemaphoreType.DMA((steps,)),
+            pltpu.SemaphoreType.DMA((hidden // STEP,)),
         ],
         compiler_params=pltpu.CompilerParams(vmem_limit_bytes=427 * 2**17),
         cost_estimate=pl.CostEstimate(

time: 34.7 us -> 34.5 us (level)
  no operation moved by 1% of the time
where the time goes in v16:
time: 34.5 us; the launch traced here: 34.3 us
  blocking collectives  22.8 us (66%)
  Pallas kernels  8.66 us (25%)
  waiting for transfers between devices  1.53 us (4%)
  other arithmetic  0.61 us (2%)
  starting transfers between devices  0.58 us (2%)
    all_to_all x1, blocking collectives, body(): lax.all_to_all(blocks, 'dp', split_axis=0, concat_axis=0, tiled=True)  13.9 us
    all_to_all x1, blocking collectives, body(): lax.all_to_all(scores, 'dp', split_axis=0, concat_axis=0, tiled=True)  8.94 us
    pallas_call x1, Pallas kernels, projections(): pl.pallas_call(project, out_shape=jax.ShapeDtypeStruct((tokens, 6 * width...  7.68 us
    ppermute x1, waiting for transfers between devices, body(): other = lax.ppermute(own, 'mp', swap)  1.52 us
  transfers between devices with their start and end apart: 2, of which 1 were waited for; matrix products, arithmetic and copies ran while one was open for 0% of the time, Pallas kernels for 24%

profile of v16, /device:TPU:0, one launch (start us, length us, event | category | flops | bytes accessed | tf_op | source)
XLA Modules:
  0.0 34.3 jit_solution(156678580598958751)
XLA Ops:
  0.0 0.5 %collective-permute-start = (bf16[512,768]{1,0:T(8,128)(2,1)}, bf16[512,768]{1,0:T(8,128)(2,1)S(1)}, u32[]{:S(2)}, u32[]{:S(2)}) collective-permute-start(bf16[512,768]{1,0:T(8,128)(2,1)} %queries.1), channel_id=1, source_target_pairs={{0,1},{1,0},{2,3},{3,2},{4,5},{5,4},{6,7},{7,6},{8,9},{9,8},{10,11... | collective-permute-start | bytes 2359304 | tf_op jit(solution)/shard_map/ppermute | solution.py:276
  0.5 0.0 copy-start.1
  0.5 0.0 copy-start
  0.5 7.7 %project.1.own = f32[192,384]{1,0:T(8,128)S(1)} custom-call(bf16[192,4096]{1,0:T(8,128)(2,1)} %inputs.1, bf16[192,7168]{1,0:T(8,128)(2,1)} %gate_pre.1, bf16[192,7168]{1,0:T(8,128)(2,1)} %up_pre.1, bf16[192,7168]{1,0:T(8,128)(2,1)} %hidden_grad.1, bf16[192,4096]{1,0:T(8,128)(2,1)} %out_grad.1, bf16[64,4096]{1,0:T(8,128)(2,1)} %bitcast.14, ...), custom_call_target="tpu_custom_call" | custom-call | flops 830472192 | bytes 11403264 | tf_op jit(solution)/shard_map/project/pallas_call | solution.py:139
  8.1 0.1 collective-permute-start.1
  8.3 1.5 %collective-permute-done.1.other = f32[192,384]{1,0:T(8,128)S(1)} collective-permute-done((f32[192,384]{1,0:T(8,128)S(1)}, f32[192,384]{1,0:T(8,128)S(1)}, u32[]{:S(2)}, u32[]{:S(2)}) %collective-permute-start.1) | collective-permute-done | bytes 294944 | tf_op jit(solution)/shard_map/ppermute | solution.py:279
  9.8 0.0 copy-done.1
  9.8 0.5 %outer.1 = f32[8,24,128]{2,1,0:T(8,128)S(1)} custom-call(f32[192,384]{1,0:T(8,128)S(1)} %project.1.own, f32[192,384]{1,0:T(8,128)S(1)} %collective-permute-done.1.other, s32[1,192]{1,0:T(1,128)S(1)} %bitcast.10), custom_call_target="tpu_custom_call" | custom-call | tf_op jit(solution)/shard_map/outer/pallas_call | solution.py:210
  10.3 13.9 %all_to_all.10.received = f32[8,24,128]{2,1,0:T(8,128)S(1)} all-to-all(f32[8,24,128]{2,1,0:T(8,128)S(1)} %outer.1), channel_id=1, replica_groups=mesh['parts'=2,'dp'=8,'mp'=2] {'dp'}, dimensions={0} | all-to-all | bytes 196608 | tf_op jit(solution)/shard_map/all_to_all | solution.py:281
  24.2 0.0 collective-permute-done.swapped
  24.2 0.0 copy-done
  24.2 0.5 %score.1 = f32[8,512]{1,0:T(8,128)S(1)} custom-call(bf16[512,768]{1,0:T(8,128)(2,1)S(1)} %copy-done, bf16[512,768]{1,0:T(8,128)(2,1)S(1)} %collective-permute-done.swapped, f32[8,24,128]{2,1,0:T(8,128)S(1)} %all_to_all.10.received), custom_call_target="tpu_custom_call" | custom-call | tf_op jit(solution)/shard_map/score/pallas_call | solution.py:248
  24.7 8.9 %all_to_all.11 = f32[8,1,512]{2,1,0:T(1,128)S(1)} all-to-all(f32[8,1,512]{2,1,0:T(1,128)S(1)} %copy.14), channel_id=1, replica_groups=mesh['parts'=2,'dp'=8,'mp'=2] {'dp'}, dimensions={0} | all-to-all | bytes 32768 | tf_op jit(solution)/shard_map/all_to_all | solution.py:283
  33.7 0.6 %reduce_sum.11 = f32[512]{0:T(512)} reduce(f32[8,1,512]{2,1,0:T(1,128)S(1)} %all_to_all.11, f32[]{:T(128)} %constant.0.clone.1), dimensions={0,1}, to_apply=%region_0.0 | reduce | flops 3584 | bytes 18436 | tf_op jit(solution)/shard_map/reduce_sum | solution.py:284
  (1 shorter events, 0.0 us)
Async XLA Ops:
  0.0 24.2 %collective-permute-start = (bf16[512,768]{1,0:T(8,128)(2,1)}, bf16[512,768]{1,0:T(8,128)(2,1)S(1)}, u32[]{:S(2)}, u32[]{:S(2)}) collective-permute-start(bf16[512,768]{1,0:T(8,128)(2,1)} %queries.1), channel_id=1, source_target_pairs={{0,1},{1,0},{2,3},{3,2},{4,5},{5,4},{6,7},{7,6},{8,9},{9,8},{10,11... | collective-permute-start | bytes 2359304 | tf_op jit(solution)/shard_map/ppermute | solution.py:276
  0.5 9.3 %copy-start.1 = (s32[192]{0:T(256)S(1)}, s32[192]{0:T(256)}, u32[]{:S(2)}) copy-start(s32[192]{0:T(256)} %param.18) | copy-start | bytes 2308
  0.5 23.7 %copy-start = (bf16[512,768]{1,0:T(8,128)(2,1)S(1)}, bf16[512,768]{1,0:T(8,128)(2,1)}, u32[]{:S(2)}) copy-start(bf16[512,768]{1,0:T(8,128)(2,1)} %queries.1) | copy-start | bytes 2359300
  8.1 1.6 %collective-permute-start.1 = (f32[192,384]{1,0:T(8,128)S(1)}, f32[192,384]{1,0:T(8,128)S(1)}, u32[]{:S(2)}, u32[]{:S(2)}) collective-permute-start(f32[192,384]{1,0:T(8,128)S(1)} %project.1.own), channel_id=1, source_target_pairs={{0,1},{1,0},{2,3},{3,2},{4,5},{5,4},{6,7},{7,6},{8,9},{9,8},{10,11... | collective-permute-start | bytes 884744 | tf_op jit(solution)/shard_map/ppermute | solution.py:279

commit v17 on v16

--- a/solution.py
+++ b/solution.py
@@ -10,7 +10,7 @@
 NT = (((1,), (1,)), ((), ()))
 STEP = 1024
 TILE = 256
-ROWS = 16
+ROWS = 32
 AHEAD = 2
 
 

time: 34.5 us -> 34.5 us (level)
  no operation moved by 1% of the time
where the time goes in v17:
time: 34.5 us; the launch traced here: 34.3 us
  blocking collectives  22.8 us (66%)
  Pallas kernels  8.66 us (25%)
  waiting for transfers between devices  1.53 us (4%)
  other arithmetic  0.61 us (2%)
  starting transfers between devices  0.58 us (2%)
    all_to_all x1, blocking collectives, body(): lax.all_to_all(blocks, 'dp', split_axis=0, concat_axis=0, tiled=True)  13.9 us
    all_to_all x1, blocking collectives, body(): lax.all_to_all(scores, 'dp', split_axis=0, concat_axis=0, tiled=True)  8.94 us
    pallas_call x1, Pallas kernels, projections(): pl.pallas_call(project, out_shape=jax.ShapeDtypeStruct((tokens, 6 * width...  7.68 us
    ppermute x1, waiting for transfers between devices, body(): other = lax.ppermute(own, 'mp', swap)  1.52 us
  transfers between devices with their start and end apart: 2, of which 1 were waited for; matrix products, arithmetic and copies ran while one was open for 0% of the time, Pallas kernels for 24%

profile of v17, /device:TPU:0, one launch (start us, length us, event | category | flops | bytes accessed | tf_op | source)
XLA Modules:
  0.0 34.3 jit_solution(156678580598958751)
XLA Ops:
  0.0 0.5 %collective-permute-start = (bf16[512,768]{1,0:T(8,128)(2,1)}, bf16[512,768]{1,0:T(8,128)(2,1)S(1)}, u32[]{:S(2)}, u32[]{:S(2)}) collective-permute-start(bf16[512,768]{1,0:T(8,128)(2,1)} %queries.1), channel_id=1, source_target_pairs={{0,1},{1,0},{2,3},{3,2},{4,5},{5,4},{6,7},{7,6},{8,9},{9,8},{10,11... | collective-permute-start | bytes 2359304 | tf_op jit(solution)/shard_map/ppermute | solution.py:276
  0.5 0.0 copy-start.1
  0.5 0.0 copy-start
  0.5 7.7 %project.1.own = f32[192,384]{1,0:T(8,128)S(1)} custom-call(bf16[192,4096]{1,0:T(8,128)(2,1)} %inputs.1, bf16[192,7168]{1,0:T(8,128)(2,1)} %gate_pre.1, bf16[192,7168]{1,0:T(8,128)(2,1)} %up_pre.1, bf16[192,7168]{1,0:T(8,128)(2,1)} %hidden_grad.1, bf16[192,4096]{1,0:T(8,128)(2,1)} %out_grad.1, bf16[64,4096]{1,0:T(8,128)(2,1)} %bitcast.14, ...), custom_call_target="tpu_custom_call" | custom-call | flops 830472192 | bytes 11403264 | tf_op jit(solution)/shard_map/project/pallas_call | solution.py:139
  8.1 0.1 collective-permute-start.1
  8.3 1.5 %collective-permute-done.1.other = f32[192,384]{1,0:T(8,128)S(1)} collective-permute-done((f32[192,384]{1,0:T(8,128)S(1)}, f32[192,384]{1,0:T(8,128)S(1)}, u32[]{:S(2)}, u32[]{:S(2)}) %collective-permute-start.1) | collective-permute-done | bytes 294944 | tf_op jit(solution)/shard_map/ppermute | solution.py:279
  9.8 0.0 copy-done.1
  9.8 0.5 %outer.1 = f32[8,24,128]{2,1,0:T(8,128)S(1)} custom-call(f32[192,384]{1,0:T(8,128)S(1)} %project.1.own, f32[192,384]{1,0:T(8,128)S(1)} %collective-permute-done.1.other, s32[1,192]{1,0:T(1,128)S(1)} %bitcast.10), custom_call_target="tpu_custom_call" | custom-call | tf_op jit(solution)/shard_map/outer/pallas_call | solution.py:210
  10.3 13.9 %all_to_all.10.received = f32[8,24,128]{2,1,0:T(8,128)S(1)} all-to-all(f32[8,24,128]{2,1,0:T(8,128)S(1)} %outer.1), channel_id=1, replica_groups=mesh['parts'=2,'dp'=8,'mp'=2] {'dp'}, dimensions={0} | all-to-all | bytes 196608 | tf_op jit(solution)/shard_map/all_to_all | solution.py:281
  24.2 0.0 collective-permute-done.swapped
  24.2 0.0 copy-done
  24.2 0.5 %score.1 = f32[8,512]{1,0:T(8,128)S(1)} custom-call(bf16[512,768]{1,0:T(8,128)(2,1)S(1)} %copy-done, bf16[512,768]{1,0:T(8,128)(2,1)S(1)} %collective-permute-done.swapped, f32[8,24,128]{2,1,0:T(8,128)S(1)} %all_to_all.10.received), custom_call_target="tpu_custom_call" | custom-call | tf_op jit(solution)/shard_map/score/pallas_call | solution.py:248
  24.7 8.9 %all_to_all.11 = f32[8,1,512]{2,1,0:T(1,128)S(1)} all-to-all(f32[8,1,512]{2,1,0:T(1,128)S(1)} %copy.14), channel_id=1, replica_groups=mesh['parts'=2,'dp'=8,'mp'=2] {'dp'}, dimensions={0} | all-to-all | bytes 32768 | tf_op jit(solution)/shard_map/all_to_all | solution.py:283
  33.7 0.6 %reduce_sum.11 = f32[512]{0:T(512)} reduce(f32[8,1,512]{2,1,0:T(1,128)S(1)} %all_to_all.11, f32[]{:T(128)} %constant.0.clone.1), dimensions={0,1}, to_apply=%region_0.0 | reduce | flops 3584 | bytes 18436 | tf_op jit(solution)/shard_map/reduce_sum | solution.py:284
  (1 shorter events, 0.0 us)
Async XLA Ops:
  0.0 24.2 %collective-permute-start = (bf16[512,768]{1,0:T(8,128)(2,1)}, bf16[512,768]{1,0:T(8,128)(2,1)S(1)}, u32[]{:S(2)}, u32[]{:S(2)}) collective-permute-start(bf16[512,768]{1,0:T(8,128)(2,1)} %queries.1), channel_id=1, source_target_pairs={{0,1},{1,0},{2,3},{3,2},{4,5},{5,4},{6,7},{7,6},{8,9},{9,8},{10,11... | collective-permute-start | bytes 2359304 | tf_op jit(solution)/shard_map/ppermute | solution.py:276
  0.5 9.3 %copy-start.1 = (s32[192]{0:T(256)S(1)}, s32[192]{0:T(256)}, u32[]{:S(2)}) copy-start(s32[192]{0:T(256)} %param.18) | copy-start | bytes 2308
  0.5 23.7 %copy-start = (bf16[512,768]{1,0:T(8,128)(2,1)S(1)}, bf16[512,768]{1,0:T(8,128)(2,1)}, u32[]{:S(2)}) copy-start(bf16[512,768]{1,0:T(8,128)(2,1)} %queries.1) | copy-start | bytes 2359300
  8.1 1.6 %collective-permute-start.1 = (f32[192,384]{1,0:T(8,128)S(1)}, f32[192,384]{1,0:T(8,128)S(1)}, u32[]{:S(2)}, u32[]{:S(2)}) collective-permute-start(f32[192,384]{1,0:T(8,128)S(1)} %project.1.own), channel_id=1, source_target_pairs={{0,1},{1,0},{2,3},{3,2},{4,5},{5,4},{6,7},{7,6},{8,9},{9,8},{10,11... | collective-permute-start | bytes 884744 | tf_op jit(solution)/shard_map/ppermute | solution.py:279

commit v18 on v16

--- a/solution.py
+++ b/solution.py
@@ -11,7 +11,7 @@
 STEP = 1024
 TILE = 256
 ROWS = 16
-AHEAD = 2
+AHEAD = 3
 
 
 def project(
@@ -44,7 +44,8 @@
     width = gate_in.shape[0]
     tokens = inputs.shape[0]
     hidden, model = gate_pre.shape[1], inputs.shape[1]
-    steps = hidden // STEP
+    edges = [0] + list(range(STEP // 2, hidden, STEP)) + [hidden]
+    steps = len(edges) - 1
     activations = ((gate_pre, v_gate), (up_pre, v_up), (hidden_grad, v_back))
     hidden_bases = ((gate_out, v_gate_out), (up_out, v_up_out), (down_in, v_down_in))
     model_bases = (
@@ -53,19 +54,23 @@
         (down_out, v_down_out),
     )
     tokens_wide = ((inputs, v_inputs), (out_grad, v_out_grad))
-    first_model = 2
+    first_model = 3
+    second_model = first_model + model // STEP // 2
     groups = []
     for step in range(steps):
-        pairs = [(pair, step * STEP, STEP) for pair in activations]
+        low, high = edges[step], edges[step + 1]
+        pairs = [(pair, low, high - low) for pair in activations]
         if step == 0:
-            pairs += [(pair, 0, hidden // 2) for pair in hidden_bases]
-        if step == steps // 2:
-            pairs += [(pair, hidden // 2, hidden // 2) for pair in hidden_bases]
+            pairs += [(pair, low, high - low) for pair in hidden_bases]
+        if step == 1:
+            pairs += [(pair, low, hidden // 2 - low) for pair in hidden_bases]
+        if low == hidden // 2:
+            pairs += [(pair, low, hidden // 2) for pair in hidden_bases]
         if step == first_model - 1:
             pairs += [(pair, 0, model) for pair in model_bases]
         if step == first_model:
             pairs += [(pair, 0, model // 2) for pair in tokens_wide]
-        if step == first_model + model // STEP // 2:
+        if step == second_model:
             pairs += [(pair, model // 2, model // 2) for pair in tokens_wide]
         groups.append(pairs)
 
@@ -79,10 +84,10 @@
         at = pl.ds(0, count // tokens)
         pltpu.make_async_copy(gate_pre.at[:, at], v_gate.at[:, at], sems.at[step]).wait()
 
-    def products(step, left):
+    def products(left):
         parts = []
         for top in range(0, tokens, ROWS):
-            at = (slice(top, top + ROWS), slice(step * STEP + left, step * STEP + left + TILE))
+            at = (slice(top, top + ROWS), slice(left, left + TILE))
             half = 0.5 * v_gate[at].astype(jnp.float32)
             up = v_up[at].astype(jnp.float32)
             back = v_back[at].astype(jnp.float32)
@@ -101,11 +106,11 @@
         else:
             total[...] += value
 
-    def hidden_dots(step, left):
-        at = slice(step * STEP + left, step * STEP + left + TILE)
+    def hidden_dots(left):
+        at = slice(left, left + TILE)
         bases = (v_gate_out, v_up_out, v_down_in)
-        for which, value in enumerate(products(step, left)):
-            add(sums.at[which], value, bases[which][:, at], step == 0 and left == 0)
+        for which, value in enumerate(products(left)):
+            add(sums.at[which], value, bases[which][:, at], left == 0)
 
     def model_dots(left):
         at = slice(left, left + TILE)
@@ -118,9 +123,9 @@
         if step + AHEAD < steps:
             start(step + AHEAD)
         wait(step)
-        for left in range(0, STEP, TILE):
-            hidden_dots(step, left)
-            model_left = (step - first_model) * STEP + left
+        for left in range(edges[step], edges[step + 1], TILE):
+            hidden_dots(left)
+            model_left = left - edges[first_model]
             if 0 <= model_left < model:
                 model_dots(model_left)
     out[:, : 2 * width] = sum_in[...]
@@ -133,8 +138,8 @@
     width = operands[5].shape[0]
     tokens, model = inputs.shape
     hidden = gate_pre.shape[1]
-    assert hidden % STEP == 0 and model % (2 * STEP) == 0 and tokens % ROWS == 0
-    assert 2 * STEP + model <= hidden and hidden % 256 == 0 and tokens == 3 * width
+    assert hidden % (2 * STEP) == STEP and model % (2 * STEP) == 0 and tokens % ROWS == 0
+    assert 3 * STEP + model <= hidden and tokens == 3 * width
     bf16 = jnp.bfloat16
     return pl.pallas_call(
         project,
@@ -154,7 +159,7 @@
             pltpu.VMEM((width, model), bf16),
             pltpu.VMEM((tokens, 2 * width), jnp.float32),
             pltpu.VMEM((4, tokens, width), jnp.float32),
-            pltpu.SemaphoreType.DMA((hidden // STEP,)),
+            pltpu.SemaphoreType.DMA((hidden // STEP + 1,)),
         ],
         compiler_params=pltpu.CompilerParams(vmem_limit_bytes=427 * 2**17),
         cost_estimate=pl.CostEstimate(

time: 34.5 us -> 34.3 us (level)
  transfers between devices with their start and end apart: 2 -> 2, of which waited for: 1 -> 1; matrix products, arithmetic and copies ran while one was open for 0% -> 0% of each run, Pallas kernels for 24% -> 23%
where the time goes in v18:
time: 34.3 us; the launch traced here: 34.1 us
  blocking collectives  22.8 us (66%)
  Pallas kernels  8.5 us (25%)
  waiting for transfers between devices  1.52 us (4%)
  other arithmetic  0.61 us (2%)
  starting transfers between devices  0.58 us (2%)
    all_to_all x1, blocking collectives, body(): lax.all_to_all(blocks, 'dp', split_axis=0, concat_axis=0, tiled=True)  13.9 us
    all_to_all x1, blocking collectives, body(): lax.all_to_all(scores, 'dp', split_axis=0, concat_axis=0, tiled=True)  8.94 us
    pallas_call x1, Pallas kernels, projections(): pl.pallas_call(project, out_shape=jax.ShapeDtypeStruct((tokens, 6 * width...  7.52 us
    ppermute x1, waiting for transfers between devices, body(): other = lax.ppermute(own, 'mp', swap)  1.52 us
  transfers between devices with their start and end apart: 2, of which 1 were waited for; matrix products, arithmetic and copies ran while one was open for 0% of the time, Pallas kernels for 23%

profile of v18, /device:TPU:0, one launch (start us, length us, event | category | flops | bytes accessed | tf_op | source)
XLA Modules:
  0.0 34.1 jit_solution(11346207822682692533)
XLA Ops:
  0.0 0.5 %collective-permute-start = (bf16[512,768]{1,0:T(8,128)(2,1)}, bf16[512,768]{1,0:T(8,128)(2,1)S(1)}, u32[]{:S(2)}, u32[]{:S(2)}) collective-permute-start(bf16[512,768]{1,0:T(8,128)(2,1)} %queries.1), channel_id=1, source_target_pairs={{0,1},{1,0},{2,3},{3,2},{4,5},{5,4},{6,7},{7,6},{8,9},{9,8},{10,11... | collective-permute-start | bytes 2359304 | tf_op jit(solution)/shard_map/ppermute | solution.py:281
  0.5 0.0 copy-start.1
  0.5 0.0 copy-start
  0.5 7.5 %project.1.own = f32[192,384]{1,0:T(8,128)S(1)} custom-call(bf16[192,4096]{1,0:T(8,128)(2,1)} %inputs.1, bf16[192,7168]{1,0:T(8,128)(2,1)} %gate_pre.1, bf16[192,7168]{1,0:T(8,128)(2,1)} %up_pre.1, bf16[192,7168]{1,0:T(8,128)(2,1)} %hidden_grad.1, bf16[192,4096]{1,0:T(8,128)(2,1)} %out_grad.1, bf16[64,4096]{1,0:T(8,128)(2,1)} %bitcast.14, ...), custom_call_target="tpu_custom_call" | custom-call | flops 830472192 | bytes 11403264 | tf_op jit(solution)/shard_map/project/pallas_call | solution.py:144
  8.0 0.1 collective-permute-start.1
  8.1 1.5 %collective-permute-done.1.other = f32[192,384]{1,0:T(8,128)S(1)} collective-permute-done((f32[192,384]{1,0:T(8,128)S(1)}, f32[192,384]{1,0:T(8,128)S(1)}, u32[]{:S(2)}, u32[]{:S(2)}) %collective-permute-start.1) | collective-permute-done | bytes 294944 | tf_op jit(solution)/shard_map/ppermute | solution.py:284
  9.6 0.0 copy-done.1
  9.6 0.5 %outer.1 = f32[8,24,128]{2,1,0:T(8,128)S(1)} custom-call(f32[192,384]{1,0:T(8,128)S(1)} %project.1.own, f32[192,384]{1,0:T(8,128)S(1)} %collective-permute-done.1.other, s32[1,192]{1,0:T(1,128)S(1)} %bitcast.10), custom_call_target="tpu_custom_call" | custom-call | tf_op jit(solution)/shard_map/outer/pallas_call | solution.py:215
  10.1 13.9 %all_to_all.10.received = f32[8,24,128]{2,1,0:T(8,128)S(1)} all-to-all(f32[8,24,128]{2,1,0:T(8,128)S(1)} %outer.1), channel_id=1, replica_groups=mesh['parts'=2,'dp'=8,'mp'=2] {'dp'}, dimensions={0} | all-to-all | bytes 196608 | tf_op jit(solution)/shard_map/all_to_all | solution.py:286
  24.0 0.0 collective-permute-done.swapped
  24.0 0.0 copy-done
  24.0 0.5 %score.1 = f32[8,512]{1,0:T(8,128)S(1)} custom-call(bf16[512,768]{1,0:T(8,128)(2,1)S(1)} %copy-done, bf16[512,768]{1,0:T(8,128)(2,1)S(1)} %collective-permute-done.swapped, f32[8,24,128]{2,1,0:T(8,128)S(1)} %all_to_all.10.received), custom_call_target="tpu_custom_call" | custom-call | tf_op jit(solution)/shard_map/score/pallas_call | solution.py:253
  24.6 8.9 %all_to_all.11 = f32[8,1,512]{2,1,0:T(1,128)S(1)} all-to-all(f32[8,1,512]{2,1,0:T(1,128)S(1)} %copy.14), channel_id=1, replica_groups=mesh['parts'=2,'dp'=8,'mp'=2] {'dp'}, dimensions={0} | all-to-all | bytes 32768 | tf_op jit(solution)/shard_map/all_to_all | solution.py:288
  33.5 0.6 %reduce_sum.11 = f32[512]{0:T(512)} reduce(f32[8,1,512]{2,1,0:T(1,128)S(1)} %all_to_all.11, f32[]{:T(128)} %constant.0.clone.1), dimensions={0,1}, to_apply=%region_0.0 | reduce | flops 3584 | bytes 18436 | tf_op jit(solution)/shard_map/reduce_sum | solution.py:289
  (1 shorter events, 0.0 us)
Async XLA Ops:
  0.0 24.0 %collective-permute-start = (bf16[512,768]{1,0:T(8,128)(2,1)}, bf16[512,768]{1,0:T(8,128)(2,1)S(1)}, u32[]{:S(2)}, u32[]{:S(2)}) collective-permute-start(bf16[512,768]{1,0:T(8,128)(2,1)} %queries.1), channel_id=1, source_target_pairs={{0,1},{1,0},{2,3},{3,2},{4,5},{5,4},{6,7},{7,6},{8,9},{9,8},{10,11... | collective-permute-start | bytes 2359304 | tf_op jit(solution)/shard_map/ppermute | solution.py:281
  0.5 9.2 %copy-start.1 = (s32[192]{0:T(256)S(1)}, s32[192]{0:T(256)}, u32[]{:S(2)}) copy-start(s32[192]{0:T(256)} %param.18) | copy-start | bytes 2308
  0.5 23.6 %copy-start = (bf16[512,768]{1,0:T(8,128)(2,1)S(1)}, bf16[512,768]{1,0:T(8,128)(2,1)}, u32[]{:S(2)}) copy-start(bf16[512,768]{1,0:T(8,128)(2,1)} %queries.1) | copy-start | bytes 2359300
  8.0 1.6 %collective-permute-start.1 = (f32[192,384]{1,0:T(8,128)S(1)}, f32[192,384]{1,0:T(8,128)S(1)}, u32[]{:S(2)}, u32[]{:S(2)}) collective-permute-start(f32[192,384]{1,0:T(8,128)S(1)} %project.1.own), channel_id=1, source_target_pairs={{0,1},{1,0},{2,3},{3,2},{4,5},{5,4},{6,7},{7,6},{8,9},{9,8},{10,11... | collective-permute-start | bytes 884744 | tf_op jit(solution)/shard_map/ppermute | solution.py:284

commit v19 on v18

--- a/solution.py
+++ b/solution.py
@@ -205,7 +205,7 @@
                 chip_to, inside = divmod(module * half + row, span)
                 count = min(span - inside, half - row)
                 put = slice(label * span + inside, label * span + inside + count)
-                out[chip_to, put, :] = packed[row : row + count]
+                out[(chip_to + chips // 2) % chips, put, :] = packed[row : row + count]
                 row += count
 
 
@@ -230,7 +230,9 @@
     core = lax.axis_index("mp")
     chips, height, lanes = received.shape
     span = height // 2
-    rows[: chips * height, :] = received[...].reshape(chips * height, lanes)
+    middle = chips // 2
+    rows[: middle * height, :] = received[middle:].reshape(middle * height, lanes)
+    rows[middle * height : chips * height, :] = received[:middle].reshape(middle * height, lanes)
     rows[chips * height :, :] = jnp.zeros((8, lanes), jnp.float32)
     grads = []
     for at in range(span):
@@ -245,7 +247,8 @@
     theirs = jnp.where(first, terms[:, coords:], terms[:, :coords])
     scores = lax.dot_general(mine, queries[...], NT, preferred_element_type=jnp.float32)
     scores += lax.dot_general(theirs, swapped[...], NT, preferred_element_type=jnp.float32)
-    out[...] = scores[:chips] + scores[chips:]
+    total = scores[:chips] + scores[chips:]
+    out[...] = jnp.concatenate([total[middle:], total[:middle]], axis=0)
 
 
 def partial_scores(queries, swapped, received):
@@ -259,6 +262,14 @@
         compiler_params=pltpu.CompilerParams(vmem_limit_bytes=6 * 2**20),
         name="score",
     )(queries, swapped, received)
+
+
+def to_all(blocks):
+    chips = blocks.shape[0]
+    order = [(i + chips // 2) % chips for i in range(chips)]
+    return lax.all_to_all(
+        blocks, "dp", split_axis=0, concat_axis=0, axis_index_groups=[order], tiled=True
+    )
 
 
 def body(
@@ -283,9 +294,9 @@
     own = projections(inputs, gate_pre, up_pre, hidden_grad, out_grad, *bases)
     other = lax.ppermute(own, "mp", swap)
     blocks = example_blocks(chips, own, other, example_ids.reshape(1, -1))
-    received = lax.all_to_all(blocks, "dp", split_axis=0, concat_axis=0, tiled=True)
+    received = to_all(blocks)
     scores = partial_scores(queries, swapped, received)[:, None]
-    pieces = lax.all_to_all(scores, "dp", split_axis=0, concat_axis=0, tiled=True)
+    pieces = to_all(scores)
     return jnp.sum(pieces, axis=0)
 
 

time: 34.3 us -> 31.8 us (0.927)
  blocking collectives: 22.8 us -> 20.3 us
    all_to_all x2, blocking collectives: 22.8 us -> 20.3 us  [to_all(): lax.all_to_all(blocks, 'dp', split_axis=0, concat_axis=0, axis_index_grou...]
  transfers between devices with their start and end apart: 2 -> 2, of which waited for: 1 -> 1; matrix products, arithmetic and copies ran while one was open for 0% -> 0% of each run, Pallas kernels for 23% -> 25%
where the time goes in v19:
time: 31.8 us; the launch traced here: 31.6 us
  blocking collectives  20.3 us (64%)
  Pallas kernels  8.51 us (27%)
  waiting for transfers between devices  1.52 us (5%)
  other arithmetic  0.61 us (2%)
  starting transfers between devices  0.58 us (2%)
    all_to_all x2, blocking collectives, to_all(): lax.all_to_all(blocks, 'dp', split_axis=0, concat_axis=0, axis_index_grou...  20.3 us
    pallas_call x1, Pallas kernels, projections(): pl.pallas_call(project, out_shape=jax.ShapeDtypeStruct((tokens, 6 * width...  7.52 us
    ppermute x1, waiting for transfers between devices, body(): other = lax.ppermute(own, 'mp', swap)  1.52 us
  transfers between devices with their start and end apart: 2, of which 1 were waited for; matrix products, arithmetic and copies ran while one was open for 0% of the time, Pallas kernels for 25%

profile of v19, /device:TPU:0, one launch (start us, length us, event | category | flops | bytes accessed | tf_op | source)
XLA Modules:
  0.0 31.6 jit_solution(10421292621012445037)
XLA Ops:
  0.0 0.5 %collective-permute-start = (bf16[512,768]{1,0:T(8,128)(2,1)}, bf16[512,768]{1,0:T(8,128)(2,1)S(1)}, u32[]{:S(2)}, u32[]{:S(2)}) collective-permute-start(bf16[512,768]{1,0:T(8,128)(2,1)} %queries.1), channel_id=1, source_target_pairs={{0,1},{1,0},{2,3},{3,2},{4,5},{5,4},{6,7},{7,6},{8,9},{9,8},{10,11... | collective-permute-start | bytes 2359304 | tf_op jit(solution)/shard_map/ppermute | solution.py:292
  0.5 0.0 copy-start.1
  0.5 0.0 copy-start
  0.5 7.5 %project.1.own = f32[192,384]{1,0:T(8,128)S(1)} custom-call(bf16[192,4096]{1,0:T(8,128)(2,1)} %inputs.1, bf16[192,7168]{1,0:T(8,128)(2,1)} %gate_pre.1, bf16[192,7168]{1,0:T(8,128)(2,1)} %up_pre.1, bf16[192,7168]{1,0:T(8,128)(2,1)} %hidden_grad.1, bf16[192,4096]{1,0:T(8,128)(2,1)} %out_grad.1, bf16[64,4096]{1,0:T(8,128)(2,1)} %bitcast.14, ...), custom_call_target="tpu_custom_call" | custom-call | flops 830472192 | bytes 11403264 | tf_op jit(solution)/shard_map/project/pallas_call | solution.py:144
  8.0 0.1 collective-permute-start.1
  8.1 1.5 %collective-permute-done.1.other = f32[192,384]{1,0:T(8,128)S(1)} collective-permute-done((f32[192,384]{1,0:T(8,128)S(1)}, f32[192,384]{1,0:T(8,128)S(1)}, u32[]{:S(2)}, u32[]{:S(2)}) %collective-permute-start.1) | collective-permute-done | bytes 294944 | tf_op jit(solution)/shard_map/ppermute | solution.py:295
  9.6 0.0 copy-done.1
  9.6 0.5 %outer.1 = f32[8,24,128]{2,1,0:T(8,128)S(1)} custom-call(f32[192,384]{1,0:T(8,128)S(1)} %project.1.own, f32[192,384]{1,0:T(8,128)S(1)} %collective-permute-done.1.other, s32[1,192]{1,0:T(1,128)S(1)} %bitcast.10), custom_call_target="tpu_custom_call" | custom-call | tf_op jit(solution)/shard_map/outer/pallas_call | solution.py:215
  10.1 12.1 %all_to_all.10.received = f32[8,24,128]{2,1,0:T(8,128)S(1)} all-to-all(f32[8,24,128]{2,1,0:T(8,128)S(1)} %outer.1), channel_id=1, replica_groups={{8,10,12,14,0,2,4,6},{9,11,13,15,1,3,5,7},{24,26,28,30,16,18,20,22},{25..., dimensions={0} | all-to-all | bytes 196608 | tf_op jit(solution)/shard_map/all_to_all | solution.py:270
  22.2 0.0 collective-permute-done.swapped
  22.2 0.0 copy-done
  22.2 0.5 %score.1 = f32[8,512]{1,0:T(8,128)S(1)} custom-call(bf16[512,768]{1,0:T(8,128)(2,1)S(1)} %copy-done, bf16[512,768]{1,0:T(8,128)(2,1)S(1)} %collective-permute-done.swapped, f32[8,24,128]{2,1,0:T(8,128)S(1)} %all_to_all.10.received), custom_call_target="tpu_custom_call" | custom-call | tf_op jit(solution)/shard_map/score/pallas_call | solution.py:256
  22.8 8.2 %all_to_all.11 = f32[8,1,512]{2,1,0:T(1,128)S(1)} all-to-all(f32[8,1,512]{2,1,0:T(1,128)S(1)} %copy.14), channel_id=1, replica_groups={{8,10,12,14,0,2,4,6},{9,11,13,15,1,3,5,7},{24,26,28,30,16,18,20,22},{25..., dimensions={0} | all-to-all | bytes 32768 | tf_op jit(solution)/shard_map/all_to_all | solution.py:270
  31.0 0.6 %reduce_sum.11 = f32[512]{0:T(512)} reduce(f32[8,1,512]{2,1,0:T(1,128)S(1)} %all_to_all.11, f32[]{:T(128)} %constant.0.clone.1), dimensions={0,1}, to_apply=%region_0.0 | reduce | flops 3584 | bytes 18436 | tf_op jit(solution)/shard_map/reduce_sum | solution.py:300
  (1 shorter events, 0.0 us)
Async XLA Ops:
  0.0 22.2 %collective-permute-start = (bf16[512,768]{1,0:T(8,128)(2,1)}, bf16[512,768]{1,0:T(8,128)(2,1)S(1)}, u32[]{:S(2)}, u32[]{:S(2)}) collective-permute-start(bf16[512,768]{1,0:T(8,128)(2,1)} %queries.1), channel_id=1, source_target_pairs={{0,1},{1,0},{2,3},{3,2},{4,5},{5,4},{6,7},{7,6},{8,9},{9,8},{10,11... | collective-permute-start | bytes 2359304 | tf_op jit(solution)/shard_map/ppermute | solution.py:292
  0.5 9.2 %copy-start.1 = (s32[192]{0:T(256)S(1)}, s32[192]{0:T(256)}, u32[]{:S(2)}) copy-start(s32[192]{0:T(256)} %param.18) | copy-start | bytes 2308
  0.5 21.8 %copy-start = (bf16[512,768]{1,0:T(8,128)(2,1)S(1)}, bf16[512,768]{1,0:T(8,128)(2,1)}, u32[]{:S(2)}) copy-start(bf16[512,768]{1,0:T(8,128)(2,1)} %queries.1) | copy-start | bytes 2359300
  8.0 1.6 %collective-permute-start.1 = (f32[192,384]{1,0:T(8,128)S(1)}, f32[192,384]{1,0:T(8,128)S(1)}, u32[]{:S(2)}, u32[]{:S(2)}) collective-permute-start(f32[192,384]{1,0:T(8,128)S(1)} %project.1.own), channel_id=1, source_target_pairs={{0,1},{1,0},{2,3},{3,2},{4,5},{5,4},{6,7},{7,6},{8,9},{9,8},{10,11... | collective-permute-start | bytes 884744 | tf_op jit(solution)/shard_map/ppermute | solution.py:295

commit v20 on v19

--- a/solution.py
+++ b/solution.py
@@ -171,6 +171,10 @@
     )(*operands)
 
 
+def first_chip(chips):
+    return chips // 2 + 1
+
+
 def two_terms(value):
     high = value.astype(jnp.bfloat16)
     return high, (value - high.astype(jnp.float32)).astype(jnp.bfloat16)
@@ -205,7 +209,7 @@
                 chip_to, inside = divmod(module * half + row, span)
                 count = min(span - inside, half - row)
                 put = slice(label * span + inside, label * span + inside + count)
-                out[(chip_to + chips // 2) % chips, put, :] = packed[row : row + count]
+                out[(chip_to - first_chip(chips)) % chips, put, :] = packed[row : row + count]
                 row += count
 
 
@@ -230,9 +234,9 @@
     core = lax.axis_index("mp")
     chips, height, lanes = received.shape
     span = height // 2
-    middle = chips // 2
-    rows[: middle * height, :] = received[middle:].reshape(middle * height, lanes)
-    rows[middle * height : chips * height, :] = received[:middle].reshape(middle * height, lanes)
+    first = first_chip(chips)
+    rows[: first * height, :] = received[chips - first :].reshape(first * height, lanes)
+    rows[first * height : chips * height, :] = received[: chips - first].reshape((chips - first) * height, lanes)
     rows[chips * height :, :] = jnp.zeros((8, lanes), jnp.float32)
     grads = []
     for at in range(span):
@@ -242,13 +246,13 @@
         grads.append(own + tail)
     terms = jnp.concatenate(two_terms(jnp.concatenate(grads, axis=1)), axis=0)
     coords = queries.shape[1]
-    first = core == 0
-    mine = jnp.where(first, terms[:, :coords], terms[:, coords:])
-    theirs = jnp.where(first, terms[:, coords:], terms[:, :coords])
+    even = core == 0
+    mine = jnp.where(even, terms[:, :coords], terms[:, coords:])
+    theirs = jnp.where(even, terms[:, coords:], terms[:, :coords])
     scores = lax.dot_general(mine, queries[...], NT, preferred_element_type=jnp.float32)
     scores += lax.dot_general(theirs, swapped[...], NT, preferred_element_type=jnp.float32)
     total = scores[:chips] + scores[chips:]
-    out[...] = jnp.concatenate([total[middle:], total[:middle]], axis=0)
+    out[...] = jnp.concatenate([total[first:], total[:first]], axis=0)
 
 
 def partial_scores(queries, swapped, received):
@@ -266,7 +270,7 @@
 
 def to_all(blocks):
     chips = blocks.shape[0]
-    order = [(i + chips // 2) % chips for i in range(chips)]
+    order = [(i + first_chip(chips)) % chips for i in range(chips)]
     return lax.all_to_all(
         blocks, "dp", split_axis=0, concat_axis=0, axis_index_groups=[order], tiled=True
     )

time: 31.8 us -> 30.9 us (0.972)
  blocking collectives: 20.3 us -> 19.4 us
    all_to_all x2, blocking collectives: 20.3 us -> 19.4 us  [to_all(): lax.all_to_all(blocks, 'dp', split_axis=0, concat_axis=0, axis_index_grou...]
  transfers between devices with their start and end apart: 2 -> 2, of which waited for: 1 -> 1; matrix products, arithmetic and copies ran while one was open for 0% -> 0% of each run, Pallas kernels for 25% -> 26%
where the time goes in v20:
time: 30.9 us; the launch traced here: 30.7 us
  blocking collectives  19.4 us (63%)
  Pallas kernels  8.51 us (28%)
  waiting for transfers between devices  1.52 us (5%)
  other arithmetic  0.61 us (2%)
  starting transfers between devices  0.58 us (2%)
    all_to_all x2, blocking collectives, to_all(): lax.all_to_all(blocks, 'dp', split_axis=0, concat_axis=0, axis_index_grou...  19.4 us
    pallas_call x1, Pallas kernels, projections(): pl.pallas_call(project, out_shape=jax.ShapeDtypeStruct((tokens, 6 * width...  7.52 us
    ppermute x1, waiting for transfers between devices, body(): other = lax.ppermute(own, 'mp', swap)  1.52 us
  transfers between devices with their start and end apart: 2, of which 1 were waited for; matrix products, arithmetic and copies ran while one was open for 0% of the time, Pallas kernels for 26%

profile of v20, /device:TPU:0, one launch (start us, length us, event | category | flops | bytes accessed | tf_op | source)
XLA Modules:
  0.0 30.7 jit_solution(18380734060110170293)
XLA Ops:
  0.0 0.5 %collective-permute-start = (bf16[512,768]{1,0:T(8,128)(2,1)}, bf16[512,768]{1,0:T(8,128)(2,1)S(1)}, u32[]{:S(2)}, u32[]{:S(2)}) collective-permute-start(bf16[512,768]{1,0:T(8,128)(2,1)} %queries.1), channel_id=1, source_target_pairs={{0,1},{1,0},{2,3},{3,2},{4,5},{5,4},{6,7},{7,6},{8,9},{9,8},{10,11... | collective-permute-start | bytes 2359304 | tf_op jit(solution)/shard_map/ppermute | solution.py:296
  0.5 0.0 copy-start.1
  0.5 0.0 copy-start
  0.5 7.5 %project.1.own = f32[192,384]{1,0:T(8,128)S(1)} custom-call(bf16[192,4096]{1,0:T(8,128)(2,1)} %inputs.1, bf16[192,7168]{1,0:T(8,128)(2,1)} %gate_pre.1, bf16[192,7168]{1,0:T(8,128)(2,1)} %up_pre.1, bf16[192,7168]{1,0:T(8,128)(2,1)} %hidden_grad.1, bf16[192,4096]{1,0:T(8,128)(2,1)} %out_grad.1, bf16[64,4096]{1,0:T(8,128)(2,1)} %bitcast.14, ...), custom_call_target="tpu_custom_call" | custom-call | flops 830472192 | bytes 11403264 | tf_op jit(solution)/shard_map/project/pallas_call | solution.py:144
  8.0 0.1 collective-permute-start.1
  8.1 1.5 %collective-permute-done.1.other = f32[192,384]{1,0:T(8,128)S(1)} collective-permute-done((f32[192,384]{1,0:T(8,128)S(1)}, f32[192,384]{1,0:T(8,128)S(1)}, u32[]{:S(2)}, u32[]{:S(2)}) %collective-permute-start.1) | collective-permute-done | bytes 294944 | tf_op jit(solution)/shard_map/ppermute | solution.py:299
  9.6 0.0 copy-done.1
  9.6 0.5 %outer.1 = f32[8,24,128]{2,1,0:T(8,128)S(1)} custom-call(f32[192,384]{1,0:T(8,128)S(1)} %project.1.own, f32[192,384]{1,0:T(8,128)S(1)} %collective-permute-done.1.other, s32[1,192]{1,0:T(1,128)S(1)} %bitcast.10), custom_call_target="tpu_custom_call" | custom-call | tf_op jit(solution)/shard_map/outer/pallas_call | solution.py:219
  10.1 11.2 %all_to_all.10.received = f32[8,24,128]{2,1,0:T(8,128)S(1)} all-to-all(f32[8,24,128]{2,1,0:T(8,128)S(1)} %outer.1), channel_id=1, replica_groups={{10,12,14,0,2,4,6,8},{11,13,15,1,3,5,7,9},{26,28,30,16,18,20,22,24},{27..., dimensions={0} | all-to-all | bytes 196608 | tf_op jit(solution)/shard_map/all_to_all | solution.py:274
  21.3 0.0 collective-permute-done.swapped
  21.3 0.0 copy-done
  21.3 0.5 %score.1 = f32[8,512]{1,0:T(8,128)S(1)} custom-call(bf16[512,768]{1,0:T(8,128)(2,1)S(1)} %copy-done, bf16[512,768]{1,0:T(8,128)(2,1)S(1)} %collective-permute-done.swapped, f32[8,24,128]{2,1,0:T(8,128)S(1)} %all_to_all.10.received), custom_call_target="tpu_custom_call" | custom-call | tf_op jit(solution)/shard_map/score/pallas_call | solution.py:260
  21.9 8.2 %all_to_all.11 = f32[8,1,512]{2,1,0:T(1,128)S(1)} all-to-all(f32[8,1,512]{2,1,0:T(1,128)S(1)} %copy.14), channel_id=1, replica_groups={{10,12,14,0,2,4,6,8},{11,13,15,1,3,5,7,9},{26,28,30,16,18,20,22,24},{27..., dimensions={0} | all-to-all | bytes 32768 | tf_op jit(solution)/shard_map/all_to_all | solution.py:274
  30.1 0.6 %reduce_sum.11 = f32[512]{0:T(512)} reduce(f32[8,1,512]{2,1,0:T(1,128)S(1)} %all_to_all.11, f32[]{:T(128)} %constant.0.clone.1), dimensions={0,1}, to_apply=%region_0.0 | reduce | flops 3584 | bytes 18436 | tf_op jit(solution)/shard_map/reduce_sum | solution.py:304
  (1 shorter events, 0.0 us)
Async XLA Ops:
  0.0 21.3 %collective-permute-start = (bf16[512,768]{1,0:T(8,128)(2,1)}, bf16[512,768]{1,0:T(8,128)(2,1)S(1)}, u32[]{:S(2)}, u32[]{:S(2)}) collective-permute-start(bf16[512,768]{1,0:T(8,128)(2,1)} %queries.1), channel_id=1, source_target_pairs={{0,1},{1,0},{2,3},{3,2},{4,5},{5,4},{6,7},{7,6},{8,9},{9,8},{10,11... | collective-permute-start | bytes 2359304 | tf_op jit(solution)/shard_map/ppermute | solution.py:296
  0.5 9.2 %copy-start.1 = (s32[192]{0:T(256)S(1)}, s32[192]{0:T(256)}, u32[]{:S(2)}) copy-start(s32[192]{0:T(256)} %param.18) | copy-start | bytes 2308
  0.5 20.9 %copy-start = (bf16[512,768]{1,0:T(8,128)(2,1)S(1)}, bf16[512,768]{1,0:T(8,128)(2,1)}, u32[]{:S(2)}) copy-start(bf16[512,768]{1,0:T(8,128)(2,1)} %queries.1) | copy-start | bytes 2359300
  8.0 1.6 %collective-permute-start.1 = (f32[192,384]{1,0:T(8,128)S(1)}, f32[192,384]{1,0:T(8,128)S(1)}, u32[]{:S(2)}, u32[]{:S(2)}) collective-permute-start(f32[192,384]{1,0:T(8,128)S(1)} %project.1.own), channel_id=1, source_target_pairs={{0,1},{1,0},{2,3},{3,2},{4,5},{5,4},{6,7},{7,6},{8,9},{9,8},{10,11... | collective-permute-start | bytes 884744 | tf_op jit(solution)/shard_map/ppermute | solution.py:299

commit v21 on v20

--- a/solution.py
+++ b/solution.py
@@ -175,6 +175,10 @@
     return chips // 2 + 1
 
 
+def first_device(chips):
+    return 2 * first_chip(chips) + 1
+
+
 def two_terms(value):
     high = value.astype(jnp.bfloat16)
     return high, (value - high.astype(jnp.float32)).astype(jnp.bfloat16)
@@ -252,14 +256,17 @@
     scores = lax.dot_general(mine, queries[...], NT, preferred_element_type=jnp.float32)
     scores += lax.dot_general(theirs, swapped[...], NT, preferred_element_type=jnp.float32)
     total = scores[:chips] + scores[chips:]
-    out[...] = jnp.concatenate([total[first:], total[:first]], axis=0)
+    for device in range(2 * chips):
+        place = (device - first_device(chips)) % (2 * chips)
+        row = total[device // 2 : device // 2 + 1]
+        out[place : place + 1, :] = jnp.where(core == device % 2, row, 0.0)
 
 
 def partial_scores(queries, swapped, received):
     chips, height, lanes = received.shape
     return pl.pallas_call(
         score,
-        out_shape=jax.ShapeDtypeStruct((chips, queries.shape[0]), jnp.float32),
+        out_shape=jax.ShapeDtypeStruct((2 * chips, queries.shape[0]), jnp.float32),
         in_specs=[pl.BlockSpec(memory_space=pltpu.VMEM)] * 3,
         out_specs=pl.BlockSpec(memory_space=pltpu.VMEM),
         scratch_shapes=[pltpu.VMEM((chips * height + 8, lanes), jnp.float32)],
@@ -268,11 +275,11 @@
     )(queries, swapped, received)
 
 
-def to_all(blocks):
-    chips = blocks.shape[0]
-    order = [(i + first_chip(chips)) % chips for i in range(chips)]
+def to_all(blocks, axes, first):
+    count = blocks.shape[0]
+    order = [(i + first) % count for i in range(count)]
     return lax.all_to_all(
-        blocks, "dp", split_axis=0, concat_axis=0, axis_index_groups=[order], tiled=True
+        blocks, axes, split_axis=0, concat_axis=0, axis_index_groups=[order], tiled=True
     )
 
 
@@ -298,9 +305,9 @@
     own = projections(inputs, gate_pre, up_pre, hidden_grad, out_grad, *bases)
     other = lax.ppermute(own, "mp", swap)
     blocks = example_blocks(chips, own, other, example_ids.reshape(1, -1))
-    received = to_all(blocks)
+    received = to_all(blocks, "dp", first_chip(chips))
     scores = partial_scores(queries, swapped, received)[:, None]
-    pieces = to_all(scores)
+    pieces = to_all(scores, ("dp", "mp"), first_device(chips))
     return jnp.sum(pieces, axis=0)
 
 

time: 30.9 us -> 30.8 us (level)
  no operation moved by 1% of the time
where the time goes in v21:
time: 30.8 us; the launch traced here: 30.6 us
  blocking collectives  19.3 us (63%)
  Pallas kernels  8.53 us (28%)
  waiting for transfers between devices  1.52 us (5%)
  other arithmetic  0.62 us (2%)
  starting transfers between devices  0.58 us (2%)
    all_to_all x2, blocking collectives, to_all(): lax.all_to_all(blocks, axes, split_axis=0, concat_axis=0, axis_index_grou...  19.3 us
    pallas_call x1, Pallas kernels, projections(): pl.pallas_call(project, out_shape=jax.ShapeDtypeStruct((tokens, 6 * width...  7.52 us
    ppermute x1, waiting for transfers between devices, body(): other = lax.ppermute(own, 'mp', swap)  1.52 us
    reduce_sum x1, other arithmetic, body(): return jnp.sum(pieces, axis=0)  0.62 us
  transfers between devices with their start and end apart: 2, of which 1 were waited for; matrix products, arithmetic and copies ran while one was open for 0% of the time, Pallas kernels for 26%

profile of v21, /device:TPU:0, one launch (start us, length us, event | category | flops | bytes accessed | tf_op | source)
XLA Modules:
  0.0 30.6 jit_solution(11863758590677052008)
XLA Ops:
  0.0 0.5 %collective-permute-start = (bf16[512,768]{1,0:T(8,128)(2,1)}, bf16[512,768]{1,0:T(8,128)(2,1)S(1)}, u32[]{:S(2)}, u32[]{:S(2)}) collective-permute-start(bf16[512,768]{1,0:T(8,128)(2,1)} %queries.1), channel_id=1, source_target_pairs={{0,1},{1,0},{2,3},{3,2},{4,5},{5,4},{6,7},{7,6},{8,9},{9,8},{10,11... | collective-permute-start | bytes 2359304 | tf_op jit(solution)/shard_map/ppermute | solution.py:303
  0.5 0.0 copy-start.1
  0.5 0.0 copy-start
  0.5 7.5 %project.1.own = f32[192,384]{1,0:T(8,128)S(1)} custom-call(bf16[192,4096]{1,0:T(8,128)(2,1)} %inputs.1, bf16[192,7168]{1,0:T(8,128)(2,1)} %gate_pre.1, bf16[192,7168]{1,0:T(8,128)(2,1)} %up_pre.1, bf16[192,7168]{1,0:T(8,128)(2,1)} %hidden_grad.1, bf16[192,4096]{1,0:T(8,128)(2,1)} %out_grad.1, bf16[64,4096]{1,0:T(8,128)(2,1)} %bitcast.14, ...), custom_call_target="tpu_custom_call" | custom-call | flops 830472192 | bytes 11403264 | tf_op jit(solution)/shard_map/project/pallas_call | solution.py:144
  8.0 0.1 collective-permute-start.1
  8.1 1.5 %collective-permute-done.1.other = f32[192,384]{1,0:T(8,128)S(1)} collective-permute-done((f32[192,384]{1,0:T(8,128)S(1)}, f32[192,384]{1,0:T(8,128)S(1)}, u32[]{:S(2)}, u32[]{:S(2)}) %collective-permute-start.1) | collective-permute-done | bytes 294944 | tf_op jit(solution)/shard_map/ppermute | solution.py:306
  9.6 0.0 copy-done.1
  9.6 0.5 %outer.1 = f32[8,24,128]{2,1,0:T(8,128)S(1)} custom-call(f32[192,384]{1,0:T(8,128)S(1)} %project.1.own, f32[192,384]{1,0:T(8,128)S(1)} %collective-permute-done.1.other, s32[1,192]{1,0:T(1,128)S(1)} %bitcast.10), custom_call_target="tpu_custom_call" | custom-call | tf_op jit(solution)/shard_map/outer/pallas_call | solution.py:223
  10.1 11.2 %all_to_all.10.received = f32[8,24,128]{2,1,0:T(8,128)S(1)} all-to-all(f32[8,24,128]{2,1,0:T(8,128)S(1)} %outer.1), channel_id=1, replica_groups={{10,12,14,0,2,4,6,8},{11,13,15,1,3,5,7,9},{26,28,30,16,18,20,22,24},{27..., dimensions={0} | all-to-all | bytes 196608 | tf_op jit(solution)/shard_map/all_to_all | solution.py:281
  21.3 0.0 collective-permute-done.swapped
  21.3 0.0 copy-done
  21.3 0.5 %score.1 = f32[16,512]{1,0:T(8,128)S(1)} custom-call(bf16[512,768]{1,0:T(8,128)(2,1)S(1)} %copy-done, bf16[512,768]{1,0:T(8,128)(2,1)S(1)} %collective-permute-done.swapped, f32[8,24,128]{2,1,0:T(8,128)S(1)} %all_to_all.10.received), custom_call_target="tpu_custom_call" | custom-call | tf_op jit(solution)/shard_map/score/pallas_call | solution.py:267
  21.9 8.1 %all_to_all.11 = f32[16,1,512]{2,1,0:T(1,128)S(1)} all-to-all(f32[16,1,512]{2,1,0:T(1,128)S(1)} %copy.14), channel_id=1, replica_groups={{11,12,13,14,15,0,1,2,3,4,5,6,7,8,9,10},{27,28,29,30,31,16,17,18,19,20,..., dimensions={0} | all-to-all | bytes 65536 | tf_op jit(solution)/shard_map/all_to_all | solution.py:281
  30.0 0.6 %reduce_sum.11 = f32[512]{0:T(512)} reduce(f32[16,1,512]{2,1,0:T(1,128)S(1)} %all_to_all.11, f32[]{:T(128)} %constant.0.clone.1), dimensions={0,1}, to_apply=%region_0.0 | reduce | flops 7680 | bytes 34820 | tf_op jit(solution)/shard_map/reduce_sum | solution.py:311
  (1 shorter events, 0.0 us)
Async XLA Ops:
  0.0 21.3 %collective-permute-start = (bf16[512,768]{1,0:T(8,128)(2,1)}, bf16[512,768]{1,0:T(8,128)(2,1)S(1)}, u32[]{:S(2)}, u32[]{:S(2)}) collective-permute-start(bf16[512,768]{1,0:T(8,128)(2,1)} %queries.1), channel_id=1, source_target_pairs={{0,1},{1,0},{2,3},{3,2},{4,5},{5,4},{6,7},{7,6},{8,9},{9,8},{10,11... | collective-permute-start | bytes 2359304 | tf_op jit(solution)/shard_map/ppermute | solution.py:303
  0.5 9.2 %copy-start.1 = (s32[192]{0:T(256)S(1)}, s32[192]{0:T(256)}, u32[]{:S(2)}) copy-start(s32[192]{0:T(256)} %param.18) | copy-start | bytes 2308
  0.5 20.9 %copy-start = (bf16[512,768]{1,0:T(8,128)(2,1)S(1)}, bf16[512,768]{1,0:T(8,128)(2,1)}, u32[]{:S(2)}) copy-start(bf16[512,768]{1,0:T(8,128)(2,1)} %queries.1) | copy-start | bytes 2359300
  8.0 1.6 %collective-permute-start.1 = (f32[192,384]{1,0:T(8,128)S(1)}, f32[192,384]{1,0:T(8,128)S(1)}, u32[]{:S(2)}, u32[]{:S(2)}) collective-permute-start(f32[192,384]{1,0:T(8,128)S(1)} %project.1.own), channel_id=1, source_target_pairs={{0,1},{1,0},{2,3},{3,2},{4,5},{5,4},{6,7},{7,6},{8,9},{9,8},{10,11... | collective-permute-start | bytes 884744 | tf_op jit(solution)/shard_map/ppermute | solution.py:306

commit v22 on v20

--- a/solution.py
+++ b/solution.py
@@ -11,7 +11,7 @@
 STEP = 1024
 TILE = 256
 ROWS = 16
-AHEAD = 3
+AHEAD = 8
 
 
 def project(

time: 30.9 us -> 30.8 us (level)
  no operation moved by 1% of the time
where the time goes in v22:
time: 30.8 us; the launch traced here: 30.6 us
  blocking collectives  19.4 us (63%)
  Pallas kernels  8.43 us (27%)
  waiting for transfers between devices  1.54 us (5%)
  other arithmetic  0.61 us (2%)
  starting transfers between devices  0.57 us (2%)
    all_to_all x2, blocking collectives, to_all(): lax.all_to_all(blocks, 'dp', split_axis=0, concat_axis=0, axis_index_grou...  19.4 us
    pallas_call x1, Pallas kernels, projections(): pl.pallas_call(project, out_shape=jax.ShapeDtypeStruct((tokens, 6 * width...  7.45 us
    ppermute x1, waiting for transfers between devices, body(): other = lax.ppermute(own, 'mp', swap)  1.53 us
  transfers between devices with their start and end apart: 2, of which 1 were waited for; matrix products, arithmetic and copies ran while one was open for 0% of the time, Pallas kernels for 26%

profile of v22, /device:TPU:0, one launch (start us, length us, event | category | flops | bytes accessed | tf_op | source)
XLA Modules:
  0.0 30.6 jit_solution(1570646879090553371)
XLA Ops:
  0.0 0.5 %collective-permute-start = (bf16[512,768]{1,0:T(8,128)(2,1)}, bf16[512,768]{1,0:T(8,128)(2,1)S(1)}, u32[]{:S(2)}, u32[]{:S(2)}) collective-permute-start(bf16[512,768]{1,0:T(8,128)(2,1)} %queries.1), channel_id=1, source_target_pairs={{0,1},{1,0},{2,3},{3,2},{4,5},{5,4},{6,7},{7,6},{8,9},{9,8},{10,11... | collective-permute-start | bytes 2359304 | tf_op jit(solution)/shard_map/ppermute | solution.py:296
  0.5 0.0 copy-start.1
  0.5 0.0 copy-start
  0.5 7.4 %project.1.own = f32[192,384]{1,0:T(8,128)S(1)} custom-call(bf16[192,4096]{1,0:T(8,128)(2,1)} %inputs.1, bf16[192,7168]{1,0:T(8,128)(2,1)} %gate_pre.1, bf16[192,7168]{1,0:T(8,128)(2,1)} %up_pre.1, bf16[192,7168]{1,0:T(8,128)(2,1)} %hidden_grad.1, bf16[192,4096]{1,0:T(8,128)(2,1)} %out_grad.1, bf16[64,4096]{1,0:T(8,128)(2,1)} %bitcast.14, ...), custom_call_target="tpu_custom_call" | custom-call | flops 830472192 | bytes 11403264 | tf_op jit(solution)/shard_map/project/pallas_call | solution.py:144
  7.9 0.1 collective-permute-start.1
  8.0 1.5 %collective-permute-done.1.other = f32[192,384]{1,0:T(8,128)S(1)} collective-permute-done((f32[192,384]{1,0:T(8,128)S(1)}, f32[192,384]{1,0:T(8,128)S(1)}, u32[]{:S(2)}, u32[]{:S(2)}) %collective-permute-start.1) | collective-permute-done | bytes 294944 | tf_op jit(solution)/shard_map/ppermute | solution.py:299
  9.6 0.0 copy-done.1
  9.6 0.5 %outer.1 = f32[8,24,128]{2,1,0:T(8,128)S(1)} custom-call(f32[192,384]{1,0:T(8,128)S(1)} %project.1.own, f32[192,384]{1,0:T(8,128)S(1)} %collective-permute-done.1.other, s32[1,192]{1,0:T(1,128)S(1)} %bitcast.10), custom_call_target="tpu_custom_call" | custom-call | tf_op jit(solution)/shard_map/outer/pallas_call | solution.py:219
  10.0 11.2 %all_to_all.10.received = f32[8,24,128]{2,1,0:T(8,128)S(1)} all-to-all(f32[8,24,128]{2,1,0:T(8,128)S(1)} %outer.1), channel_id=1, replica_groups={{10,12,14,0,2,4,6,8},{11,13,15,1,3,5,7,9},{26,28,30,16,18,20,22,24},{27..., dimensions={0} | all-to-all | bytes 196608 | tf_op jit(solution)/shard_map/all_to_all | solution.py:274
  21.2 0.0 collective-permute-done.swapped
  21.2 0.0 copy-done
  21.2 0.5 %score.1 = f32[8,512]{1,0:T(8,128)S(1)} custom-call(bf16[512,768]{1,0:T(8,128)(2,1)S(1)} %copy-done, bf16[512,768]{1,0:T(8,128)(2,1)S(1)} %collective-permute-done.swapped, f32[8,24,128]{2,1,0:T(8,128)S(1)} %all_to_all.10.received), custom_call_target="tpu_custom_call" | custom-call | tf_op jit(solution)/shard_map/score/pallas_call | solution.py:260
  21.8 8.2 %all_to_all.11 = f32[8,1,512]{2,1,0:T(1,128)S(1)} all-to-all(f32[8,1,512]{2,1,0:T(1,128)S(1)} %copy.14), channel_id=1, replica_groups={{10,12,14,0,2,4,6,8},{11,13,15,1,3,5,7,9},{26,28,30,16,18,20,22,24},{27..., dimensions={0} | all-to-all | bytes 32768 | tf_op jit(solution)/shard_map/all_to_all | solution.py:274
  30.0 0.6 %reduce_sum.11 = f32[512]{0:T(512)} reduce(f32[8,1,512]{2,1,0:T(1,128)S(1)} %all_to_all.11, f32[]{:T(128)} %constant.0.clone.1), dimensions={0,1}, to_apply=%region_0.0 | reduce | flops 3584 | bytes 18436 | tf_op jit(solution)/shard_map/reduce_sum | solution.py:304
  (1 shorter events, 0.0 us)
Async XLA Ops:
  0.0 21.2 %collective-permute-start = (bf16[512,768]{1,0:T(8,128)(2,1)}, bf16[512,768]{1,0:T(8,128)(2,1)S(1)}, u32[]{:S(2)}, u32[]{:S(2)}) collective-permute-start(bf16[512,768]{1,0:T(8,128)(2,1)} %queries.1), channel_id=1, source_target_pairs={{0,1},{1,0},{2,3},{3,2},{4,5},{5,4},{6,7},{7,6},{8,9},{9,8},{10,11... | collective-permute-start | bytes 2359304 | tf_op jit(solution)/shard_map/ppermute | solution.py:296
  0.5 9.1 %copy-start.1 = (s32[192]{0:T(256)S(1)}, s32[192]{0:T(256)}, u32[]{:S(2)}) copy-start(s32[192]{0:T(256)} %param.18) | copy-start | bytes 2308
  0.5 20.8 %copy-start = (bf16[512,768]{1,0:T(8,128)(2,1)S(1)}, bf16[512,768]{1,0:T(8,128)(2,1)}, u32[]{:S(2)}) copy-start(bf16[512,768]{1,0:T(8,128)(2,1)} %queries.1) | copy-start | bytes 2359300
  7.9 1.6 %collective-permute-start.1 = (f32[192,384]{1,0:T(8,128)S(1)}, f32[192,384]{1,0:T(8,128)S(1)}, u32[]{:S(2)}, u32[]{:S(2)}) collective-permute-start(f32[192,384]{1,0:T(8,128)S(1)} %project.1.own), channel_id=1, source_target_pairs={{0,1},{1,0},{2,3},{3,2},{4,5},{5,4},{6,7},{7,6},{8,9},{9,8},{10,11... | collective-permute-start | bytes 884744 | tf_op jit(solution)/shard_map/ppermute | solution.py:299

commit v23 on v22

--- a/solution.py
+++ b/solution.py
@@ -293,10 +293,11 @@
 ):
     chips = lax.axis_size("dp")
     swap = [(0, 1), (1, 0)]
-    swapped = lax.ppermute(queries, "mp", swap)
     bases = [base.T for base in (gate_in, gate_out, up_in, up_out, down_in, down_out)]
     own = projections(inputs, gate_pre, up_pre, hidden_grad, out_grad, *bases)
     other = lax.ppermute(own, "mp", swap)
+    other, queries = lax.optimization_barrier((other, queries))
+    swapped = lax.ppermute(queries, "mp", swap)
     blocks = example_blocks(chips, own, other, example_ids.reshape(1, -1))
     received = to_all(blocks)
     scores = partial_scores(queries, swapped, received)[:, None]

time: 30.8 us -> 30.8 us (level)
  waiting for transfers between devices: 1.54 us -> 1.21 us
  starting transfers between devices: 0.57 us -> 0.89 us
    ppermute x1, starting transfers between devices: 0.11 us -> 0.52 us  [body(): other = lax.ppermute(own, 'mp', swap)]
    ppermute x1, waiting for transfers between devices: 1.53 us -> 1.21 us  [body(): other = lax.ppermute(own, 'mp', swap)]
  transfers between devices with their start and end apart: 2 -> 2, of which waited for: 1 -> 1; matrix products, arithmetic and copies ran while one was open for 0% -> 0% of each run, Pallas kernels for 26% -> 2%
where the time goes in v23:
time: 30.8 us; the launch traced here: 30.6 us
  blocking collectives  19.4 us (63%)
  Pallas kernels  8.42 us (27%)
  waiting for transfers between devices  1.21 us (4%)
  starting transfers between devices  0.89 us (3%)
  other arithmetic  0.61 us (2%)
    all_to_all x2, blocking collectives, to_all(): lax.all_to_all(blocks, 'dp', split_axis=0, concat_axis=0, axis_index_grou...  19.4 us
    pallas_call x1, Pallas kernels, projections(): pl.pallas_call(project, out_shape=jax.ShapeDtypeStruct((tokens, 6 * width...  7.44 us
    ppermute x1, waiting for transfers between devices, body(): other = lax.ppermute(own, 'mp', swap)  1.21 us
  transfers between devices with their start and end apart: 2, of which 1 were waited for; matrix products, arithmetic and copies ran while one was open for 0% of the time, Pallas kernels for 2%

profile of v23, /device:TPU:0, one launch (start us, length us, event | category | flops | bytes accessed | tf_op | source)
XLA Modules:
  0.0 30.6 jit_solution(13054119272306668357)
XLA Ops:
  0.0 0.0 copy-start
  0.0 0.0 copy-start.1
  0.0 7.4 %project.1.own = f32[192,384]{1,0:T(8,128)S(1)} custom-call(bf16[192,4096]{1,0:T(8,128)(2,1)} %inputs.1, bf16[192,7168]{1,0:T(8,128)(2,1)} %gate_pre.1, bf16[192,7168]{1,0:T(8,128)(2,1)} %up_pre.1, bf16[192,7168]{1,0:T(8,128)(2,1)} %hidden_grad.1, bf16[192,4096]{1,0:T(8,128)(2,1)} %out_grad.1, bf16[64,4096]{1,0:T(8,128)(2,1)} %bitcast.14, ...), custom_call_target="tpu_custom_call" | custom-call | flops 830472192 | bytes 11403264 | tf_op jit(solution)/shard_map/project/pallas_call | solution.py:144
  7.4 0.5 %collective-permute-start = (f32[192,384]{1,0:T(8,128)S(1)}, f32[192,384]{1,0:T(8,128)S(1)}, u32[]{:S(2)}, u32[]{:S(2)}) collective-permute-start(f32[192,384]{1,0:T(8,128)S(1)} %project.1.own), channel_id=1, source_target_pairs={{0,1},{1,0},{2,3},{3,2},{4,5},{5,4},{6,7},{7,6},{8,9},{9,8},{10,11... | collective-permute-start | bytes 884744 | tf_op jit(solution)/shard_map/ppermute | solution.py:298
  8.0 1.2 %collective-permute-done.other = f32[192,384]{1,0:T(8,128)S(1)} collective-permute-done((f32[192,384]{1,0:T(8,128)S(1)}, f32[192,384]{1,0:T(8,128)S(1)}, u32[]{:S(2)}, u32[]{:S(2)}) %collective-permute-start) | collective-permute-done | bytes 294944 | tf_op jit(solution)/shard_map/ppermute | solution.py:298
  9.2 0.0 copy-done
  9.2 0.4 %collective-permute-start.1 = (bf16[512,768]{1,0:T(8,128)(2,1)S(1)}, bf16[512,768]{1,0:T(8,128)(2,1)S(1)}, u32[]{:S(2)}, u32[]{:S(2)}) collective-permute-start(bf16[512,768]{1,0:T(8,128)(2,1)S(1)} %copy-done), channel_id=1, source_target_pairs={{0,1},{1,0},{2,3},{3,2},{4,5},{5,4},{6,7},{7,6},{8,9},{9,8},{10,11... | collective-permute-start | bytes 2359304 | tf_op jit(solution)/shard_map/ppermute | solution.py:300
  9.6 0.0 copy-done.1
  9.6 0.5 %outer.1 = f32[8,24,128]{2,1,0:T(8,128)S(1)} custom-call(f32[192,384]{1,0:T(8,128)S(1)} %project.1.own, f32[192,384]{1,0:T(8,128)S(1)} %collective-permute-done.other, s32[1,192]{1,0:T(1,128)S(1)} %bitcast.10), custom_call_target="tpu_custom_call" | custom-call | tf_op jit(solution)/shard_map/outer/pallas_call | solution.py:219
  10.0 11.2 %all_to_all.10.received = f32[8,24,128]{2,1,0:T(8,128)S(1)} all-to-all(f32[8,24,128]{2,1,0:T(8,128)S(1)} %outer.1), channel_id=1, replica_groups={{10,12,14,0,2,4,6,8},{11,13,15,1,3,5,7,9},{26,28,30,16,18,20,22,24},{27..., dimensions={0} | all-to-all | bytes 196608 | tf_op jit(solution)/shard_map/all_to_all | solution.py:274
  21.2 0.0 collective-permute-done.1.swapped
  21.2 0.5 %score.1 = f32[8,512]{1,0:T(8,128)S(1)} custom-call(bf16[512,768]{1,0:T(8,128)(2,1)S(1)} %copy-done, bf16[512,768]{1,0:T(8,128)(2,1)S(1)} %collective-permute-done.1.swapped, f32[8,24,128]{2,1,0:T(8,128)S(1)} %all_to_all.10.received), custom_call_target="tpu_custom_call" | custom-call | tf_op jit(solution)/shard_map/score/pallas_call | solution.py:260
  21.8 8.2 %all_to_all.11 = f32[8,1,512]{2,1,0:T(1,128)S(1)} all-to-all(f32[8,1,512]{2,1,0:T(1,128)S(1)} %copy.14), channel_id=1, replica_groups={{10,12,14,0,2,4,6,8},{11,13,15,1,3,5,7,9},{26,28,30,16,18,20,22,24},{27..., dimensions={0} | all-to-all | bytes 32768 | tf_op jit(solution)/shard_map/all_to_all | solution.py:274
  30.0 0.6 %reduce_sum.11 = f32[512]{0:T(512)} reduce(f32[8,1,512]{2,1,0:T(1,128)S(1)} %all_to_all.11, f32[]{:T(128)} %constant.0.clone.1), dimensions={0,1}, to_apply=%region_0.0 | reduce | flops 3584 | bytes 18436 | tf_op jit(solution)/shard_map/reduce_sum | solution.py:305
  (1 shorter events, 0.0 us)
Async XLA Ops:
  0.0 9.2 %copy-start = (bf16[512,768]{1,0:T(8,128)(2,1)S(1)}, bf16[512,768]{1,0:T(8,128)(2,1)}, u32[]{:S(2)}) copy-start(bf16[512,768]{1,0:T(8,128)(2,1)} %queries) | copy-start | bytes 2359300
  0.0 9.6 %copy-start.1 = (s32[192]{0:T(256)S(1)}, s32[192]{0:T(256)}, u32[]{:S(2)}) copy-start(s32[192]{0:T(256)} %param.18) | copy-start | bytes 2308
  7.4 1.7 %collective-permute-start = (f32[192,384]{1,0:T(8,128)S(1)}, f32[192,384]{1,0:T(8,128)S(1)}, u32[]{:S(2)}, u32[]{:S(2)}) collective-permute-start(f32[192,384]{1,0:T(8,128)S(1)} %project.1.own), channel_id=1, source_target_pairs={{0,1},{1,0},{2,3},{3,2},{4,5},{5,4},{6,7},{7,6},{8,9},{9,8},{10,11... | collective-permute-start | bytes 884744 | tf_op jit(solution)/shard_map/ppermute | solution.py:298
  9.2 12.0 %collective-permute-start.1 = (bf16[512,768]{1,0:T(8,128)(2,1)S(1)}, bf16[512,768]{1,0:T(8,128)(2,1)S(1)}, u32[]{:S(2)}, u32[]{:S(2)}) collective-permute-start(bf16[512,768]{1,0:T(8,128)(2,1)S(1)} %copy-done), channel_id=1, source_target_pairs={{0,1},{1,0},{2,3},{3,2},{4,5},{5,4},{6,7},{7,6},{8,9},{9,8},{10,11... | collective-permute-start | bytes 2359304 | tf_op jit(solution)/shard_map/ppermute | solution.py:300

commit v24 on v22

--- a/solution.py
+++ b/solution.py
@@ -171,8 +171,9 @@
     )(*operands)
 
 
-def first_chip(chips):
-    return chips // 2 + 1
+def listed(chips):
+    first = chips // 2 + 1
+    return [first] + [chip for chip in range(chips) if chip != first]
 
 
 def two_terms(value):
@@ -185,6 +186,7 @@
     width = own.shape[1] // 6
     half = width // 2
     span = 3 * half // chips
+    order = listed(chips)
     summed[...] = (own[...] + other[...]).T
     own_label = 2 * chip + core
     tail_label = jnp.where(core == 1, 2 * chip - 1, -1)
@@ -209,7 +211,7 @@
                 chip_to, inside = divmod(module * half + row, span)
                 count = min(span - inside, half - row)
                 put = slice(label * span + inside, label * span + inside + count)
-                out[(chip_to - first_chip(chips)) % chips, put, :] = packed[row : row + count]
+                out[order.index(chip_to), put, :] = packed[row : row + count]
                 row += count
 
 
@@ -234,9 +236,9 @@
     core = lax.axis_index("mp")
     chips, height, lanes = received.shape
     span = height // 2
-    first = first_chip(chips)
-    rows[: first * height, :] = received[chips - first :].reshape(first * height, lanes)
-    rows[first * height : chips * height, :] = received[: chips - first].reshape((chips - first) * height, lanes)
+    order = listed(chips)
+    for place, chip in enumerate(order):
+        rows[chip * height : (chip + 1) * height, :] = received[place]
     rows[chips * height :, :] = jnp.zeros((8, lanes), jnp.float32)
     grads = []
     for at in range(span):
@@ -252,7 +254,7 @@
     scores = lax.dot_general(mine, queries[...], NT, preferred_element_type=jnp.float32)
     scores += lax.dot_general(theirs, swapped[...], NT, preferred_element_type=jnp.float32)
     total = scores[:chips] + scores[chips:]
-    out[...] = jnp.concatenate([total[first:], total[:first]], axis=0)
+    out[...] = jnp.concatenate([total[chip : chip + 1] for chip in order], axis=0)
 
 
 def partial_scores(queries, swapped, received):
@@ -270,9 +272,8 @@
 
 def to_all(blocks):
     chips = blocks.shape[0]
-    order = [(i + first_chip(chips)) % chips for i in range(chips)]
     return lax.all_to_all(
-        blocks, "dp", split_axis=0, concat_axis=0, axis_index_groups=[order], tiled=True
+        blocks, "dp", split_axis=0, concat_axis=0, axis_index_groups=[listed(chips)], tiled=True
     )
 
 

time: 30.8 us -> 30.9 us (level)
  no operation moved by 1% of the time
where the time goes in v24:
time: 30.9 us; the launch traced here: 30.7 us
  blocking collectives  19.5 us (63%)
  Pallas kernels  8.43 us (27%)
  waiting for transfers between devices  1.54 us (5%)
  other arithmetic  0.61 us (2%)
  starting transfers between devices  0.57 us (2%)
    all_to_all x2, blocking collectives, to_all(): lax.all_to_all(blocks, 'dp', split_axis=0, concat_axis=0, axis_index_grou...  19.5 us
    pallas_call x1, Pallas kernels, projections(): pl.pallas_call(project, out_shape=jax.ShapeDtypeStruct((tokens, 6 * width...  7.45 us
    ppermute x1, waiting for transfers between devices, body(): other = lax.ppermute(own, 'mp', swap)  1.53 us
  transfers between devices with their start and end apart: 2, of which 1 were waited for; matrix products, arithmetic and copies ran while one was open for 0% of the time, Pallas kernels for 26%

profile of v24, /device:TPU:0, one launch (start us, length us, event | category | flops | bytes accessed | tf_op | source)
XLA Modules:
  0.0 30.7 jit_solution(11398027924125893908)
XLA Ops:
  0.0 0.5 %collective-permute-start = (bf16[512,768]{1,0:T(8,128)(2,1)}, bf16[512,768]{1,0:T(8,128)(2,1)S(1)}, u32[]{:S(2)}, u32[]{:S(2)}) collective-permute-start(bf16[512,768]{1,0:T(8,128)(2,1)} %queries.1), channel_id=1, source_target_pairs={{0,1},{1,0},{2,3},{3,2},{4,5},{5,4},{6,7},{7,6},{8,9},{9,8},{10,11... | collective-permute-start | bytes 2359304 | tf_op jit(solution)/shard_map/ppermute | solution.py:297
  0.5 0.0 copy-start.1
  0.5 0.0 copy-start
  0.5 7.4 %project.1.own = f32[192,384]{1,0:T(8,128)S(1)} custom-call(bf16[192,4096]{1,0:T(8,128)(2,1)} %inputs.1, bf16[192,7168]{1,0:T(8,128)(2,1)} %gate_pre.1, bf16[192,7168]{1,0:T(8,128)(2,1)} %up_pre.1, bf16[192,7168]{1,0:T(8,128)(2,1)} %hidden_grad.1, bf16[192,4096]{1,0:T(8,128)(2,1)} %out_grad.1, bf16[64,4096]{1,0:T(8,128)(2,1)} %bitcast.14, ...), custom_call_target="tpu_custom_call" | custom-call | flops 830472192 | bytes 11403264 | tf_op jit(solution)/shard_map/project/pallas_call | solution.py:144
  7.9 0.1 collective-permute-start.1
  8.0 1.5 %collective-permute-done.1.other = f32[192,384]{1,0:T(8,128)S(1)} collective-permute-done((f32[192,384]{1,0:T(8,128)S(1)}, f32[192,384]{1,0:T(8,128)S(1)}, u32[]{:S(2)}, u32[]{:S(2)}) %collective-permute-start.1) | collective-permute-done | bytes 294944 | tf_op jit(solution)/shard_map/ppermute | solution.py:300
  9.6 0.0 copy-done.1
  9.6 0.5 %outer.1 = f32[8,24,128]{2,1,0:T(8,128)S(1)} custom-call(f32[192,384]{1,0:T(8,128)S(1)} %project.1.own, f32[192,384]{1,0:T(8,128)S(1)} %collective-permute-done.1.other, s32[1,192]{1,0:T(1,128)S(1)} %bitcast.10), custom_call_target="tpu_custom_call" | custom-call | tf_op jit(solution)/shard_map/outer/pallas_call | solution.py:221
  10.0 11.0 %all_to_all.10.received = f32[8,24,128]{2,1,0:T(8,128)S(1)} all-to-all(f32[8,24,128]{2,1,0:T(8,128)S(1)} %outer.1), channel_id=1, replica_groups={{10,0,2,4,6,8,12,14},{11,1,3,5,7,9,13,15},{26,16,18,20,22,24,28,30},{27..., dimensions={0} | all-to-all | bytes 196608 | tf_op jit(solution)/shard_map/all_to_all | solution.py:275
  21.0 0.0 collective-permute-done.swapped
  21.0 0.0 copy-done
  21.0 0.5 %score.1 = f32[8,512]{1,0:T(8,128)S(1)} custom-call(bf16[512,768]{1,0:T(8,128)(2,1)S(1)} %copy-done, bf16[512,768]{1,0:T(8,128)(2,1)S(1)} %collective-permute-done.swapped, f32[8,24,128]{2,1,0:T(8,128)S(1)} %all_to_all.10.received), custom_call_target="tpu_custom_call" | custom-call | tf_op jit(solution)/shard_map/score/pallas_call | solution.py:262
  21.6 8.5 %all_to_all.11 = f32[8,1,512]{2,1,0:T(1,128)S(1)} all-to-all(f32[8,1,512]{2,1,0:T(1,128)S(1)} %copy.14), channel_id=1, replica_groups={{10,0,2,4,6,8,12,14},{11,1,3,5,7,9,13,15},{26,16,18,20,22,24,28,30},{27..., dimensions={0} | all-to-all | bytes 32768 | tf_op jit(solution)/shard_map/all_to_all | solution.py:275
  30.1 0.6 %reduce_sum.11 = f32[512]{0:T(512)} reduce(f32[8,1,512]{2,1,0:T(1,128)S(1)} %all_to_all.11, f32[]{:T(128)} %constant.0.clone.1), dimensions={0,1}, to_apply=%region_0.0 | reduce | flops 3584 | bytes 18436 | tf_op jit(solution)/shard_map/reduce_sum | solution.py:305
  (1 shorter events, 0.0 us)
Async XLA Ops:
  0.0 21.0 %collective-permute-start = (bf16[512,768]{1,0:T(8,128)(2,1)}, bf16[512,768]{1,0:T(8,128)(2,1)S(1)}, u32[]{:S(2)}, u32[]{:S(2)}) collective-permute-start(bf16[512,768]{1,0:T(8,128)(2,1)} %queries.1), channel_id=1, source_target_pairs={{0,1},{1,0},{2,3},{3,2},{4,5},{5,4},{6,7},{7,6},{8,9},{9,8},{10,11... | collective-permute-start | bytes 2359304 | tf_op jit(solution)/shard_map/ppermute | solution.py:297
  0.5 9.1 %copy-start.1 = (s32[192]{0:T(256)S(1)}, s32[192]{0:T(256)}, u32[]{:S(2)}) copy-start(s32[192]{0:T(256)} %param.18) | copy-start | bytes 2308
  0.5 20.5 %copy-start = (bf16[512,768]{1,0:T(8,128)(2,1)S(1)}, bf16[512,768]{1,0:T(8,128)(2,1)}, u32[]{:S(2)}) copy-start(bf16[512,768]{1,0:T(8,128)(2,1)} %queries.1) | copy-start | bytes 2359300
  7.9 1.6 %collective-permute-start.1 = (f32[192,384]{1,0:T(8,128)S(1)}, f32[192,384]{1,0:T(8,128)S(1)}, u32[]{:S(2)}, u32[]{:S(2)}) collective-permute-start(f32[192,384]{1,0:T(8,128)S(1)} %project.1.own), channel_id=1, source_target_pairs={{0,1},{1,0},{2,3},{3,2},{4,5},{5,4},{6,7},{7,6},{8,9},{9,8},{10,11... | collective-permute-start | bytes 884744 | tf_op jit(solution)/shard_map/ppermute | solution.py:300

commit v25 on v21

--- a/solution.py
+++ b/solution.py
@@ -11,7 +11,7 @@
 STEP = 1024
 TILE = 256
 ROWS = 16
-AHEAD = 3
+AHEAD = 8
 
 
 def project(
@@ -26,7 +26,8 @@
     up_out,
     down_in,
     down_out,
-    out,
+    kept,
+    given,
     v_inputs,
     v_gate,
     v_up,
@@ -128,9 +129,15 @@
             model_left = left - edges[first_model]
             if 0 <= model_left < model:
                 model_dots(model_left)
-    out[:, : 2 * width] = sum_in[...]
-    out[:, 2 * width : 4 * width] = jnp.concatenate([0.5 * sums[0], sums[1]], axis=1)
-    out[:, 4 * width :] = jnp.concatenate([sums[2], sums[3]], axis=1)
+    core = lax.axis_index("mp")
+    half = tokens // 2
+    for out, which in ((kept, core), (given, 1 - core)):
+        rows = pl.ds(pl.multiple_of(which * half, half), half)
+        out[:, : 2 * width] = sum_in[rows, :]
+        out[:, 2 * width : 4 * width] = jnp.concatenate(
+            [0.5 * sums[0, rows, :], sums[1, rows, :]], axis=1
+        )
+        out[:, 4 * width :] = jnp.concatenate([sums[2, rows, :], sums[3, rows, :]], axis=1)
 
 
 def projections(*operands):
@@ -143,9 +150,9 @@
     bf16 = jnp.bfloat16
     return pl.pallas_call(
         project,
-        out_shape=jax.ShapeDtypeStruct((tokens, 6 * width), jnp.float32),
+        out_shape=[jax.ShapeDtypeStruct((tokens // 2, 6 * width), jnp.float32)] * 2,
         in_specs=[pl.BlockSpec(memory_space=pltpu.HBM)] * len(operands),
-        out_specs=pl.BlockSpec(memory_space=pltpu.VMEM),
+        out_specs=[pl.BlockSpec(memory_space=pltpu.VMEM)] * 2,
         scratch_shapes=[
             pltpu.VMEM((tokens, model), bf16),
             pltpu.VMEM((tokens, hidden), bf16),
@@ -190,9 +197,9 @@
     half = width // 2
     span = 3 * half // chips
     summed[...] = (own[...] + other[...]).T
-    own_label = 2 * chip + core
-    tail_label = jnp.where(core == 1, 2 * chip - 1, -1)
-    masks = [(ids[...] == label).astype(jnp.float32) for label in (tail_label, own_label)]
+    label = 2 * chip + core
+    mine = ids[pl.ds(core, 1), :]
+    masks = [(mine == each).astype(jnp.float32) for each in (label - 1, label)]
     lane = lax.broadcasted_iota(jnp.int32, (half, 2 * width), 1)
     for module, (left, right) in enumerate(((0, 2), (1, 3), (4, 5))):
         factor = summed[left * width : (left + 1) * width, :]
@@ -241,25 +248,29 @@
     first = first_chip(chips)
     rows[: first * height, :] = received[chips - first :].reshape(first * height, lanes)
     rows[first * height : chips * height, :] = received[: chips - first].reshape((chips - first) * height, lanes)
-    rows[chips * height :, :] = jnp.zeros((8, lanes), jnp.float32)
     grads = []
-    for at in range(span):
-        own = rows[pl.ds(span + at, chips, stride=height), :]
-        tail = rows[pl.ds(at, chips, stride=height), :]
-        tail = jnp.concatenate([tail[1:], jnp.zeros_like(tail[:1])], axis=0)
-        grads.append(own + tail)
-    terms = jnp.concatenate(two_terms(jnp.concatenate(grads, axis=1)), axis=0)
+    for label in range(2):
+        parts = [rows[pl.ds(label * span + at, chips, stride=height), :] for at in range(span)]
+        grads.append(jnp.concatenate(parts, axis=1))
+    terms = jnp.concatenate(two_terms(jnp.concatenate(grads, axis=0)), axis=0)
     coords = queries.shape[1]
     even = core == 0
     mine = jnp.where(even, terms[:, :coords], terms[:, coords:])
     theirs = jnp.where(even, terms[:, coords:], terms[:, :coords])
     scores = lax.dot_general(mine, queries[...], NT, preferred_element_type=jnp.float32)
     scores += lax.dot_general(theirs, swapped[...], NT, preferred_element_type=jnp.float32)
-    total = scores[:chips] + scores[chips:]
+    total = scores[: 2 * chips] + scores[2 * chips :]
+    none = jnp.zeros_like(total[:1])
+    tails = [total[chip : chip + 1] for chip in range(chips)] + [none]
+    owns = [total[chips + chip : chips + chip + 1] for chip in range(chips)]
     for device in range(2 * chips):
         place = (device - first_device(chips)) % (2 * chips)
-        row = total[device // 2 : device // 2 + 1]
-        out[place : place + 1, :] = jnp.where(core == device % 2, row, 0.0)
+        chip = device // 2
+        if device % 2 == 0:
+            row = jnp.where(even, owns[chip], tails[chip])
+        else:
+            row = jnp.where(even, tails[chip + 1], owns[chip])
+        out[place : place + 1, :] = row
 
 
 def partial_scores(queries, swapped, received):
@@ -269,7 +280,7 @@
         out_shape=jax.ShapeDtypeStruct((2 * chips, queries.shape[0]), jnp.float32),
         in_specs=[pl.BlockSpec(memory_space=pltpu.VMEM)] * 3,
         out_specs=pl.BlockSpec(memory_space=pltpu.VMEM),
-        scratch_shapes=[pltpu.VMEM((chips * height + 8, lanes), jnp.float32)],
+        scratch_shapes=[pltpu.VMEM((chips * height, lanes), jnp.float32)],
         compiler_params=pltpu.CompilerParams(vmem_limit_bytes=6 * 2**20),
         name="score",
     )(queries, swapped, received)
@@ -302,9 +313,9 @@
     swap = [(0, 1), (1, 0)]
     swapped = lax.ppermute(queries, "mp", swap)
     bases = [base.T for base in (gate_in, gate_out, up_in, up_out, down_in, down_out)]
-    own = projections(inputs, gate_pre, up_pre, hidden_grad, out_grad, *bases)
-    other = lax.ppermute(own, "mp", swap)
-    blocks = example_blocks(chips, own, other, example_ids.reshape(1, -1))
+    own, given = projections(inputs, gate_pre, up_pre, hidden_grad, out_grad, *bases)
+    other = lax.ppermute(given, "mp", swap)
+    blocks = example_blocks(chips, own, other, example_ids.reshape(2, -1))
     received = to_all(blocks, "dp", first_chip(chips))
     scores = partial_scores(queries, swapped, received)[:, None]
     pieces = to_all(scores, ("dp", "mp"), first_device(chips))

time: 30.8 us -> 30.6 us (level)
  no operation moved by 1% of the time
where the time goes in v25:
time: 30.6 us; the launch traced here: 30.4 us
  blocking collectives  19.3 us (63%)
  Pallas kernels  8.51 us (28%)
  waiting for transfers between devices  1.24 us (4%)
  other arithmetic  0.62 us (2%)
  starting transfers between devices  0.57 us (2%)
    all_to_all x2, blocking collectives, to_all(): lax.all_to_all(blocks, axes, split_axis=0, concat_axis=0, axis_index_grou...  19.3 us
    pallas_call x1, Pallas kernels, projections(): pl.pallas_call(project, out_shape=[jax.ShapeDtypeStruct((tokens // 2, 6 *...  7.5 us
    ppermute x1, waiting for transfers between devices, body(): other = lax.ppermute(given, 'mp', swap)  1.24 us
    reduce_sum x1, other arithmetic, body(): return jnp.sum(pieces, axis=0)  0.62 us
  transfers between devices with their start and end apart: 2, of which 1 were waited for; matrix products, arithmetic and copies ran while one was open for 0% of the time, Pallas kernels for 26%

profile of v25, /device:TPU:0, one launch (start us, length us, event | category | flops | bytes accessed | tf_op | source)
XLA Modules:
  0.0 30.4 jit_solution(3122964198223850808)
XLA Ops:
  0.0 0.5 %collective-permute-start = (bf16[512,768]{1,0:T(8,128)(2,1)}, bf16[512,768]{1,0:T(8,128)(2,1)S(1)}, u32[]{:S(2)}, u32[]{:S(2)}) collective-permute-start(bf16[512,768]{1,0:T(8,128)(2,1)} %queries.1), channel_id=1, source_target_pairs={{0,1},{1,0},{2,3},{3,2},{4,5},{5,4},{6,7},{7,6},{8,9},{9,8},{10,11... | collective-permute-start | bytes 2359304 | tf_op jit(solution)/shard_map/ppermute | solution.py:314
  0.5 0.0 copy-start.1
  0.5 0.0 copy-start
  0.5 7.5 %project.1 = (f32[96,384]{1,0:T(8,128)S(1)}, f32[96,384]{1,0:T(8,128)S(1)}) custom-call(bf16[192,4096]{1,0:T(8,128)(2,1)} %inputs.1, bf16[192,7168]{1,0:T(8,128)(2,1)} %gate_pre.1, bf16[192,7168]{1,0:T(8,128)(2,1)} %up_pre.1, bf16[192,7168]{1,0:T(8,128)(2,1)} %hidden_grad.1, bf16[192,4096]{1,0:T(8,128)(2,1)} %out_grad.1, bf16[64,4096]{1,0:T(8,128)(2,1)} %bitcast.12, ...), custom_call_target="tpu_custom_call" | custom-call | flops 830472192 | bytes 11403264 | tf_op jit(solution)/shard_map/project/pallas_call | solution.py:151
  8.0 0.1 collective-permute-start.1
  8.1 0.0 copy-done.1
  8.1 0.1 reshape.4.ids
  8.2 1.2 %collective-permute-done.1.other = f32[96,384]{1,0:T(8,128)S(1)} collective-permute-done((f32[96,384]{1,0:T(8,128)S(1)}, f32[96,384]{1,0:T(8,128)S(1)}, u32[]{:S(2)}, u32[]{:S(2)}) %collective-permute-start.1) | collective-permute-done | bytes 147488 | tf_op jit(solution)/shard_map/ppermute | solution.py:317
  9.4 0.4 %outer.1 = f32[8,24,128]{2,1,0:T(8,128)S(1)} custom-call(f32[96,384]{1,0:T(8,128)S(1)} %get-tuple-element.7.own, f32[96,384]{1,0:T(8,128)S(1)} %collective-permute-done.1.other, s32[2,96]{1,0:T(2,128)S(1)} %reshape.4.ids), custom_call_target="tpu_custom_call" | custom-call | tf_op jit(solution)/shard_map/outer/pallas_call | solution.py:230
  9.9 11.2 %all_to_all.10.received = f32[8,24,128]{2,1,0:T(8,128)S(1)} all-to-all(f32[8,24,128]{2,1,0:T(8,128)S(1)} %outer.1), channel_id=1, replica_groups={{10,12,14,0,2,4,6,8},{11,13,15,1,3,5,7,9},{26,28,30,16,18,20,22,24},{27..., dimensions={0} | all-to-all | bytes 196608 | tf_op jit(solution)/shard_map/all_to_all | solution.py:292
  21.1 0.0 collective-permute-done.swapped
  21.1 0.0 copy-done
  21.1 0.6 %score.1 = f32[16,512]{1,0:T(8,128)S(1)} custom-call(bf16[512,768]{1,0:T(8,128)(2,1)S(1)} %copy-done, bf16[512,768]{1,0:T(8,128)(2,1)S(1)} %collective-permute-done.swapped, f32[8,24,128]{2,1,0:T(8,128)S(1)} %all_to_all.10.received), custom_call_target="tpu_custom_call" | custom-call | tf_op jit(solution)/shard_map/score/pallas_call | solution.py:278
  21.7 8.1 %all_to_all.11 = f32[16,1,512]{2,1,0:T(1,128)S(1)} all-to-all(f32[16,1,512]{2,1,0:T(1,128)S(1)} %copy.14), channel_id=1, replica_groups={{11,12,13,14,15,0,1,2,3,4,5,6,7,8,9,10},{27,28,29,30,31,16,17,18,19,20,..., dimensions={0} | all-to-all | bytes 65536 | tf_op jit(solution)/shard_map/all_to_all | solution.py:292
  29.8 0.6 %reduce_sum.11 = f32[512]{0:T(512)} reduce(f32[16,1,512]{2,1,0:T(1,128)S(1)} %all_to_all.11, f32[]{:T(128)} %constant.0.clone.1), dimensions={0,1}, to_apply=%region_0.0 | reduce | flops 7680 | bytes 34820 | tf_op jit(solution)/shard_map/reduce_sum | solution.py:322
  (1 shorter events, 0.0 us)
Async XLA Ops:
  0.0 21.1 %collective-permute-start = (bf16[512,768]{1,0:T(8,128)(2,1)}, bf16[512,768]{1,0:T(8,128)(2,1)S(1)}, u32[]{:S(2)}, u32[]{:S(2)}) collective-permute-start(bf16[512,768]{1,0:T(8,128)(2,1)} %queries.1), channel_id=1, source_target_pairs={{0,1},{1,0},{2,3},{3,2},{4,5},{5,4},{6,7},{7,6},{8,9},{9,8},{10,11... | collective-permute-start | bytes 2359304 | tf_op jit(solution)/shard_map/ppermute | solution.py:314
  0.5 7.6 %copy-start.1 = (s32[192]{0:T(256)S(1)}, s32[192]{0:T(256)}, u32[]{:S(2)}) copy-start(s32[192]{0:T(256)} %param.18) | copy-start | bytes 2308
  0.5 20.6 %copy-start = (bf16[512,768]{1,0:T(8,128)(2,1)S(1)}, bf16[512,768]{1,0:T(8,128)(2,1)}, u32[]{:S(2)}) copy-start(bf16[512,768]{1,0:T(8,128)(2,1)} %queries.1) | copy-start | bytes 2359300
  8.0 1.4 %collective-permute-start.1 = (f32[96,384]{1,0:T(8,128)S(1)}, f32[96,384]{1,0:T(8,128)S(1)}, u32[]{:S(2)}, u32[]{:S(2)}) collective-permute-start(f32[96,384]{1,0:T(8,128)S(1)} %get-tuple-element.8), channel_id=1, source_target_pairs={{0,1},{1,0},{2,3},{3,2},{4,5},{5,4},{6,7},{7,6},{8,9},{9,8},{10,11... | collective-permute-start | bytes 442376 | tf_op jit(solution)/shard_map/ppermute | solution.py:317

commit v26 on v25

--- a/solution.py
+++ b/solution.py
@@ -76,9 +76,10 @@
         groups.append(pairs)
 
     def start(step):
-        for (source, target), low, length in groups[step]:
+        for index, ((source, target), low, length) in enumerate(groups[step]):
             at = pl.ds(low, length)
-            pltpu.make_async_copy(source.at[:, at], target.at[:, at], sems.at[step]).start()
+            copy = pltpu.make_async_copy(source.at[:, at], target.at[:, at], sems.at[step])
+            copy.start(priority=index % 2)
 
     def wait(step):
         count = sum(source.shape[0] * length for (source, _), _, length in groups[step])

time: 30.6 us -> 32.3 us (1.056)
  Pallas kernels: 8.51 us -> 10.3 us
    pallas_call x1, Pallas kernels: 7.5 us -> 9.25 us  [projections(): pl.pallas_call(project, out_shape=[jax.ShapeDtypeStruct((tokens // 2, 6 *...]
  transfers between devices with their start and end apart: 2 -> 2, of which waited for: 1 -> 1; matrix products, arithmetic and copies ran while one was open for 0% -> 0% of each run, Pallas kernels for 26% -> 30%
where the time goes in v26:
time: 32.3 us; the launch traced here: 32.1 us
  blocking collectives  19.3 us (60%)
  Pallas kernels  10.3 us (32%)
  waiting for transfers between devices  1.23 us (4%)
  other arithmetic  0.62 us (2%)
  starting transfers between devices  0.57 us (2%)
    all_to_all x2, blocking collectives, to_all(): lax.all_to_all(blocks, axes, split_axis=0, concat_axis=0, axis_index_grou...  19.3 us
    pallas_call x1, Pallas kernels, projections(): pl.pallas_call(project, out_shape=[jax.ShapeDtypeStruct((tokens // 2, 6 *...  9.25 us
    ppermute x1, waiting for transfers between devices, body(): other = lax.ppermute(given, 'mp', swap)  1.23 us
  transfers between devices with their start and end apart: 2, of which 1 were waited for; matrix products, arithmetic and copies ran while one was open for 0% of the time, Pallas kernels for 30%

profile of v26, /device:TPU:0, one launch (start us, length us, event | category | flops | bytes accessed | tf_op | source)
XLA Modules:
  0.0 32.1 jit_solution(13837834786036031971)
XLA Ops:
  0.0 0.5 %collective-permute-start = (bf16[512,768]{1,0:T(8,128)(2,1)}, bf16[512,768]{1,0:T(8,128)(2,1)S(1)}, u32[]{:S(2)}, u32[]{:S(2)}) collective-permute-start(bf16[512,768]{1,0:T(8,128)(2,1)} %queries.1), channel_id=1, source_target_pairs={{0,1},{1,0},{2,3},{3,2},{4,5},{5,4},{6,7},{7,6},{8,9},{9,8},{10,11... | collective-permute-start | bytes 2359304 | tf_op jit(solution)/shard_map/ppermute | solution.py:315
  0.5 0.0 copy-start.1
  0.5 0.0 copy-start
  0.5 9.2 %project.1 = (f32[96,384]{1,0:T(8,128)S(1)}, f32[96,384]{1,0:T(8,128)S(1)}) custom-call(bf16[192,4096]{1,0:T(8,128)(2,1)} %inputs.1, bf16[192,7168]{1,0:T(8,128)(2,1)} %gate_pre.1, bf16[192,7168]{1,0:T(8,128)(2,1)} %up_pre.1, bf16[192,7168]{1,0:T(8,128)(2,1)} %hidden_grad.1, bf16[192,4096]{1,0:T(8,128)(2,1)} %out_grad.1, bf16[64,4096]{1,0:T(8,128)(2,1)} %bitcast.12, ...), custom_call_target="tpu_custom_call" | custom-call | flops 830472192 | bytes 11403264 | tf_op jit(solution)/shard_map/project/pallas_call | solution.py:152
  9.7 0.1 collective-permute-start.1
  9.8 0.0 copy-done.1
  9.8 0.1 reshape.4.ids
  9.9 1.2 %collective-permute-done.1.other = f32[96,384]{1,0:T(8,128)S(1)} collective-permute-done((f32[96,384]{1,0:T(8,128)S(1)}, f32[96,384]{1,0:T(8,128)S(1)}, u32[]{:S(2)}, u32[]{:S(2)}) %collective-permute-start.1) | collective-permute-done | bytes 147488 | tf_op jit(solution)/shard_map/ppermute | solution.py:318
  11.2 0.4 %outer.1 = f32[8,24,128]{2,1,0:T(8,128)S(1)} custom-call(f32[96,384]{1,0:T(8,128)S(1)} %get-tuple-element.7.own, f32[96,384]{1,0:T(8,128)S(1)} %collective-permute-done.1.other, s32[2,96]{1,0:T(2,128)S(1)} %reshape.4.ids), custom_call_target="tpu_custom_call" | custom-call | tf_op jit(solution)/shard_map/outer/pallas_call | solution.py:231
  11.6 11.2 %all_to_all.10.received = f32[8,24,128]{2,1,0:T(8,128)S(1)} all-to-all(f32[8,24,128]{2,1,0:T(8,128)S(1)} %outer.1), channel_id=1, replica_groups={{10,12,14,0,2,4,6,8},{11,13,15,1,3,5,7,9},{26,28,30,16,18,20,22,24},{27..., dimensions={0} | all-to-all | bytes 196608 | tf_op jit(solution)/shard_map/all_to_all | solution.py:293
  22.8 0.0 collective-permute-done.swapped
  22.8 0.0 copy-done
  22.8 0.6 %score.1 = f32[16,512]{1,0:T(8,128)S(1)} custom-call(bf16[512,768]{1,0:T(8,128)(2,1)S(1)} %copy-done, bf16[512,768]{1,0:T(8,128)(2,1)S(1)} %collective-permute-done.swapped, f32[8,24,128]{2,1,0:T(8,128)S(1)} %all_to_all.10.received), custom_call_target="tpu_custom_call" | custom-call | tf_op jit(solution)/shard_map/score/pallas_call | solution.py:279
  23.4 8.1 %all_to_all.11 = f32[16,1,512]{2,1,0:T(1,128)S(1)} all-to-all(f32[16,1,512]{2,1,0:T(1,128)S(1)} %copy.14), channel_id=1, replica_groups={{11,12,13,14,15,0,1,2,3,4,5,6,7,8,9,10},{27,28,29,30,31,16,17,18,19,20,..., dimensions={0} | all-to-all | bytes 65536 | tf_op jit(solution)/shard_map/all_to_all | solution.py:293
  31.5 0.6 %reduce_sum.11 = f32[512]{0:T(512)} reduce(f32[16,1,512]{2,1,0:T(1,128)S(1)} %all_to_all.11, f32[]{:T(128)} %constant.0.clone.1), dimensions={0,1}, to_apply=%region_0.0 | reduce | flops 7680 | bytes 34820 | tf_op jit(solution)/shard_map/reduce_sum | solution.py:323
  (1 shorter events, 0.0 us)
Async XLA Ops:
  0.0 22.8 %collective-permute-start = (bf16[512,768]{1,0:T(8,128)(2,1)}, bf16[512,768]{1,0:T(8,128)(2,1)S(1)}, u32[]{:S(2)}, u32[]{:S(2)}) collective-permute-start(bf16[512,768]{1,0:T(8,128)(2,1)} %queries.1), channel_id=1, source_target_pairs={{0,1},{1,0},{2,3},{3,2},{4,5},{5,4},{6,7},{7,6},{8,9},{9,8},{10,11... | collective-permute-start | bytes 2359304 | tf_op jit(solution)/shard_map/ppermute | solution.py:315
  0.5 9.4 %copy-start.1 = (s32[192]{0:T(256)S(1)}, s32[192]{0:T(256)}, u32[]{:S(2)}) copy-start(s32[192]{0:T(256)} %param.18) | copy-start | bytes 2308
  0.5 22.4 %copy-start = (bf16[512,768]{1,0:T(8,128)(2,1)S(1)}, bf16[512,768]{1,0:T(8,128)(2,1)}, u32[]{:S(2)}) copy-start(bf16[512,768]{1,0:T(8,128)(2,1)} %queries.1) | copy-start | bytes 2359300
  9.7 1.4 %collective-permute-start.1 = (f32[96,384]{1,0:T(8,128)S(1)}, f32[96,384]{1,0:T(8,128)S(1)}, u32[]{:S(2)}, u32[]{:S(2)}) collective-permute-start(f32[96,384]{1,0:T(8,128)S(1)} %get-tuple-element.8), channel_id=1, source_target_pairs={{0,1},{1,0},{2,3},{3,2},{4,5},{5,4},{6,7},{7,6},{8,9},{9,8},{10,11... | collective-permute-start | bytes 442376 | tf_op jit(solution)/shard_map/ppermute | solution.py:318

commit v27 on v25

--- a/solution.py
+++ b/solution.py
@@ -210,7 +210,7 @@
             both = jnp.concatenate([two, two], axis=0)
             term = lax.dot_general(one, both, NT, preferred_element_type=jnp.float32)
             product = term if product is None else product + term
-        products[module] = product
+        products[module, : 2 * width, :] = product
         for label in range(2):
             even = products[module, pl.ds(label * width, half, stride=2), :]
             odd = products[module, pl.ds(label * width + 1, half, stride=2), :]
@@ -234,7 +234,7 @@
         out_specs=pl.BlockSpec(memory_space=pltpu.VMEM),
         scratch_shapes=[
             pltpu.VMEM(own.shape[::-1], jnp.float32),
-            pltpu.VMEM((3, 2 * width, 2 * width), jnp.float32),
+            pltpu.VMEM((3, 2 * width + 8, 2 * width), jnp.float32),
         ],
         compiler_params=pltpu.CompilerParams(vmem_limit_bytes=6 * 2**20),
         name="outer",
@@ -280,7 +280,7 @@
         out_shape=jax.ShapeDtypeStruct((2 * chips, queries.shape[0]), jnp.float32),
         in_specs=[pl.BlockSpec(memory_space=pltpu.VMEM)] * 3,
         out_specs=pl.BlockSpec(memory_space=pltpu.VMEM),
-        scratch_shapes=[pltpu.VMEM((chips * height, lanes), jnp.float32)],
+        scratch_shapes=[pltpu.VMEM(((chips + 1) * height, lanes), jnp.float32)],
         compiler_params=pltpu.CompilerParams(vmem_limit_bytes=6 * 2**20),
         name="score",
     )(queries, swapped, received)

time: 30.6 us -> 30.6 us (level)
  no operation moved by 1% of the time
where the time goes in v27:
time: 30.6 us; the launch traced here: 30.4 us
  blocking collectives  19.3 us (63%)
  Pallas kernels  8.51 us (28%)
  waiting for transfers between devices  1.24 us (4%)
  other arithmetic  0.62 us (2%)
  starting transfers between devices  0.57 us (2%)
    all_to_all x2, blocking collectives, to_all(): lax.all_to_all(blocks, axes, split_axis=0, concat_axis=0, axis_index_grou...  19.3 us
    pallas_call x1, Pallas kernels, projections(): pl.pallas_call(project, out_shape=[jax.ShapeDtypeStruct((tokens // 2, 6 *...  7.5 us
    ppermute x1, waiting for transfers between devices, body(): other = lax.ppermute(given, 'mp', swap)  1.24 us
    reduce_sum x1, other arithmetic, body(): return jnp.sum(pieces, axis=0)  0.62 us
  transfers between devices with their start and end apart: 2, of which 1 were waited for; matrix products, arithmetic and copies ran while one was open for 0% of the time, Pallas kernels for 26%

profile of v27, /device:TPU:0, one launch (start us, length us, event | category | flops | bytes accessed | tf_op | source)
XLA Modules:
  0.0 30.4 jit_solution(12747692650403891978)
XLA Ops:
  0.0 0.5 %collective-permute-start = (bf16[512,768]{1,0:T(8,128)(2,1)}, bf16[512,768]{1,0:T(8,128)(2,1)S(1)}, u32[]{:S(2)}, u32[]{:S(2)}) collective-permute-start(bf16[512,768]{1,0:T(8,128)(2,1)} %queries.1), channel_id=1, source_target_pairs={{0,1},{1,0},{2,3},{3,2},{4,5},{5,4},{6,7},{7,6},{8,9},{9,8},{10,11... | collective-permute-start | bytes 2359304 | tf_op jit(solution)/shard_map/ppermute | solution.py:314
  0.5 0.0 copy-start.1
  0.5 0.0 copy-start
  0.5 7.5 %project.1 = (f32[96,384]{1,0:T(8,128)S(1)}, f32[96,384]{1,0:T(8,128)S(1)}) custom-call(bf16[192,4096]{1,0:T(8,128)(2,1)} %inputs.1, bf16[192,7168]{1,0:T(8,128)(2,1)} %gate_pre.1, bf16[192,7168]{1,0:T(8,128)(2,1)} %up_pre.1, bf16[192,7168]{1,0:T(8,128)(2,1)} %hidden_grad.1, bf16[192,4096]{1,0:T(8,128)(2,1)} %out_grad.1, bf16[64,4096]{1,0:T(8,128)(2,1)} %bitcast.12, ...), custom_call_target="tpu_custom_call" | custom-call | flops 830472192 | bytes 11403264 | tf_op jit(solution)/shard_map/project/pallas_call | solution.py:151
  8.0 0.1 collective-permute-start.1
  8.1 0.0 copy-done.1
  8.1 0.1 reshape.4.ids
  8.2 1.2 %collective-permute-done.1.other = f32[96,384]{1,0:T(8,128)S(1)} collective-permute-done((f32[96,384]{1,0:T(8,128)S(1)}, f32[96,384]{1,0:T(8,128)S(1)}, u32[]{:S(2)}, u32[]{:S(2)}) %collective-permute-start.1) | collective-permute-done | bytes 147488 | tf_op jit(solution)/shard_map/ppermute | solution.py:317
  9.4 0.4 %outer.1 = f32[8,24,128]{2,1,0:T(8,128)S(1)} custom-call(f32[96,384]{1,0:T(8,128)S(1)} %get-tuple-element.7.own, f32[96,384]{1,0:T(8,128)S(1)} %collective-permute-done.1.other, s32[2,96]{1,0:T(2,128)S(1)} %reshape.4.ids), custom_call_target="tpu_custom_call" | custom-call | tf_op jit(solution)/shard_map/outer/pallas_call | solution.py:230
  9.9 11.2 %all_to_all.10.received = f32[8,24,128]{2,1,0:T(8,128)S(1)} all-to-all(f32[8,24,128]{2,1,0:T(8,128)S(1)} %outer.1), channel_id=1, replica_groups={{10,12,14,0,2,4,6,8},{11,13,15,1,3,5,7,9},{26,28,30,16,18,20,22,24},{27..., dimensions={0} | all-to-all | bytes 196608 | tf_op jit(solution)/shard_map/all_to_all | solution.py:292
  21.1 0.0 collective-permute-done.swapped
  21.1 0.0 copy-done
  21.1 0.6 %score.1 = f32[16,512]{1,0:T(8,128)S(1)} custom-call(bf16[512,768]{1,0:T(8,128)(2,1)S(1)} %copy-done, bf16[512,768]{1,0:T(8,128)(2,1)S(1)} %collective-permute-done.swapped, f32[8,24,128]{2,1,0:T(8,128)S(1)} %all_to_all.10.received), custom_call_target="tpu_custom_call" | custom-call | tf_op jit(solution)/shard_map/score/pallas_call | solution.py:278
  21.7 8.1 %all_to_all.11 = f32[16,1,512]{2,1,0:T(1,128)S(1)} all-to-all(f32[16,1,512]{2,1,0:T(1,128)S(1)} %copy.14), channel_id=1, replica_groups={{11,12,13,14,15,0,1,2,3,4,5,6,7,8,9,10},{27,28,29,30,31,16,17,18,19,20,..., dimensions={0} | all-to-all | bytes 65536 | tf_op jit(solution)/shard_map/all_to_all | solution.py:292
  29.8 0.6 %reduce_sum.11 = f32[512]{0:T(512)} reduce(f32[16,1,512]{2,1,0:T(1,128)S(1)} %all_to_all.11, f32[]{:T(128)} %constant.0.clone.1), dimensions={0,1}, to_apply=%region_0.0 | reduce | flops 7680 | bytes 34820 | tf_op jit(solution)/shard_map/reduce_sum | solution.py:322
  (1 shorter events, 0.0 us)
Async XLA Ops:
  0.0 21.1 %collective-permute-start = (bf16[512,768]{1,0:T(8,128)(2,1)}, bf16[512,768]{1,0:T(8,128)(2,1)S(1)}, u32[]{:S(2)}, u32[]{:S(2)}) collective-permute-start(bf16[512,768]{1,0:T(8,128)(2,1)} %queries.1), channel_id=1, source_target_pairs={{0,1},{1,0},{2,3},{3,2},{4,5},{5,4},{6,7},{7,6},{8,9},{9,8},{10,11... | collective-permute-start | bytes 2359304 | tf_op jit(solution)/shard_map/ppermute | solution.py:314
  0.5 7.6 %copy-start.1 = (s32[192]{0:T(256)S(1)}, s32[192]{0:T(256)}, u32[]{:S(2)}) copy-start(s32[192]{0:T(256)} %param.18) | copy-start | bytes 2308
  0.5 20.6 %copy-start = (bf16[512,768]{1,0:T(8,128)(2,1)S(1)}, bf16[512,768]{1,0:T(8,128)(2,1)}, u32[]{:S(2)}) copy-start(bf16[512,768]{1,0:T(8,128)(2,1)} %queries.1) | copy-start | bytes 2359300
  8.0 1.4 %collective-permute-start.1 = (f32[96,384]{1,0:T(8,128)S(1)}, f32[96,384]{1,0:T(8,128)S(1)}, u32[]{:S(2)}, u32[]{:S(2)}) collective-permute-start(f32[96,384]{1,0:T(8,128)S(1)} %get-tuple-element.8), channel_id=1, source_target_pairs={{0,1},{1,0},{2,3},{3,2},{4,5},{5,4},{6,7},{7,6},{8,9},{9,8},{10,11... | collective-permute-start | bytes 442376 | tf_op jit(solution)/shard_map/ppermute | solution.py:317
